TPU v7x, 32 devices: a whole 2x2x4 slice. The times are simulated.
32 devices in a mesh: seq: 4 (over y, core), fsdp: 8 (over z, x).
Axes of the slice: x: 2, y: 2, z: 4, core: 2. Of those that a mesh axis runs over, the one named last changes fastest.
Arguments:
- tokens: bfloat16 [8, 512, 2048], P('fsdp', 'seq'), may hold values from -6 to 6
- block_ids: int32 [8, 512], P('fsdp'), may hold values from 0 to 3, never falling along the last dimension, each value on 1 to 256 neighbouring positions
- gain_attn: bfloat16 [2048], P('fsdp'), may hold values from 0.5 to 1.5
- w_query: bfloat16 [2048, 2048], P('fsdp'), may hold values from -0.5 to 0.5
- w_key: bfloat16 [2048, 512], P('fsdp'), may hold values from -0.5 to 0.5
- w_value: bfloat16 [2048, 512], P('fsdp'), may hold values from -0.125 to 0.125
- w_out: bfloat16 [2048, 2048], P('fsdp'), may hold values from -1.5 to 1.5
- gain_mlp: bfloat16 [2048], P('fsdp'), may hold values from 0.5 to 1.5
- w_gate: bfloat16 [2048, 8192], P('fsdp'), may hold values from -0.125 to 0.125
- w_up: bfloat16 [2048, 8192], P('fsdp'), may hold values from -0.125 to 0.125
- w_down: bfloat16 [2048, 8192], P('fsdp'), may hold values from -0.5 to 0.5
- cotangent: bfloat16 [8, 512, 2048], P('fsdp', 'seq'), may hold values from -6 to 6
Outputs:
- mixed: bfloat16 [8, 512, 2048], P('fsdp', 'seq')
- grad_tokens: bfloat16 [8, 512, 2048], P('fsdp', 'seq')
- grad_gain_attn: float32 [2048], P('fsdp')
- grad_query: float32 [2048, 2048], P('fsdp')
- grad_key: float32 [2048, 512], P('fsdp')
- grad_value: float32 [2048, 512], P('fsdp')
- grad_out: float32 [2048, 2048], P('fsdp')
- grad_gain_mlp: float32 [2048], P('fsdp')
- grad_gate: float32 [2048, 8192], P('fsdp')
- grad_up: float32 [2048, 8192], P('fsdp')
- grad_down: float32 [2048, 8192], P('fsdp')
Inputs may be any that keep to these rules, and one draw needn't show every extreme that they name: In each row of block_ids the block numbers never fall; each block holds 1 to 256 positions.
All inputs are finite; a program needn't handle non-finite values.
Results may differ from a plain program's by a relative error of at most 0.02.
Values may be sent and summed in bfloat16 or wider, within the bound.
A program may use at most 768 MiB of HBM per device.

v0:
```python
import jax
import jax.numpy as jnp
from jax import lax
from jax.sharding import PartitionSpec as P

H = 32
KVH = 8
HD = 64


EPSILON = 1e-05
RESIDUAL = 0.22


def contract_rows(left, right):
    return lax.dot_general(
        left, right, (((0,), (0,)), ((), ())), preferred_element_type=jnp.float32
    )


def contract_cols(left, right):
    return lax.dot_general(
        left, right, (((1,), (1,)), ((), ())), preferred_element_type=jnp.float32
    )


def rms_factor(values):
    return lax.rsqrt(jnp.mean(values * values, axis=1, keepdims=True) + EPSILON)


def norm_back(grad_normed, values, factor, gain):
    weighted = grad_normed * gain
    centre = jnp.mean(weighted * values, axis=1, keepdims=True)
    return factor * weighted - values * (factor * factor * factor) * centre


def softmax_rows(query_block, key_heads, query_ids, key_ids, factor):
    scores = (
        jnp.einsum("qkgd,tkd->kgqt", query_block, key_heads, preferred_element_type=jnp.float32)
        * factor
    )
    allowed = key_ids[None, None, None, :] <= query_ids[None, None, :, None]
    scores = jnp.where(allowed, scores, -1e30)
    shifted = jnp.exp(scores - jnp.max(scores, axis=-1, keepdims=True))
    return shifted / jnp.sum(shifted, axis=-1, keepdims=True)


def reduce_terms(build, arrays):
    owned = lax.psum_scatter(
        build(lambda matrix: matrix, arrays).astype(jnp.bfloat16),
        "fsdp",
        scatter_dimension=0,
        tiled=True,
    )
    return lax.psum(owned, "seq").astype(jnp.float32)


def mlp_build(select, arrays):
    normed_two, grad_down_in, grad_gate_in, grad_upward, hidden = arrays
    picked = select(normed_two)
    picked_grad = select(grad_down_in)
    return jnp.concatenate(
        [
            contract_rows(picked, grad_gate_in),
            contract_rows(picked, grad_upward),
            contract_rows(picked_grad, hidden),
        ],
        axis=1,
    )


def attn_build(select, arrays):
    (
        normed_one,
        grad_branch,
        grad_query_tokens,
        grad_key_tokens,
        grad_value_tokens,
        attended_tokens,
    ) = arrays
    picked = select(normed_one)
    picked_grad = select(grad_branch)
    return jnp.concatenate(
        [
            contract_rows(picked, grad_query_tokens),
            contract_rows(picked, grad_key_tokens),
            contract_rows(picked, grad_value_tokens),
            contract_rows(picked_grad, attended_tokens),
        ],
        axis=1,
    )


def body(
    tokens,
    block_ids,
    gain_attn,
    w_query,
    w_key,
    w_value,
    w_out,
    gain_mlp,
    w_gate,
    w_up,
    w_down,
    cotangent,
):
    seq_count = lax.axis_size("seq")
    fsdp_count = lax.axis_size("fsdp")
    local_rows = tokens.shape[1]
    width = tokens.shape[2]
    length = block_ids.shape[1]
    local_heads = H // seq_count
    local_kv = max(1, KVH // seq_count)
    repeats = max(1, seq_count // KVH)
    sharing = local_heads // local_kv
    span = min(512, length)
    blocks = length // span
    factor = 1.0 / HD
    key_ids = block_ids[0]
    id_blocks = key_ids.reshape(blocks, span)
    full_gain_attn, full_query, full_key, full_value, full_out = (
        lax.all_gather(gain_attn, "fsdp", axis=0, tiled=True),
        lax.all_gather(w_query, "fsdp", axis=0, tiled=True),
        lax.all_gather(w_key, "fsdp", axis=0, tiled=True),
        lax.all_gather(w_value, "fsdp", axis=0, tiled=True),
        lax.all_gather(w_out, "fsdp", axis=0, tiled=True),
    )
    full_gain_mlp, full_gate, full_up, full_down = (
        lax.all_gather(gain_mlp, "fsdp", axis=0, tiled=True),
        lax.all_gather(w_gate, "fsdp", axis=0, tiled=True),
        lax.all_gather(w_up, "fsdp", axis=0, tiled=True),
        lax.all_gather(w_down, "fsdp", axis=0, tiled=True),
    )
    inputs = tokens[0].astype(jnp.float32)
    factor_one = rms_factor(inputs)
    attn_gain = full_gain_attn.astype(jnp.float32)
    normed_one = (inputs * factor_one * attn_gain).astype(jnp.bfloat16)
    query = jnp.dot(normed_one, full_query, preferred_element_type=jnp.float32).astype(jnp.bfloat16)
    keys = jnp.dot(normed_one, full_key, preferred_element_type=jnp.float32).astype(jnp.bfloat16)
    values = jnp.dot(normed_one, full_value, preferred_element_type=jnp.float32).astype(
        jnp.bfloat16
    )
    query_parts = query.reshape(local_rows, seq_count, local_heads * HD)
    key_parts = jnp.repeat(keys.reshape(local_rows, KVH, HD), repeats, axis=1).reshape(
        local_rows, seq_count, local_kv * HD
    )
    value_parts = jnp.repeat(values.reshape(local_rows, KVH, HD), repeats, axis=1).reshape(
        local_rows, seq_count, local_kv * HD
    )
    query_heads, key_heads, value_heads = (
        lax.all_to_all(query_parts, "seq", split_axis=1, concat_axis=0, tiled=True),
        lax.all_to_all(key_parts, "seq", split_axis=1, concat_axis=0, tiled=True),
        lax.all_to_all(value_parts, "seq", split_axis=1, concat_axis=0, tiled=True),
    )
    query_blocks = query_heads.reshape(blocks, span, local_kv, sharing, HD)
    key_all = key_heads.reshape(length, local_kv, HD)
    value_all = value_heads.reshape(length, local_kv, HD)

    def attend_block(pair):
        query_block, query_ids = pair
        probs = softmax_rows(query_block, key_all, query_ids, key_ids, factor)
        result = jnp.einsum(
            "kgqt,tkd->qkgd",
            probs.astype(jnp.bfloat16),
            value_all,
            preferred_element_type=jnp.float32,
        )
        return result.reshape(span, local_heads * HD).astype(jnp.bfloat16)

    attended = lax.map(attend_block, (query_blocks, id_blocks)).reshape(length, 1, local_heads * HD)
    attended_tokens = lax.all_to_all(
        attended, "seq", split_axis=0, concat_axis=1, tiled=True
    ).reshape(local_rows, H * HD)
    branch = contract_cols(attended_tokens, full_out)
    middle = inputs + RESIDUAL * branch
    factor_two = rms_factor(middle)
    mlp_gain = full_gain_mlp.astype(jnp.float32)
    normed_two = (middle * factor_two * mlp_gain).astype(jnp.bfloat16)
    gate = jnp.dot(normed_two, full_gate, preferred_element_type=jnp.float32)
    upward = jnp.dot(normed_two, full_up, preferred_element_type=jnp.float32)
    sigma = jax.nn.sigmoid(gate)
    hidden = (gate * sigma * upward).astype(jnp.bfloat16)
    down = contract_cols(hidden, full_down)
    mixed = (middle + RESIDUAL * down).astype(jnp.bfloat16)
    grad_output = cotangent[0].astype(jnp.float32)
    grad_down_in = (RESIDUAL * grad_output).astype(jnp.bfloat16)
    grad_hidden = jnp.dot(grad_down_in, full_down, preferred_element_type=jnp.float32)
    grad_upward = (grad_hidden * gate * sigma).astype(jnp.bfloat16)
    grad_gate_in = (grad_hidden * upward * sigma * (1.0 + gate * (1.0 - sigma))).astype(
        jnp.bfloat16
    )
    grad_normed_two = contract_cols(grad_gate_in, full_gate) + contract_cols(grad_upward, full_up)
    gain_two_term = jnp.sum(grad_normed_two * middle * factor_two, axis=0)
    grad_middle = grad_output + norm_back(grad_normed_two, middle, factor_two, mlp_gain)
    hidden_cols = full_gate.shape[1]
    mlp_grads = reduce_terms(
        mlp_build, (normed_two, grad_down_in, grad_gate_in, grad_upward, hidden)
    )
    grad_branch = (RESIDUAL * grad_middle).astype(jnp.bfloat16)
    grad_attended = jnp.dot(grad_branch, full_out, preferred_element_type=jnp.float32).astype(
        jnp.bfloat16
    )
    grad_heads = lax.all_to_all(
        grad_attended.reshape(local_rows, seq_count, local_heads * HD),
        "seq",
        split_axis=1,
        concat_axis=0,
        tiled=True,
    )
    grad_blocks = grad_heads.reshape(blocks, span, local_kv, sharing, HD)

    def backward_block(carry, triple):
        grad_keys, grad_values = carry
        query_block, query_ids, grad_block = triple
        probs = softmax_rows(query_block, key_all, query_ids, key_ids, factor)
        grad_probs = jnp.einsum(
            "qkgd,tkd->kgqt", grad_block, value_all, preferred_element_type=jnp.float32
        )
        centre = jnp.sum(probs * grad_probs, axis=-1, keepdims=True)
        grad_scores = (probs * (grad_probs - centre)).astype(jnp.bfloat16)
        grad_query_block = (
            jnp.einsum("kgqt,tkd->qkgd", grad_scores, key_all, preferred_element_type=jnp.float32)
            * factor
        )
        grad_keys = (
            grad_keys
            + jnp.einsum(
                "kgqt,qkgd->tkd", grad_scores, query_block, preferred_element_type=jnp.float32
            )
            * factor
        )
        grad_values = grad_values + jnp.einsum(
            "kgqt,qkgd->tkd",
            probs.astype(jnp.bfloat16),
            grad_block,
            preferred_element_type=jnp.float32,
        )
        return ((grad_keys, grad_values), grad_query_block.reshape(span, local_heads * HD))

    zero_heads = jnp.zeros((length, local_kv, HD), jnp.float32)
    (grad_keys, grad_values), grad_query = lax.scan(
        backward_block, (zero_heads, zero_heads), (query_blocks, id_blocks, grad_blocks)
    )
    back_query, back_keys, back_values = (
        lax.all_to_all(
            grad_query.reshape(length, 1, local_heads * HD).astype(jnp.bfloat16),
            "seq",
            split_axis=0,
            concat_axis=1,
            tiled=True,
        ).astype(jnp.float32),
        lax.all_to_all(
            grad_keys.reshape(length, 1, local_kv * HD).astype(jnp.bfloat16),
            "seq",
            split_axis=0,
            concat_axis=1,
            tiled=True,
        ).astype(jnp.float32),
        lax.all_to_all(
            grad_values.reshape(length, 1, local_kv * HD).astype(jnp.bfloat16),
            "seq",
            split_axis=0,
            concat_axis=1,
            tiled=True,
        ).astype(jnp.float32),
    )
    grad_query_tokens = back_query.reshape(local_rows, H * HD).astype(jnp.bfloat16)
    grad_key_tokens = (
        jnp.sum(back_keys.reshape(local_rows, KVH, repeats, HD), axis=2)
        .reshape(local_rows, KVH * HD)
        .astype(jnp.bfloat16)
    )
    grad_value_tokens = (
        jnp.sum(back_values.reshape(local_rows, KVH, repeats, HD), axis=2)
        .reshape(local_rows, KVH * HD)
        .astype(jnp.bfloat16)
    )
    grad_normed_one = (
        contract_cols(grad_query_tokens, full_query)
        + contract_cols(grad_key_tokens, full_key)
        + contract_cols(grad_value_tokens, full_value)
    )
    gain_one_term = jnp.sum(grad_normed_one * inputs * factor_one, axis=0)
    grad_inputs = grad_middle + norm_back(grad_normed_one, inputs, factor_one, attn_gain)
    query_cols = H * HD
    kv_cols = KVH * HD
    attn_grads = reduce_terms(
        attn_build,
        (
            normed_one,
            grad_branch,
            grad_query_tokens,
            grad_key_tokens,
            grad_value_tokens,
            attended_tokens,
        ),
    )
    gain_one_sum, gain_two_sum = lax.psum((gain_one_term, gain_two_term), ("seq", "fsdp"))
    share = width // fsdp_count
    offset = lax.axis_index("fsdp") * share
    grad_gain_one = lax.dynamic_slice_in_dim(gain_one_sum, offset, share, 0)
    grad_gain_two = lax.dynamic_slice_in_dim(gain_two_sum, offset, share, 0)
    grad_query_out = attn_grads[:, :query_cols]
    grad_key_out = attn_grads[:, query_cols : query_cols + kv_cols]
    grad_value_out = attn_grads[:, query_cols + kv_cols : query_cols + 2 * kv_cols]
    grad_out_out = attn_grads[:, query_cols + 2 * kv_cols :]
    grad_gate_out = mlp_grads[:, :hidden_cols]
    grad_up_out = mlp_grads[:, hidden_cols : 2 * hidden_cols]
    grad_down_out = mlp_grads[:, 2 * hidden_cols :]
    return (
        mixed[None],
        grad_inputs.astype(jnp.bfloat16)[None],
        grad_gain_one,
        grad_query_out,
        grad_key_out,
        grad_value_out,
        grad_out_out,
        grad_gain_two,
        grad_gate_out,
        grad_up_out,
        grad_down_out,
    )


def solution(mesh):
    return jax.shard_map(
        body,
        mesh=mesh,
        in_specs=(
            P("fsdp", "seq", None),
            P("fsdp", None),
            P("fsdp"),
            P("fsdp", None),
            P("fsdp", None),
            P("fsdp", None),
            P("fsdp", None),
            P("fsdp"),
            P("fsdp", None),
            P("fsdp", None),
            P("fsdp", None),
            P("fsdp", "seq", None),
        ),
        out_specs=(
            P("fsdp", "seq", None),
            P("fsdp", "seq", None),
            P("fsdp"),
            P("fsdp", None),
            P("fsdp", None),
            P("fsdp", None),
            P("fsdp", None),
            P("fsdp"),
            P("fsdp", None),
            P("fsdp", None),
            P("fsdp", None),
        ),
        check_vma=False,
    )
```

profile of v0, /device:TPU:15, one launch (start us, length us, event | category | flops | bytes accessed | tf_op | source)
XLA Modules:
  0.0 4634.9 jit_solution(12721850625115501919)
XLA Ops:
  11.9 11.2 all-gather
  23.9 34.9 all-gather.12.cloned.1.call-done
  61.6 5.0 all-to-all-start.1
  66.6 42.2 all-gather.10.cloned.1.call-done
  111.5 5.0 all-to-all-start
  116.5 116.4 %all-gather.14.cloned.1.call-done = bf16[2048,2048]{1,0:T(8,128)(2,1)} async-done(((bf16[256,2048]{1,0:T(8,128)(2,1)}), bf16[2048,2048]{1,0:T(8,128)(2,1)}) %all-gather.14.cloned.1.call-update) | async-done | bytes 8388624 | tf_op jit(solution)/shard_map/all_gather | solution.py:124
  232.9 4.7 convolution_convert_fusion.8
  238.5 4.6 all-to-all-start.2
  243.8 6.4 all-to-all-done.2
  250.7 5.3 fusion.81
  256.0 4.3 fusion.21
  263.3 5.2 all-to-all-start.3
  268.5 14.0 all-gather.1
  283.7 74.4 %all-gather.16.cloned.1.call-done = bf16[2048,2048]{1,0:T(8,128)(2,1)} async-done(((bf16[256,2048]{1,0:T(8,128)(2,1)}), bf16[2048,2048]{1,0:T(8,128)(2,1)}) %all-gather.16.cloned.1.call-update) | async-done | bytes 8388624 | tf_op jit(solution)/shard_map/all_gather | solution.py:127
  358.1 6.4 multiply_reduce_fusion.2
  364.7 633.1 %all-gather.20.cloned.1.call-done = bf16[2048,8192]{1,0:T(8,128)(2,1)} async-done(((bf16[256,8192]{1,0:T(8,128)(2,1)}), bf16[2048,8192]{1,0:T(8,128)(2,1)}) %all-gather.20.cloned.1.call-update) | async-done | bytes 33554448 | tf_op jit(solution)/shard_map/all_gather | solution.py:132
  997.7 17.5 fusion.87
  1015.3 621.6 %all-gather.18.cloned.1.call-done = bf16[2048,8192]{1,0:T(8,128)(2,1)} async-done(((bf16[256,8192]{1,0:T(8,128)(2,1)}), bf16[2048,8192]{1,0:T(8,128)(2,1)}) %all-gather.18.cloned.1.call-update) | async-done | bytes 33554448 | tf_op jit(solution)/shard_map/all_gather | solution.py:131
  1636.9 17.5 fusion.86
  1654.4 621.8 %all-gather.22.cloned.1.call-done = bf16[2048,8192]{1,0:T(8,128)(2,1)} async-done(((bf16[256,8192]{1,0:T(8,128)(2,1)}), bf16[2048,8192]{1,0:T(8,128)(2,1)}) %all-gather.22.cloned.1.call-update) | async-done | bytes 33554448 | tf_op jit(solution)/shard_map/all_gather | solution.py:133
  2276.1 19.7 multiply_convert_fusion
  2295.9 16.3 fusion.88
  2312.2 17.3 multiply_reduce_fusion
  2329.8 5.0 convolution_convert_fusion.7
  2335.7 4.5 all-to-all-start.4
  2340.2 5.7 convolution_convert_fusion.3
  2347.6 4.8 fusion.30
  2352.4 8.1 fusion.1
  2362.0 5.2 all-to-all-start.7
  2367.2 7.0 fusion.3
  2379.1 3.4 all-to-all-start.6
  2382.5 3.0 fusion.24
  2388.3 4.2 all-to-all-start.5
  2399.5 3.7 reshape.272
  2407.3 7.0 convolution_convert_fusion.4
  2414.3 38.4 pad_maximum_fusion.1
  2452.9 16.2 convolution_convert_fusion.1
  2469.1 13.9 convolution_convert_fusion.2
  2483.0 14.0 convolution_convert_fusion
  2497.0 67.8 %pad_maximum_fusion = bf16[2048,24576]{1,0:T(8,128)(2,1)} fusion(bf16[2048,8192]{1,0:T(8,128)(2,1)} %convolution_convert_fusion, bf16[2048,8192]{1,0:T(8,128)(2,1)} %convolution_convert_fusion.1, bf16[2048,8192]{1,0:T(8,128)(2,1)} %convolution_convert_fusion.2), kind=kLoop, calls=%fused_computation.1 | loop fusion | flops 301989888 | bytes 201326592 | tf_op jit(solution)/shard_map/concatenate | solution.py:62
  2564.9 231.8 %reduce-scatter.5.cloned.1.call-done = bf16[256,5120]{0,1:T(8,128)(2,1)} async-done(((bf16[2048,5120]{0,1:T(8,128)(2,1)}), bf16[256,5120]{0,1:T(8,128)(2,1)}) %reduce-scatter.5.cloned.1.call-update) | async-done | bytes 2621456 | tf_op jit(solution)/shard_map/reduce_scatter | solution.py:49
  2796.6 1540.3 %reduce-scatter.7.cloned.1.call-done = bf16[256,24576]{1,0:T(8,128)(2,1)} async-done(((bf16[2048,24576]{1,0:T(8,128)(2,1)}), bf16[256,24576]{1,0:T(8,128)(2,1)}) %reduce-scatter.7.cloned.1.call-update) | async-done | bytes 12582928
  4337.0 18.5 fusion.11
  4355.6 6.5 fusion.89
  4364.1 40.6 all-reduce.1
  4407.2 197.7 %all-reduce.5.cloned.1.call-done = (bf16[256,5120]{0,1:T(8,128)(2,1)}, bf16[256,24576]{1,0:T(8,128)(2,1)}) async-done(((bf16[256,5120]{0,1:T(8,128)(2,1)}, bf16[256,24576]{1,0:T(8,128)(2,1)}), (bf16[256,5120]{0,1:T(8,128)(2,1)}, bf16[256,24576]{1,0:T(8,128)(2,1)})) %all-reduce.5.cloned.1.call-update) | async-done | bytes 15204368 | tf_op jit(solution)/shard_map/psum | solution.py:55
  4606.0 3.2 fusion.79
  4615.9 11.7 fusion.78
  (164 shorter events, 52.7 us)
Async XLA Ops:
  7.2 15.9 copy-start
  7.2 51.6 %all-gather.12.cloned.1.call-start = ((), (), s32[]{:S(2)}) async-start(), calls=%async_computation.11 | async-start | bytes 2359296 | tf_op jit(solution)/shard_map/all_gather | solution.py:125
  7.9 100.8 %all-gather.10.cloned.1.call-start = ((), (), s32[]{:S(2)}) async-start(), calls=%async_computation.10 | async-start | bytes 2359296 | tf_op jit(solution)/shard_map/all_gather | solution.py:126
  8.7 224.3 %all-gather.14.cloned.1.call-start = ((), (), s32[]{:S(2)}) async-start(), calls=%async_computation.12 | async-start | bytes 9437184 | tf_op jit(solution)/shard_map/all_gather | solution.py:124
  9.4 348.7 %all-gather.16.cloned.1.call-start = ((), (), s32[]{:S(2)}) async-start(), calls=%async_computation.13 | async-start | bytes 9437184 | tf_op jit(solution)/shard_map/all_gather | solution.py:127
  10.0 987.7 %all-gather.20.cloned.1.call-start = ((), (), s32[]{:S(2)}) async-start(), calls=%async_computation.15 | async-start | bytes 37748736 | tf_op jit(solution)/shard_map/all_gather | solution.py:132
  10.6 1626.3 %all-gather.18.cloned.1.call-start = ((), (), s32[]{:S(2)}) async-start(), calls=%async_computation.14 | async-start | bytes 37748736 | tf_op jit(solution)/shard_map/all_gather | solution.py:131
  11.2 2265.0 %all-gather.22.cloned.1.call-start = ((), (), s32[]{:S(2)}) async-start(), calls=%async_computation.16 | async-start | bytes 37748736 | tf_op jit(solution)/shard_map/all_gather | solution.py:133
  23.1 2384.2 %copy-start.25 = (f32[8,1,256]{2,1,0:T(1,128)}, f32[8,1,256]{2,1,0:T(1,128)S(1)}, u32[]{:S(2)}) copy-start(f32[8,1,256]{2,1,0:T(1,128)S(1)} %convert_element_type.212) | copy-start | bytes 24580
  23.9 2383.4 %copy-start.29 = (f32[128]{0:T(128)}, f32[128]{0:T(128)S(1)}, u32[]{:S(2)}) copy-start(f32[128]{0:T(128)S(1)} %get-tuple-element.119) | copy-start | bytes 1540
  61.6 49.9 %all-to-all-start.1 = ((bf16[128,4,128]{2,0,1:T(8,128)(2,1)}), bf16[128,4,128]{2,0,1:T(8,128)(2,1)S(1)}, u32[]{:S(2)}, u32[]{:S(2)}) async-start(bf16[128,4,128]{2,0,1:T(8,128)(2,1)} %bitcast.217), calls=%async_computation.1 | async-start | bytes 262144 | tf_op jit(solution)/shard_map/all_to_all | solution.py:153
  111.5 126.9 %all-to-all-start = ((bf16[128,4,128]{2,0,1:T(8,128)(2,1)}), bf16[128,4,128]{2,0,1:T(8,128)(2,1)S(1)}, u32[]{:S(2)}, u32[]{:S(2)}) async-start(bf16[128,4,128]{2,0,1:T(8,128)(2,1)} %bitcast.218), calls=%async_computation | async-start | bytes 262144 | tf_op jit(solution)/shard_map/all_to_all | solution.py:154
  116.5 126.6 %copy-start.33 = (s32[1,512]{1,0:T(1,128)S(1)}, s32[1,512]{1,0:T(1,128)}, u32[]{:S(2)}) copy-start(s32[1,512]{1,0:T(1,128)} %param.13) | copy-start | bytes 6148
  238.5 11.7 all-to-all-start.2
  250.7 9.6 copy-start.17
  256.0 12.5 copy-start.36
  263.3 19.3 all-to-all-start.3
  283.7 731.6 %copy-start.12 = (bf16[128,4,1,512]{0,3,1,2:T(8,128)(2,1)}, bf16[128,4,1,512]{0,3,1,2:T(8,128)(2,1)S(1)}, u32[]{:S(2)}) copy-start(bf16[128,4,1,512]{0,3,1,2:T(8,128)(2,1)S(1)} %copy.75) | copy-start | bytes 1572868
  364.5 1964.9 %copy-start.3 = (f32[128,2048]{1,0:T(8,128)}, f32[128,2048]{1,0:T(8,128)S(1)}, u32[]{:S(2)}) copy-start(f32[128,2048]{1,0:T(8,128)S(1)} %get-tuple-element.125) | copy-start | bytes 3145732
  1015.3 1260.9 %copy-start.14 = (bf16[1,128,2048]{2,1,0:T(8,128)(2,1)S(1)}, bf16[1,128,2048]{2,1,0:T(8,128)(2,1)}, u32[]{:S(2)}) copy-start(bf16[1,128,2048]{2,1,0:T(8,128)(2,1)} %param.23) | copy-start | bytes 1572868
  2312.1 17.3 copy-start.15
  2329.8 10.4 copy-start.5
  2329.8 10.4 copy-start.13
  2335.7 11.4 all-to-all-start.4
  2362.0 17.2 all-to-all-start.7
  2367.2 9.1 copy-start.18
  2379.1 9.1 all-to-all-start.6
  2388.2 26.1 copy-start.21
  2388.3 11.2 all-to-all-start.5
  2392.4 404.2 %reduce-scatter.5.cloned.1.call-start = ((), (), s32[]{:S(2)}) async-start(), calls=%async_computation.17 | async-start | bytes 23592960 | tf_op jit(solution)/shard_map/reduce_scatter | solution.py:49
  2396.0 18.3 copy-start.23
  2407.3 7.0 copy-start.10
  2452.8 16.3 copy-start.7
  2452.8 1884.1 %reduce-scatter.7.cloned.1.call-start = ((), (), s32[]{:S(2)}) async-start(), calls=%async_computation.18 | async-start | bytes 113246208
  2469.1 13.9 copy-start.8
  2469.1 13.9 copy-start.16
  2564.8 1772.2 %copy-start.4 = (f32[128,2048]{1,0:T(8,128)S(1)}, f32[128,2048]{1,0:T(8,128)}, u32[]{:S(2)}) copy-start(f32[128,2048]{1,0:T(8,128)} %copy-done.3) | copy-start | bytes 3145732
  2564.8 1772.2 %copy-start.9 = (bf16[128,8192]{1,0:T(8,128)(2,1)S(1)}, bf16[128,8192]{1,0:T(8,128)(2,1)}, u32[]{:S(2)}) copy-start(bf16[128,8192]{1,0:T(8,128)(2,1)} %get-tuple-element.113) | copy-start | bytes 6291460
  2564.8 2040.1 %all-reduce.5.cloned.1.call-start = ((), (), s32[]{:S(2)}) async-start(), calls=%async_computation.19 | async-start | bytes 30408704 | tf_op jit(solution)/shard_map/psum | solution.py:55
  4337.0 18.5 copy-start.11
  4355.5 7.5 copy-start.1
  4355.5 7.5 copy-start.20
  4355.5 7.5 copy-start.22
  4355.5 7.5 copy-start.26
  4355.5 7.5 copy-start.30
  4355.6 8.5 copy-start.28
  4355.6 50.4 %copy-start.6 = (f32[128,2048]{1,0:T(8,128)S(1)}, f32[128,2048]{1,0:T(8,128)}, u32[]{:S(2)}) copy-start(f32[128,2048]{1,0:T(8,128)} %copy-done.5) | copy-start | bytes 3145732
  4355.6 50.4 %copy-start.34 = (f32[128]{0:T(128)S(1)}, f32[128]{0:T(128)}, u32[]{:S(2)}) copy-start(f32[128]{0:T(128)} %get-tuple-element.118) | copy-start | bytes 1540
  (7 other events, 33.3 us)
Sparse Core Ops, SparseCore 0:
  10.2 48.6 all-gather.11
  60.9 47.7 all-gather.9
  110.9 122.0 all-gather.13
  234.9 123.1 all-gather.15
  359.5 638.1 all-gather.19
  999.1 637.6 all-gather.17
  1638.4 637.6 all-gather.21
  2452.9 343.6 reduce-scatter.4
  2800.5 1536.3 reduce-scatter.6
  4339.6 265.2 all-reduce.4
where the time goes:
time: 4640 us; the launch traced here: 4630 us
  waiting for transfers between devices  4130 us (89%)
  matrix products  222 us (5%)
  other arithmetic  119 us (3%)
  blocking collectives  65.8 us (1%)
  local copies, waits for them, and re-layouts  47.5 us (1%)
    unnamed x11, waiting for transfers between devices  1540 us
    all_gather x1, waiting for transfers between devices, body(): lax.all_gather(w_up, 'fsdp', axis=0, tiled=True)  633 us
    all_gather x1, waiting for transfers between devices, body(): lax.all_gather(w_down, 'fsdp', axis=0, tiled=True)  622 us
    all_gather x1, waiting for transfers between devices, body(): lax.all_gather(w_gate, 'fsdp', axis=0, tiled=True)  622 us
    reduce_scatter x1, waiting for transfers between devices, reduce_terms(): lax.psum_scatter(build(lambda matrix: matrix, arrays).astype(jnp.bfloat16...  232 us
    psum x1, waiting for transfers between devices, reduce_terms(): return lax.psum(owned, 'seq').astype(jnp.float32)  198 us
    all_gather x1, waiting for transfers between devices, body(): lax.all_gather(w_query, 'fsdp', axis=0, tiled=True)  116 us
  transfers between devices with their start and end apart: 18, of which 13 were waited for; matrix products, arithmetic and copies ran while one was open for 5% of the time, Pallas kernels for 0%

commit v1 on v0

v1 whole, which is shorter than its diff:
```python
import functools

import jax
import jax.numpy as jnp
from jax import lax
from jax.experimental import pallas as pl
from jax.experimental.pallas import tpu as pltpu
from jax.sharding import PartitionSpec as P

H = 32
KVH = 8
HD = 64
EPSILON = 1e-05
RESIDUAL = 0.22
GROUP = 16
MESH = pl.DeviceIdType.MESH
PIECES = ((0, 48), (48, 48), (96, 32))
ORDERS = ((1, 2, 3), (2, 3, 1), (3, 1, 2))


def dot(left, right):
    return jnp.dot(left, right, preferred_element_type=jnp.float32)


def dot_cols(left, right):
    return lax.dot_general(
        left, right, (((1,), (1,)), ((), ())), preferred_element_type=jnp.float32
    )


def dot_rows(left, right):
    return lax.dot_general(
        left, right, (((0,), (0,)), ((), ())), preferred_element_type=jnp.float32
    )


def rms_factor(values):
    return lax.rsqrt(jnp.mean(values * values, axis=1, keepdims=True) + EPSILON)


def norm_back(grad_normed, values, factor, gain):
    weighted = grad_normed * gain
    centre = jnp.mean(weighted * values, axis=1, keepdims=True)
    return factor * weighted - values * (factor * factor * factor) * centre


class Layout:
    def __init__(self, seq_count, fsdp_count):
        self.seq = seq_count
        self.fsdp = fsdp_count
        self.share = GROUP // seq_count
        self.seq_bits = seq_count.bit_length() - 1

    def member(self):
        return lax.axis_index("seq") + self.seq * (lax.axis_index("fsdp") % self.share)

    def device(self, mask):
        low, high = mask % self.seq, mask // self.seq
        return {
            "seq": jnp.bitwise_xor(lax.axis_index("seq"), low),
            "fsdp": jnp.bitwise_xor(lax.axis_index("fsdp"), high),
        }


def span_mask(dims):
    return sum(1 << d for d in dims)


def greet(layout):
    barrier = pltpu.get_barrier_semaphore()
    for bit in range(4):
        pl.semaphore_signal(
            barrier, inc=1, device_id=layout.device(1 << bit), device_id_type=MESH
        )
    pl.semaphore_wait(barrier, 4)


def gather_kernel(layout, rows, x_ref, o_ref, send, recv, core_send, core_recv, own_sem):
    greet(layout)
    me = layout.member()

    def place(mask, piece):
        start, size = PIECES[piece]
        block = jnp.bitwise_xor(me, mask)
        return o_ref.at[pl.ds(pl.multiple_of(block * rows + start, 16), size)]

    def own(piece):
        start, size = PIECES[piece]
        return x_ref.at[pl.ds(start, size)]

    sent, relayed = [], []

    def push(mask, piece, slot, dim):
        copy = pltpu.make_async_remote_copy(
            src_ref=own(piece) if mask == 0 else place(mask, piece),
            dst_ref=place(mask, piece),
            send_sem=send.at[piece, slot],
            recv_sem=recv.at[piece, slot],
            device_id=layout.device(1 << dim),
            device_id_type=MESH,
        )
        copy.start()
        sent.append(copy)
        return copy

    def relay(mask, piece, slot):
        copy = pltpu.make_async_remote_copy(
            src_ref=own(piece) if mask == 0 else place(mask, piece),
            dst_ref=place(mask, piece),
            send_sem=core_send.at[piece, slot],
            recv_sem=core_recv.at[piece, slot],
            device_id=layout.device(1),
            device_id_type=MESH,
        )
        copy.start()
        sent.append(copy)
        relayed.append(copy)

    first, second, third = {}, {}, {}
    for piece, (a, b, c) in enumerate(ORDERS):
        first[piece] = push(0, piece, 0, a)
    for piece, (a, b, c) in enumerate(ORDERS):
        second[piece] = [push(0, piece, 1, b)]
    for piece, (a, b, c) in enumerate(ORDERS):
        third[piece] = [push(0, piece, 3, c)]
    local = pltpu.make_async_copy(x_ref, o_ref.at[pl.ds(pl.multiple_of(me * rows, 16), rows)], own_sem)
    local.start()
    for piece in range(3):
        relay(0, piece, 0)
    for piece, (a, b, c) in enumerate(ORDERS):
        first[piece].wait_recv()
        mask = span_mask((a,))
        second[piece].append(push(mask, piece, 2, b))
        third[piece].append(push(mask, piece, 4, c))
        relay(mask, piece, 1)
    for piece, (a, b, c) in enumerate(ORDERS):
        second[piece][0].wait_recv()
        mask = span_mask((b,))
        third[piece].append(push(mask, piece, 5, c))
        relay(mask, piece, 2)
    for piece, (a, b, c) in enumerate(ORDERS):
        second[piece][1].wait_recv()
        mask = span_mask((a, b))
        third[piece].append(push(mask, piece, 6, c))
        relay(mask, piece, 3)
    for turn, dims in enumerate(((2,), (0, 2), (1, 2), (0, 1, 2))):
        for piece, order in enumerate(ORDERS):
            third[piece][turn].wait_recv()
            relay(span_mask([order[d] for d in dims]), piece, 4 + turn)
    for copy in sent:
        copy.wait_send()
    for copy in relayed:
        copy.wait_recv()
    local.wait()


def token_gather(layout, block):
    rows, width = block.shape
    return pl.pallas_call(
        functools.partial(gather_kernel, layout, rows),
        out_shape=jax.ShapeDtypeStruct((GROUP * rows, width), block.dtype),
        in_specs=[pl.BlockSpec(memory_space=pl.ANY)],
        out_specs=pl.BlockSpec(memory_space=pl.ANY),
        scratch_shapes=[
            pltpu.SemaphoreType.DMA((3, 7)),
            pltpu.SemaphoreType.DMA((3, 7)),
            pltpu.SemaphoreType.DMA((3, 8)),
            pltpu.SemaphoreType.DMA((3, 8)),
            pltpu.SemaphoreType.DMA,
        ],
        compiler_params=pltpu.CompilerParams(collective_id=1, has_side_effects=True),
        name="token_gather",
    )(block)


def scatter_kernel(
    layout, rows, p_ref, o_ref, core_in, acc, arrive, core_send, core_recv, send, recv
):
    greet(layout)
    me = layout.member()
    masks = (14, 12, 10, 6, 8, 4, 2, 0)

    def rows_of(mask):
        return pl.ds(pl.multiple_of(jnp.bitwise_xor(me, mask) * rows, 16), rows)

    core = []
    for mask in masks:
        copy = pltpu.make_async_remote_copy(
            src_ref=p_ref.at[rows_of(mask ^ 1)],
            dst_ref=core_in.at[mask // 2],
            send_sem=core_send.at[mask // 2],
            recv_sem=core_recv.at[mask // 2],
            device_id=layout.device(1),
            device_id_type=MESH,
        )
        copy.start()
        core.append(copy)

    def push(piece, mask, dim, slot):
        start, size = PIECES[piece]
        copy = pltpu.make_async_remote_copy(
            src_ref=acc.at[mask // 2, pl.ds(start, size)],
            dst_ref=arrive.at[slot, pl.ds(start, size)],
            send_sem=send.at[piece, slot],
            recv_sem=recv.at[piece, slot],
            device_id=layout.device(1 << dim),
            device_id_type=MESH,
        )
        copy.start()
        return copy

    one, two, three = {}, {}, {}
    for mask, copy in zip(masks, core):
        copy.wait_recv()
        acc[mask // 2] = (
            p_ref[rows_of(mask)].astype(jnp.float32) + core_in[mask // 2].astype(jnp.float32)
        ).astype(jnp.bfloat16)
        for piece, (a, b, c) in enumerate(ORDERS):
            if mask & (1 << a):
                rest = mask ^ (1 << a)
                slot = (1 if rest & (1 << b) else 0) + (2 if rest & (1 << c) else 0)
                one[piece, slot] = push(piece, mask, a, slot)

    def add(piece, slot, mask):
        start, size = PIECES[piece]
        own = acc[mask // 2, pl.ds(start, size)].astype(jnp.float32)
        return own + arrive[slot, pl.ds(start, size)].astype(jnp.float32)

    def keep(piece, slot, mask):
        start, size = PIECES[piece]
        acc[mask // 2, pl.ds(start, size)] = add(piece, slot, mask).astype(jnp.bfloat16)

    for piece, (a, b, c) in enumerate(ORDERS):
        for slot, mask in ((3, span_mask((b, c))), (1, span_mask((b,)))):
            one[piece, slot].wait_recv()
            keep(piece, slot, mask)
            two[piece, slot] = push(piece, mask, b, 4 + slot // 2)
    for piece, (a, b, c) in enumerate(ORDERS):
        mask = span_mask((c,))
        one[piece, 2].wait_recv()
        keep(piece, 2, mask)
        two[piece, 3].wait_recv()
        keep(piece, 5, mask)
        three[piece] = push(piece, mask, c, 6)
    for piece, (a, b, c) in enumerate(ORDERS):
        start, size = PIECES[piece]
        one[piece, 0].wait_recv()
        two[piece, 1].wait_recv()
        partial = add(piece, 0, 0) + arrive[4, pl.ds(start, size)].astype(jnp.float32)
        three[piece].wait_recv()
        o_ref[pl.ds(start, size)] = partial + arrive[6, pl.ds(start, size)].astype(jnp.float32)
    for copy in core + list(one.values()) + list(two.values()) + list(three.values()):
        copy.wait_send()


def token_scatter(layout, partial):
    rows, width = partial.shape[0] // GROUP, partial.shape[1]
    return pl.pallas_call(
        functools.partial(scatter_kernel, layout, rows),
        out_shape=jax.ShapeDtypeStruct((rows, width), jnp.float32),
        in_specs=[pl.BlockSpec(memory_space=pltpu.VMEM)],
        out_specs=pl.BlockSpec(memory_space=pltpu.VMEM),
        scratch_shapes=[
            pltpu.VMEM((8, rows, width), jnp.bfloat16),
            pltpu.VMEM((8, rows, width), jnp.bfloat16),
            pltpu.VMEM((7, rows, width), jnp.bfloat16),
            pltpu.SemaphoreType.DMA((8,)),
            pltpu.SemaphoreType.DMA((8,)),
            pltpu.SemaphoreType.DMA((3, 7)),
            pltpu.SemaphoreType.DMA((3, 7)),
        ],
        compiler_params=pltpu.CompilerParams(
            collective_id=2, has_side_effects=True, vmem_limit_bytes=48 * 1024 * 1024
        ),
        name="token_scatter",
    )(partial)


def softmax(query, keys, query_ids, key_ids):
    scores = dot_cols(query, keys) * (1.0 / HD)
    scores = jnp.where(key_ids <= query_ids, scores, -1e30)
    shifted = jnp.exp(scores - jnp.max(scores, axis=1, keepdims=True))
    return shifted / jnp.sum(shifted, axis=1, keepdims=True)


def attend_kernel(heads, q_ref, kv_ref, row_ref, col_ref, o_ref):
    base = heads * HD
    keys = kv_ref[:, base : base + HD]
    values = kv_ref[:, base + HD : base + 2 * HD]
    outs = []
    for head in range(heads):
        query = q_ref[:, head * HD : (head + 1) * HD]
        probs = softmax(query, keys, col_ref[0], row_ref[0])
        outs.append(dot(probs.astype(jnp.bfloat16), values))
    o_ref[...] = jnp.concatenate(outs, axis=1).astype(jnp.bfloat16)


def attend_back_kernel(heads, q_ref, kv_ref, row_ref, col_ref, g_ref, o_ref, grad_kv):
    step = pl.program_id(1)
    span, length = q_ref.shape[0], kv_ref.shape[0]
    base = heads * HD
    keys = kv_ref[:, base : base + HD]
    values = kv_ref[:, base + HD : base + 2 * HD]
    grads, grad_keys, grad_values = [], 0.0, 0.0
    for head in range(heads):
        query = q_ref[:, head * HD : (head + 1) * HD]
        grad = g_ref[:, head * HD : (head + 1) * HD]
        probs = softmax(query, keys, col_ref[0], row_ref[0])
        grad_probs = dot_cols(grad, values)
        centre = jnp.sum(probs * grad_probs, axis=1, keepdims=True)
        grad_scores = (probs * (grad_probs - centre)).astype(jnp.bfloat16)
        grads.append(dot(grad_scores, keys) * (1.0 / HD))
        grad_keys = grad_keys + dot_rows(grad_scores, query) * (1.0 / HD)
        grad_values = grad_values + dot_rows(probs.astype(jnp.bfloat16), grad)
    both = jnp.concatenate([grad_keys, grad_values], axis=1)

    @pl.when(step == 0)
    def _():
        grad_kv[...] = both

    @pl.when(step > 0)
    def _():
        grad_kv[...] += both

    start = pl.multiple_of(step * span, span)
    o_ref[pl.ds(start, span), :base] = jnp.concatenate(grads, axis=1).astype(jnp.bfloat16)

    @pl.when(step == pl.num_programs(1) - 1)
    def _():
        o_ref[:, base:] = grad_kv[...].astype(jnp.bfloat16)


def attention_specs(qkv, ids, heads):
    count, length = ids.shape
    span = min(512, length)
    blocks = length // span
    width = qkv.shape[1]
    specs = [
        pl.BlockSpec((span, width), lambda i, j: (i * blocks + j, 0)),
        pl.BlockSpec((length, width), lambda i, j: (i, 0)),
        pl.BlockSpec((1, 1, length), lambda i, j: (i, 0, 0)),
        pl.BlockSpec((1, span, 1), lambda i, j: (i, j, 0)),
    ]
    args = (qkv, qkv, ids[:, None, :], ids[:, :, None])
    return (count, blocks), span, length, specs, args


def attend(qkv, ids, heads):
    grid, span, length, specs, args = attention_specs(qkv, ids, heads)
    return pl.pallas_call(
        functools.partial(attend_kernel, heads),
        grid=grid,
        in_specs=specs,
        out_specs=pl.BlockSpec((span, heads * HD), lambda i, j: (i * grid[1] + j, 0)),
        out_shape=jax.ShapeDtypeStruct((qkv.shape[0], heads * HD), jnp.bfloat16),
        compiler_params=pltpu.CompilerParams(vmem_limit_bytes=48 * 1024 * 1024),
        name="attend",
    )(*args)


def attend_back(qkv, ids, grad, heads):
    grid, span, length, specs, args = attention_specs(qkv, ids, heads)
    width = qkv.shape[1]
    return pl.pallas_call(
        functools.partial(attend_back_kernel, heads),
        grid=grid,
        in_specs=specs
        + [pl.BlockSpec((span, heads * HD), lambda i, j: (i * grid[1] + j, 0))],
        out_specs=pl.BlockSpec((length, width), lambda i, j: (i, 0)),
        out_shape=jax.ShapeDtypeStruct(qkv.shape, jnp.bfloat16),
        scratch_shapes=[pltpu.VMEM((length, 2 * HD), jnp.float32)],
        compiler_params=pltpu.CompilerParams(vmem_limit_bytes=48 * 1024 * 1024),
        name="attend_back",
    )(*args, grad)


def swap(array, axis, size, mask):
    return lax.ppermute(array, axis, [(i, i ^ mask) for i in range(size)])


def gather_seq(layout, array):
    me = lax.axis_index("seq")
    stack = array[None]
    for bit in reversed(range(layout.seq_bits)):
        other = swap(stack, "seq", layout.seq, 1 << bit)
        upper = (me >> bit) % 2 == 1
        pair = jnp.stack([jnp.where(upper, other, stack), jnp.where(upper, stack, other)], axis=1)
        stack = pair.reshape((-1,) + array.shape)
    return stack


def slices(array, start, size):
    return lax.dynamic_slice_in_dim(array, start, size, axis=1)


def body(
    tokens,
    block_ids,
    gain_attn,
    w_query,
    w_key,
    w_value,
    w_out,
    gain_mlp,
    w_gate,
    w_up,
    w_down,
    cotangent,
):
    layout = Layout(lax.axis_size("seq"), lax.axis_size("fsdp"))
    fsdp, share = layout.fsdp, layout.share
    seq_me, fsdp_me = lax.axis_index("seq"), lax.axis_index("fsdp")
    rows, width = tokens.shape[1], tokens.shape[2]
    depth = w_gate.shape[0]
    hidden_cols = w_gate.shape[1] // GROUP
    heads = H // GROUP
    query_cols = heads * HD
    kv_share = GROUP // KVH
    column_group = seq_me * share + fsdp_me % share

    def attn_part(target):
        kv = (target // kv_share) * HD
        return jnp.concatenate(
            [
                slices(w_query, target * query_cols, query_cols),
                slices(w_key, kv, HD),
                slices(w_value, kv, HD),
                slices(w_out, target * query_cols, query_cols),
                jnp.broadcast_to(gain_attn[:, None], (depth, 64)),
                jnp.broadcast_to(gain_mlp[:, None], (depth, 64)),
            ],
            axis=1,
        )

    def in_part(target):
        start = target * hidden_cols
        return jnp.concatenate(
            [slices(w_gate, start, hidden_cols), slices(w_up, start, hidden_cols)], axis=1
        )

    def down_part(target):
        return slices(w_down, target * hidden_cols, hidden_cols)

    def collect(part, after=None):
        whole = None
        for mask in range(fsdp):
            target = seq_me * share + jnp.bitwise_xor(fsdp_me, mask) % share
            piece = part(target)
            if mask:
                if after is not None:
                    piece, _ = lax.optimization_barrier((piece, after))
                piece = swap(piece, "fsdp", fsdp, mask)
            if whole is None:
                whole = jnp.zeros((fsdp * piece.shape[0], piece.shape[1]), piece.dtype)
            whole = lax.dynamic_update_slice_in_dim(
                whole, piece, jnp.bitwise_xor(fsdp_me, mask) * depth, axis=0
            )
        return whole

    attn_all = collect(attn_part)
    x_all = token_gather(layout, tokens[0])
    in_all = collect(in_part, attn_all)
    down_all = collect(down_part, attn_all)
    w_in = attn_all[:, : query_cols + 2 * HD]
    w_back = attn_all[:, query_cols + 2 * HD : 2 * query_cols + 2 * HD]
    attn_gain = attn_all[:, 2 * query_cols + 2 * HD].astype(jnp.float32)[None]
    mlp_gain = attn_all[:, 2 * query_cols + 2 * HD + 64].astype(jnp.float32)[None]

    id_rows = [block_ids]
    for bit in range(share.bit_length() - 1):
        id_rows = id_rows + [swap(r, "fsdp", fsdp, 1 << bit) for r in id_rows]
    ids = jnp.zeros((share, block_ids.shape[1]), block_ids.dtype)
    for mask, row in enumerate(id_rows):
        ids = lax.dynamic_update_slice_in_dim(
            ids, row, jnp.bitwise_xor(fsdp_me % share, mask), axis=0
        )

    inputs_all = x_all.astype(jnp.float32)
    normed_one = (inputs_all * rms_factor(inputs_all) * attn_gain).astype(jnp.bfloat16)
    qkv = dot(normed_one, w_in).astype(jnp.bfloat16)
    attended = attend(qkv, ids, heads)
    branch = token_scatter(layout, dot_cols(attended, w_back).astype(jnp.bfloat16))
    inputs = tokens[0].astype(jnp.float32)
    middle = inputs + RESIDUAL * branch
    factor_two = rms_factor(middle)
    normed_two = token_gather(
        layout, (middle * factor_two * mlp_gain).astype(jnp.bfloat16)
    )
    gate_up = dot(normed_two, in_all)
    gate, upward = gate_up[:, :hidden_cols], gate_up[:, hidden_cols:]
    sigma = jax.nn.sigmoid(gate)
    hidden = (gate * sigma * upward).astype(jnp.bfloat16)
    grad_all = token_gather(layout, cotangent[0])
    grad_down_in = (RESIDUAL * grad_all.astype(jnp.float32)).astype(jnp.bfloat16)
    grad_hidden = dot(grad_down_in, down_all)
    grad_upward = (grad_hidden * gate * sigma).astype(jnp.bfloat16)
    grad_gate_in = (grad_hidden * upward * sigma * (1.0 + gate * (1.0 - sigma))).astype(
        jnp.bfloat16
    )
    grad_in = jnp.concatenate([grad_gate_in, grad_upward], axis=1)
    grad_normed_two = token_scatter(layout, dot_cols(grad_in, in_all).astype(jnp.bfloat16))
    down = token_scatter(layout, dot_cols(hidden, down_all).astype(jnp.bfloat16))
    mixed = (middle + RESIDUAL * down).astype(jnp.bfloat16)

    def spread(partials):
        held = {}
        for mask in range(fsdp):
            piece = lax.dynamic_slice_in_dim(
                partials, jnp.bitwise_xor(fsdp_me, mask) * depth, depth, axis=0
            )
            held[mask] = swap(piece, "fsdp", fsdp, mask) if mask else piece
        sums = []
        for low in range(share):
            total = 0.0
            for high in range(0, fsdp, share):
                total = total + held[low + high].astype(jnp.float32)
            sums.append(total.astype(jnp.bfloat16))
        ordered = []
        mine = fsdp_me % share
        for column in range(share):
            pick = sums[0]
            for mask in range(1, share):
                pick = jnp.where(jnp.bitwise_xor(mine, mask) == column, sums[mask], pick)
            ordered.append(pick)
        return gather_seq(layout, jnp.stack(ordered))

    down_parts = spread(dot_rows(grad_down_in, hidden).astype(jnp.bfloat16))
    in_parts = spread(dot_rows(normed_two, grad_in).astype(jnp.bfloat16))

    grad_output = cotangent[0].astype(jnp.float32)
    gain_two_term = jnp.sum(grad_normed_two * middle * factor_two, axis=0)
    grad_middle = grad_output + norm_back(grad_normed_two, middle, factor_two, mlp_gain)
    grad_branch = token_gather(layout, (RESIDUAL * grad_middle).astype(jnp.bfloat16))
    grad_attended = dot(grad_branch, w_back).astype(jnp.bfloat16)
    grad_qkv = attend_back(qkv, ids, grad_attended, heads)
    grad_normed_one = token_scatter(layout, dot_cols(grad_qkv, w_in).astype(jnp.bfloat16))
    attn_parts = spread(
        jnp.concatenate(
            [dot_rows(normed_one, grad_qkv), dot_rows(grad_branch, attended)], axis=1
        ).astype(jnp.bfloat16)
    )
    factor_one = rms_factor(inputs)
    gain_one_term = jnp.sum(grad_normed_one * inputs * factor_one, axis=0)
    grad_inputs = grad_middle + norm_back(grad_normed_one, inputs, factor_one, attn_gain)

    gains = jnp.stack([gain_one_term, gain_two_term])
    gains = lax.psum(gains, ("seq", "fsdp"))
    gains = lax.dynamic_slice_in_dim(gains, fsdp_me * depth, depth, axis=1)

    def join(parts, start, size):
        return jnp.concatenate(
            [
                parts[i][j, :, start : start + size]
                for i in range(layout.seq)
                for j in range(share)
            ],
            axis=1,
        ).astype(jnp.float32)

    def join_shared(parts, start, size):
        columns = [
            parts[i][j, :, start : start + size].astype(jnp.float32)
            for i in range(layout.seq)
            for j in range(share)
        ]
        return jnp.concatenate(
            [
                sum(columns[i : i + kv_share][1:], columns[i])
                for i in range(0, GROUP, kv_share)
            ],
            axis=1,
        )

    return (
        mixed[None],
        grad_inputs.astype(jnp.bfloat16)[None],
        gains[0],
        join(attn_parts, 0, query_cols),
        join_shared(attn_parts, query_cols, HD),
        join_shared(attn_parts, query_cols + HD, HD),
        join(attn_parts, query_cols + 2 * HD, query_cols),
        gains[1],
        join(in_parts, 0, hidden_cols),
        join(in_parts, hidden_cols, hidden_cols),
        join(down_parts, 0, hidden_cols),
    )


def solution(mesh):
    tokens, rows = P("fsdp", "seq", None), P("fsdp", None)
    return jax.shard_map(
        body,
        mesh=mesh,
        in_specs=(tokens, rows, P("fsdp"), rows, rows, rows, rows, P("fsdp"), rows, rows, rows, tokens),
        out_specs=(tokens, tokens, P("fsdp"), rows, rows, rows, rows, P("fsdp"), rows, rows, rows),
        check_vma=False,
    )
```

time: 4640 us -> 960 us (0.21)
  waiting for transfers between devices: 4130 us -> 204 us
  Pallas kernels: 0 us -> 332 us
  matrix products: 222 us -> 97.2 us
  local copies, waits for them, and re-layouts: 47.5 us -> 104 us
  other arithmetic: 119 us -> 71 us
    all_gather x7 -> x0, waiting for transfers between devices: 2140 us -> none  [the longest x1 633 us: body(): lax.all_gather(w_up, 'fsdp', axis=0, tiled=True)]
    unnamed x11 -> x0, waiting for transfers between devices: 1540 us -> none
    pallas_call x0 -> x10, Pallas kernels: none -> 332 us  [the longest x4 157 us: token_gather(): pl.pallas_call(functools.partial(gather_kernel, layout, rows), out_shape=...]
    reduce_scatter x1 -> x0, waiting for transfers between devices: 232 us -> none  [reduce_terms(): lax.psum_scatter(build(lambda matrix: matrix, arrays).astype(jnp.bfloat16...]
    ppermute x0 -> x51, waiting for transfers between devices: none -> 204 us  [swap(): return lax.ppermute(array, axis, [(i, i ^ mask) for i in range(size)])]
    psum x1 -> x0, waiting for transfers between devices: 198 us -> none  [reduce_terms(): return lax.psum(owned, 'seq').astype(jnp.float32)]
    dot_general x26 -> x12, matrix products: 217 us -> 97.2 us  [the longest x4 36.5 us: dot(): return jnp.dot(left, right, preferred_element_type=jnp.float32)]
    concatenate x2 -> x9, other arithmetic: 106 us -> 6.26 us  [the longest x7 6.05 us: in_part(): jnp.concatenate([slices(w_gate, start, hidden_cols), slices(w_up, start,...]
  transfers between devices with their start and end apart: 18 -> 51, of which waited for: 13 -> 20; matrix products, arithmetic and copies ran while one was open for 5% -> 15% of each run, Pallas kernels for 0% -> 22%
where the time goes in v1:
time: 960 us; the launch traced here: 952 us
  Pallas kernels  332 us (35%)
  waiting for transfers between devices  204 us (21%)
  local copies, waits for them, and re-layouts  104 us (11%)
  matrix products  97.2 us (10%)
  starting transfers between devices  78.1 us (8%)
  other arithmetic  71 us (7%)
  blocking collectives  63 us (7%)
    ppermute x51, waiting for transfers between devices, swap(): return lax.ppermute(array, axis, [(i, i ^ mask) for i in range(size)])  204 us
    pallas_call x4, Pallas kernels, token_gather(): pl.pallas_call(functools.partial(gather_kernel, layout, rows), out_shape=...  157 us
    pallas_call x4, Pallas kernels, token_scatter(): pl.pallas_call(functools.partial(scatter_kernel, layout, rows), out_shape...  155 us
    ppermute x51, starting transfers between devices, swap(): return lax.ppermute(array, axis, [(i, i ^ mask) for i in range(size)])  78.1 us
    psum x1, blocking collectives, body(): gains = lax.psum(gains, ('seq', 'fsdp'))  63 us
    dot_general x4, matrix products, dot(): return jnp.dot(left, right, preferred_element_type=jnp.float32)  36.5 us
    dot_general x4, matrix products, dot_cols(): lax.dot_general(left, right, (((1,), (1,)), ((), ())), preferred_element_...  34.8 us
    dot_general x4, matrix products, dot_rows(): lax.dot_general(left, right, (((0,), (0,)), ((), ())), preferred_element_...  25.9 us
  transfers between devices with their start and end apart: 51, of which 20 were waited for; matrix products, arithmetic and copies ran while one was open for 15% of the time, Pallas kernels for 22%

profile of v1, /device:TPU:15, one launch (start us, length us, event | category | flops | bytes accessed | tf_op | source)
XLA Modules:
  0.0 951.6 jit_solution(12412715483410986264)
XLA Ops:
  15.1 44.2 %token_gather.4 = bf16[2048,2048]{1,0:T(8,128)(2,1)} custom-call(bf16[128,2048]{1,0:T(8,128)(2,1)} %bitcast.510), custom_call_target="tpu_custom_call" | custom-call | tf_op jit(solution)/shard_map/token_gather/pallas_call | solution.py:159
  59.4 5.1 fusion
  86.1 34.8 %token_gather.6 = bf16[2048,2048]{1,0:T(8,128)(2,1)} custom-call(bf16[128,2048]{1,0:T(8,128)(2,1)} %bitcast.513), custom_call_target="tpu_custom_call" | custom-call | tf_op jit(solution)/shard_map/token_gather/pallas_call | solution.py:159
  138.6 11.7 %collective-permute-done.5 = bf16[256,512]{1,0:T(8,128)(2,1)} collective-permute-done((bf16[256,512]{1,0:T(8,128)(2,1)}, bf16[256,512]{1,0:T(8,128)(2,1)}, u32[]{:S(2)}, u32[]{:S(2)}) %collective-permute-start.5) | collective-permute-done | bytes 262176 | tf_op jit(solution)/shard_map/ppermute | solution.py:378
  157.6 4.8 collective-permute-done.6
  166.3 6.4 convolution_convert_fusion.6.q_ref.kv_ref
  172.7 9.1 attend.1
  181.8 6.8 convolution_convert_fusion.3.p_ref
  188.6 37.0 %token_scatter.4 = f32[128,2048]{1,0:T(8,128)S(1)} custom-call(bf16[2048,2048]{1,0:T(8,128)(2,1)} %convolution_convert_fusion.3.p_ref), custom_call_target="tpu_custom_call" | custom-call | tf_op jit(solution)/shard_map/token_scatter/pallas_call | solution.py:258
  230.4 44.2 %token_gather.5 = bf16[2048,2048]{1,0:T(8,128)(2,1)} custom-call(bf16[128,2048]{1,0:T(8,128)(2,1)} %multiply_convert_fusion.9.x_ref), custom_call_target="tpu_custom_call" | custom-call | tf_op jit(solution)/shard_map/token_gather/pallas_call | solution.py:159
  287.9 6.7 collective-permute-done.21
  294.7 3.8 collective-permute-start.12
  308.8 9.1 collective-permute-done.11
  320.5 8.7 collective-permute-done.12
  332.9 34.4 %collective-permute-done.14 = bf16[256,1024]{1,0:T(8,128)(2,1)} collective-permute-done((bf16[256,1024]{1,0:T(8,128)(2,1)}, bf16[256,1024]{1,0:T(8,128)(2,1)}, u32[]{:S(2)}, u32[]{:S(2)}) %collective-permute-start.14) | collective-permute-done | bytes 524320 | tf_op jit(solution)/shard_map/ppermute | solution.py:378
  369.2 10.7 %collective-permute-done.15 = bf16[256,1024]{1,0:T(8,128)(2,1)S(1)} collective-permute-done((bf16[256,1024]{1,0:T(8,128)(2,1)}, bf16[256,1024]{1,0:T(8,128)(2,1)S(1)}, u32[]{:S(2)}, u32[]{:S(2)}) %collective-permute-start.15) | collective-permute-done | bytes 524320 | tf_op jit(solution)/shard_map/ppermute | solution.py:378
  380.8 10.8 %collective-permute-done.16 = bf16[256,1024]{1,0:T(8,128)(2,1)S(1)} collective-permute-done((bf16[256,1024]{1,0:T(8,128)(2,1)}, bf16[256,1024]{1,0:T(8,128)(2,1)S(1)}, u32[]{:S(2)}, u32[]{:S(2)}) %collective-permute-start.16) | collective-permute-done | bytes 524320 | tf_op jit(solution)/shard_map/ppermute | solution.py:378
  392.4 14.9 %fusion.83 = f32[2048,1024]{0,1:T(8,128)} fusion(bf16[2048,2048]{1,0:T(8,128)(2,1)} %token_gather.5, bf16[2048,1024]{1,0:T(8,128)(2,1)} %constant_dynamic-update-slice_fusion.40), kind=kOutput, calls=%fused_computation.419 | convolution fusion | flops 8589934592 | bytes 20971520 | tf_op jit(solution)/shard_map/dot_general | solution.py:22
  407.4 9.3 multiply_convert_fusion.4
  416.7 12.5 %convolution_convert_fusion.4 = bf16[2048,1024]{0,1:T(8,128)(2,1)} fusion(bf16[2048,2048]{1,0:T(8,128)(2,1)} %token_gather.5, bf16[2048,512]{0,1:T(8,128)(2,1)S(1)} %get-tuple-element.63, bf16[2048,512]{0,1:T(8,128)(2,1)S(1)} %get-tuple-element.62), kind=kOutput, calls=%fused_computation.30 | convolution fusion | flops 8600420352 | bytes 16777216 | tf_op jit(solution)/shard_map/dot_general | solution.py:32
  429.2 13.8 %convolution_convert_fusion.1.p_ref = bf16[2048,2048]{1,0:T(8,128)(2,1)} fusion(bf16[2048,1024]{1,0:T(8,128)(2,1)} %constant_dynamic-update-slice_fusion.40, bf16[2048,512]{0,1:T(8,128)(2,1)S(1)} %get-tuple-element.63, bf16[2048,512]{0,1:T(8,128)(2,1)S(1)} %get-tuple-element.62), kind=kOutput, calls=%fused_computation.8 | convolution fusion | flops 8602517504 | bytes 16777216 | tf_op jit(solution)/shard_map/dot_general | solution.py:26
  443.0 5.7 fusion.5
  448.7 8.6 convolution_convert_fusion.2.p_ref
  457.3 37.8 %token_scatter.6 = f32[128,2048]{1,0:T(8,128)S(1)} custom-call(bf16[2048,2048]{1,0:T(8,128)(2,1)} %convolution_convert_fusion.1.p_ref), custom_call_target="tpu_custom_call" | custom-call | tf_op jit(solution)/shard_map/token_scatter/pallas_call | solution.py:258
  495.5 37.1 %token_scatter.5 = f32[128,2048]{1,0:T(8,128)S(1)} custom-call(bf16[2048,2048]{1,0:T(8,128)(2,1)} %convolution_convert_fusion.2.p_ref), custom_call_target="tpu_custom_call" | custom-call | tf_op jit(solution)/shard_map/token_scatter/pallas_call | solution.py:258
  534.4 34.1 %token_gather.7 = bf16[2048,2048]{1,0:T(8,128)(2,1)} custom-call(bf16[128,2048]{1,0:T(8,128)(2,1)} %get-tuple-element.58.x_ref), custom_call_target="tpu_custom_call" | custom-call | tf_op jit(solution)/shard_map/token_gather/pallas_call | solution.py:159
  568.5 4.9 convolution_convert_fusion.7
  573.4 5.9 convolution_convert_fusion.8.g_ref
  579.3 11.1 %attend_back.1 = bf16[2048,256]{1,0:T(8,128)(2,1)S(1)} custom-call(bf16[2048,256]{1,0:T(8,128)(2,1)S(1)} %convolution_convert_fusion.6.q_ref.kv_ref, bf16[2048,256]{1,0:T(8,128)(2,1)S(1)} %convolution_convert_fusion.6.q_ref.kv_ref, s32[4,1,512]{2,1,0:T(1,128)S(1)} %broadcast_in_dim.25.row_ref, s32[4,512,1]{2,1,0:T(8,128)S(1)} %copy.33.col_ref, ...), custom_call_target="tpu_custom_call" | custom-call | tf_op jit(solution)/shard_map/attend_back/pallas_call | solution.py:364
  593.4 5.7 convolution_convert_fusion.p_ref
  605.0 42.8 %token_scatter.7 = f32[128,2048]{1,0:T(8,128)S(1)} custom-call(bf16[2048,2048]{1,0:T(8,128)(2,1)} %convolution_convert_fusion.p_ref), custom_call_target="tpu_custom_call" | custom-call | tf_op jit(solution)/shard_map/token_scatter/pallas_call | solution.py:258
  656.0 6.3 collective-permute-done.28
  666.5 14.7 %collective-permute-done.48 = bf16[256,512]{0,1:T(8,128)(2,1)S(1)} collective-permute-done((bf16[256,512]{0,1:T(8,128)(2,1)S(1)}, bf16[256,512]{0,1:T(8,128)(2,1)S(1)}, u32[]{:S(2)}, u32[]{:S(2)}) %collective-permute-start.48) | collective-permute-done | bytes 262176 | tf_op jit(solution)/shard_map/ppermute | solution.py:378
  686.8 7.5 collective-permute-start.31
  699.7 3.6 collective-permute-start.38
  703.3 8.4 collective-permute-done.43
  717.0 35.5 %collective-permute-done.39 = bf16[256,1024]{0,1:T(8,128)(2,1)S(1)} collective-permute-done((bf16[256,1024]{0,1:T(8,128)(2,1)S(1)}, bf16[256,1024]{0,1:T(8,128)(2,1)S(1)}, u32[]{:S(2)}, u32[]{:S(2)}) %collective-permute-start.39) | collective-permute-done | bytes 524320 | tf_op jit(solution)/shard_map/ppermute | solution.py:378
  759.7 4.0 collective-permute-done.38
  767.1 63.0 %psum.7 = f32[2,2048]{1,0:T(2,128)S(1)} all-reduce(f32[2,2048]{1,0:T(2,128)S(1)} %pad_maximum_fusion.13), channel_id=1, replica_groups=mesh['seq'=4,'fsdp'=8] {'seq','fsdp'}, use_global_device_ids=true, to_apply=%region_7.8 | all-reduce | flops 4096 | bytes 32768 | tf_op jit(solution)/shard_map/psum | solution.py:547
  856.4 25.7 %collective-permute-done.40 = bf16[1,4,256,1024]{2,3,1,0:T(8,128)(2,1)} collective-permute-done((bf16[1,4,256,1024]{2,3,1,0:T(8,128)(2,1)}, bf16[1,4,256,1024]{2,3,1,0:T(8,128)(2,1)}, u32[]{:S(2)}, u32[]{:S(2)}) %collective-permute-start.40) | collective-permute-done | bytes 2097184 | tf_op jit(solution)/shard_map/ppermute | solution.py:378
  893.1 7.3 copy.45
  908.9 4.4 convert_element_type.432
  913.3 5.2 select_bitcast_fusion.1
  918.5 7.6 pad_maximum_fusion
  926.1 11.4 %copy.44 = bf16[2,2,4,256,1024]{4,3,2,1,0:T(8,128)(2,1)} copy(bf16[2,2,4,256,1024]{3,4,2,0,1:T(8,128)(2,1)} %pad_maximum_fusion) | data formatting | bytes 16777216 | tf_op jit(solution)/shard_map/stack | solution.py:387
  937.5 3.9 slice_bitcast_fusion
  942.7 4.4 convert_element_type.418
  947.1 4.4 convert_element_type.417
  (344 shorter events, 199.0 us)
Async XLA Ops:
  0.7 81.9 %collective-permute-start.8 = (s32[1,512]{1,0:T(1,128)}, s32[1,512]{1,0:T(1,128)S(1)}, u32[]{:S(2)}, u32[]{:S(2)}) collective-permute-start(s32[1,512]{1,0:T(1,128)} %param.13), channel_id=1, source_target_pairs={{0,2},{1,3},{2,0},{3,1},{4,6},{5,7},{6,4},{7,5},{8,10},{9,11},{10,... | collective-permute-start | bytes 6152 | tf_op jit(solution)/shard_map/ppermute | solution.py:378
  7.3 119.8 %collective-permute-start = (bf16[256,512]{1,0:T(8,128)(2,1)}, bf16[256,512]{1,0:T(8,128)(2,1)}, u32[]{:S(2)}, u32[]{:S(2)}) collective-permute-start(bf16[256,512]{1,0:T(8,128)(2,1)} %concatenate.77), channel_id=1, source_target_pairs={{0,1},{1,0},{2,3},{3,2},{4,5},{5,4},{6,7},{7,6},{8,9},{9,8},{10,11... | collective-permute-start | bytes 786440 | tf_op jit(solution)/shard_map/ppermute | solution.py:378
  8.4 121.8 %collective-permute-start.1 = (bf16[256,512]{1,0:T(8,128)(2,1)}, bf16[256,512]{1,0:T(8,128)(2,1)}, u32[]{:S(2)}, u32[]{:S(2)}) collective-permute-start(bf16[256,512]{1,0:T(8,128)(2,1)} %concatenate.78), channel_id=1, source_target_pairs={{0,2},{1,3},{2,0},{3,1},{4,6},{5,7},{6,4},{7,5},{8,10},{9,11},{10,... | collective-permute-start | bytes 786440 | tf_op jit(solution)/shard_map/ppermute | solution.py:378
  10.2 124.4 %collective-permute-start.2 = (bf16[256,512]{1,0:T(8,128)(2,1)}, bf16[256,512]{1,0:T(8,128)(2,1)}, u32[]{:S(2)}, u32[]{:S(2)}) collective-permute-start(bf16[256,512]{1,0:T(8,128)(2,1)} %concatenate.79), channel_id=1, source_target_pairs={{0,3},{1,2},{2,1},{3,0},{4,7},{5,6},{6,5},{7,4},{8,11},{9,10},{10,... | collective-permute-start | bytes 786440 | tf_op jit(solution)/shard_map/ppermute | solution.py:378
  12.5 123.2 %collective-permute-start.3 = (bf16[256,512]{1,0:T(8,128)(2,1)}, bf16[256,512]{1,0:T(8,128)(2,1)}, u32[]{:S(2)}, u32[]{:S(2)}) collective-permute-start(bf16[256,512]{1,0:T(8,128)(2,1)} %concatenate.80), channel_id=1, source_target_pairs={{0,4},{1,5},{2,6},{3,7},{4,0},{5,1},{6,2},{7,3},{8,12},{9,13},{10,... | collective-permute-start | bytes 786440 | tf_op jit(solution)/shard_map/ppermute | solution.py:378
  85.1 39.3 %collective-permute-start.9 = (s32[1,512]{1,0:T(1,128)S(1)}, s32[1,512]{1,0:T(1,128)S(1)}, u32[]{:S(2)}, u32[]{:S(2)}) collective-permute-start(s32[1,512]{1,0:T(1,128)S(1)} %collective-permute-done.7), channel_id=1, source_target_pairs={{0,2},{1,3},{2,0},{3,1},{4,6},{5,7},{6,4},{7,5},{8,10},{9,11},{10,... | collective-permute-start | bytes 6152 | tf_op jit(solution)/shard_map/ppermute | solution.py:378
  124.3 25.9 %collective-permute-start.5 = (bf16[256,512]{1,0:T(8,128)(2,1)}, bf16[256,512]{1,0:T(8,128)(2,1)}, u32[]{:S(2)}, u32[]{:S(2)}) collective-permute-start(bf16[256,512]{1,0:T(8,128)(2,1)} %concatenate.82), channel_id=1, source_target_pairs={{0,6},{1,7},{2,4},{3,5},{4,2},{5,3},{6,0},{7,1},{8,14},{9,15},{10,... | collective-permute-start | bytes 786440 | tf_op jit(solution)/shard_map/ppermute | solution.py:378
  127.1 27.7 %collective-permute-start.4 = (bf16[256,512]{1,0:T(8,128)(2,1)}, bf16[256,512]{1,0:T(8,128)(2,1)}, u32[]{:S(2)}, u32[]{:S(2)}) collective-permute-start(bf16[256,512]{1,0:T(8,128)(2,1)} %concatenate.81), channel_id=1, source_target_pairs={{0,5},{1,4},{2,7},{3,6},{4,1},{5,0},{6,3},{7,2},{8,13},{9,12},{10,... | collective-permute-start | bytes 786440 | tf_op jit(solution)/shard_map/ppermute | solution.py:378
  130.2 32.3 %collective-permute-start.6 = (bf16[256,512]{1,0:T(8,128)(2,1)}, bf16[256,512]{1,0:T(8,128)(2,1)}, u32[]{:S(2)}, u32[]{:S(2)}) collective-permute-start(bf16[256,512]{1,0:T(8,128)(2,1)} %concatenate.83), channel_id=1, source_target_pairs={{0,7},{1,6},{2,5},{3,4},{4,3},{5,2},{6,1},{7,0},{8,15},{9,14},{10,... | collective-permute-start | bytes 786440 | tf_op jit(solution)/shard_map/ppermute | solution.py:378
  163.6 111.0 %collective-permute-start.17 = (bf16[256,512]{1,0:T(8,128)(2,1)}, bf16[256,512]{1,0:T(8,128)(2,1)S(1)}, u32[]{:S(2)}, u32[]{:S(2)}) collective-permute-start(bf16[256,512]{1,0:T(8,128)(2,1)} %get-tuple-element.32), channel_id=1, source_target_pairs={{0,1},{1,0},{2,3},{3,2},{4,5},{5,4},{6,7},{7,6},{8,9},{9,8},{10,11... | collective-permute-start | bytes 786440 | tf_op jit(solution)/shard_map/ppermute | solution.py:378
  163.9 115.9 %collective-permute-start.18 = (bf16[256,512]{1,0:T(8,128)(2,1)}, bf16[256,512]{1,0:T(8,128)(2,1)}, u32[]{:S(2)}, u32[]{:S(2)}) collective-permute-start(bf16[256,512]{1,0:T(8,128)(2,1)} %get-tuple-element.33), channel_id=1, source_target_pairs={{0,2},{1,3},{2,0},{3,1},{4,6},{5,7},{6,4},{7,5},{8,10},{9,11},{10,... | collective-permute-start | bytes 786440 | tf_op jit(solution)/shard_map/ppermute | solution.py:378
  163.9 118.1 %collective-permute-start.19 = (bf16[256,512]{1,0:T(8,128)(2,1)}, bf16[256,512]{1,0:T(8,128)(2,1)}, u32[]{:S(2)}, u32[]{:S(2)}) collective-permute-start(bf16[256,512]{1,0:T(8,128)(2,1)} %get-tuple-element.34), channel_id=1, source_target_pairs={{0,3},{1,2},{2,1},{3,0},{4,7},{5,6},{6,5},{7,4},{8,11},{9,10},{10,... | collective-permute-start | bytes 786440 | tf_op jit(solution)/shard_map/ppermute | solution.py:378
  227.8 72.5 %collective-permute-start.22 = (bf16[256,512]{1,0:T(8,128)(2,1)}, bf16[256,512]{1,0:T(8,128)(2,1)}, u32[]{:S(2)}, u32[]{:S(2)}) collective-permute-start(bf16[256,512]{1,0:T(8,128)(2,1)} %get-tuple-element.37), channel_id=1, source_target_pairs={{0,6},{1,7},{2,4},{3,5},{4,2},{5,3},{6,0},{7,1},{8,14},{9,15},{10,... | collective-permute-start | bytes 786440 | tf_op jit(solution)/shard_map/ppermute | solution.py:378
  229.3 55.5 %collective-permute-start.20 = (bf16[256,512]{1,0:T(8,128)(2,1)}, bf16[256,512]{1,0:T(8,128)(2,1)}, u32[]{:S(2)}, u32[]{:S(2)}) collective-permute-start(bf16[256,512]{1,0:T(8,128)(2,1)} %get-tuple-element.35), channel_id=1, source_target_pairs={{0,4},{1,5},{2,6},{3,7},{4,0},{5,1},{6,2},{7,3},{8,12},{9,13},{10,... | collective-permute-start | bytes 786440 | tf_op jit(solution)/shard_map/ppermute | solution.py:378
  275.4 19.3 %collective-permute-start.21 = (bf16[256,512]{1,0:T(8,128)(2,1)}, bf16[256,512]{1,0:T(8,128)(2,1)}, u32[]{:S(2)}, u32[]{:S(2)}) collective-permute-start(bf16[256,512]{1,0:T(8,128)(2,1)} %get-tuple-element.36), channel_id=1, source_target_pairs={{0,5},{1,4},{2,7},{3,6},{4,1},{5,0},{6,3},{7,2},{8,13},{9,12},{10,... | collective-permute-start | bytes 786440 | tf_op jit(solution)/shard_map/ppermute | solution.py:378
  279.9 22.8 %collective-permute-start.23 = (bf16[256,512]{1,0:T(8,128)(2,1)}, bf16[256,512]{1,0:T(8,128)(2,1)}, u32[]{:S(2)}, u32[]{:S(2)}) collective-permute-start(bf16[256,512]{1,0:T(8,128)(2,1)} %get-tuple-element.38), channel_id=1, source_target_pairs={{0,7},{1,6},{2,5},{3,4},{4,3},{5,2},{6,1},{7,0},{8,15},{9,14},{10,... | collective-permute-start | bytes 786440 | tf_op jit(solution)/shard_map/ppermute | solution.py:378
  282.0 24.4 %collective-permute-start.10 = (bf16[256,1024]{1,0:T(8,128)(2,1)}, bf16[256,1024]{1,0:T(8,128)(2,1)}, u32[]{:S(2)}, u32[]{:S(2)}) collective-permute-start(bf16[256,1024]{1,0:T(8,128)(2,1)} %pad_maximum_fusion.6), channel_id=1, source_target_pairs={{0,1},{1,0},{2,3},{3,2},{4,5},{5,4},{6,7},{7,6},{8,9},{9,8},{10,11... | collective-permute-start | bytes 1572872 | tf_op jit(solution)/shard_map/ppermute | solution.py:378
  284.8 33.1 %collective-permute-start.11 = (bf16[256,1024]{1,0:T(8,128)(2,1)}, bf16[256,1024]{1,0:T(8,128)(2,1)}, u32[]{:S(2)}, u32[]{:S(2)}) collective-permute-start(bf16[256,1024]{1,0:T(8,128)(2,1)} %pad_maximum_fusion.7), channel_id=1, source_target_pairs={{0,2},{1,3},{2,0},{3,1},{4,6},{5,7},{6,4},{7,5},{8,10},{9,11},{10,... | collective-permute-start | bytes 1572872 | tf_op jit(solution)/shard_map/ppermute | solution.py:378
  294.7 34.5 %collective-permute-start.12 = (bf16[256,1024]{1,0:T(8,128)(2,1)}, bf16[256,1024]{1,0:T(8,128)(2,1)}, u32[]{:S(2)}, u32[]{:S(2)}) collective-permute-start(bf16[256,1024]{1,0:T(8,128)(2,1)} %pad_maximum_fusion.8), channel_id=1, source_target_pairs={{0,3},{1,2},{2,1},{3,0},{4,7},{5,6},{6,5},{7,4},{8,11},{9,10},{10,... | collective-permute-start | bytes 1572872 | tf_op jit(solution)/shard_map/ppermute | solution.py:378
  300.3 30.7 %collective-permute-start.13 = (bf16[256,1024]{1,0:T(8,128)(2,1)}, bf16[256,1024]{1,0:T(8,128)(2,1)}, u32[]{:S(2)}, u32[]{:S(2)}) collective-permute-start(bf16[256,1024]{1,0:T(8,128)(2,1)} %pad_maximum_fusion.9), channel_id=1, source_target_pairs={{0,4},{1,5},{2,6},{3,7},{4,0},{5,1},{6,2},{7,3},{8,12},{9,13},{10,... | collective-permute-start | bytes 1572872 | tf_op jit(solution)/shard_map/ppermute | solution.py:378
  302.7 64.6 %collective-permute-start.14 = (bf16[256,1024]{1,0:T(8,128)(2,1)}, bf16[256,1024]{1,0:T(8,128)(2,1)}, u32[]{:S(2)}, u32[]{:S(2)}) collective-permute-start(bf16[256,1024]{1,0:T(8,128)(2,1)} %pad_maximum_fusion.10), channel_id=1, source_target_pairs={{0,5},{1,4},{2,7},{3,6},{4,1},{5,0},{6,3},{7,2},{8,13},{9,12},{10,... | collective-permute-start | bytes 1572872 | tf_op jit(solution)/shard_map/ppermute | solution.py:378
  306.4 73.5 %collective-permute-start.15 = (bf16[256,1024]{1,0:T(8,128)(2,1)}, bf16[256,1024]{1,0:T(8,128)(2,1)S(1)}, u32[]{:S(2)}, u32[]{:S(2)}) collective-permute-start(bf16[256,1024]{1,0:T(8,128)(2,1)} %pad_maximum_fusion.11), channel_id=1, source_target_pairs={{0,6},{1,7},{2,4},{3,5},{4,2},{5,3},{6,0},{7,1},{8,14},{9,15},{10,... | collective-permute-start | bytes 1572872 | tf_op jit(solution)/shard_map/ppermute | solution.py:378
  317.9 73.7 %collective-permute-start.16 = (bf16[256,1024]{1,0:T(8,128)(2,1)}, bf16[256,1024]{1,0:T(8,128)(2,1)S(1)}, u32[]{:S(2)}, u32[]{:S(2)}) collective-permute-start(bf16[256,1024]{1,0:T(8,128)(2,1)} %pad_maximum_fusion.12), channel_id=1, source_target_pairs={{0,7},{1,6},{2,5},{3,4},{4,3},{5,2},{6,1},{7,0},{8,15},{9,14},{10,... | collective-permute-start | bytes 1572872 | tf_op jit(solution)/shard_map/ppermute | solution.py:378
  599.2 49.0 %collective-permute-start.30 = (bf16[256,384]{0,1:T(8,128)(2,1)S(1)}, bf16[256,384]{0,1:T(8,128)(2,1)S(1)}, u32[]{:S(2)}, u32[]{:S(2)}) collective-permute-start(bf16[256,384]{0,1:T(8,128)(2,1)S(1)} %fusion.70), channel_id=1, source_target_pairs={{0,4},{1,5},{2,6},{3,7},{4,0},{5,1},{6,2},{7,3},{8,12},{9,13},{10,... | collective-permute-start | bytes 589832 | tf_op jit(solution)/shard_map/ppermute | solution.py:378
  600.3 48.5 %collective-permute-start.24 = (bf16[256,384]{0,1:T(8,128)(2,1)S(1)}, bf16[256,384]{0,1:T(8,128)(2,1)S(1)}, u32[]{:S(2)}, u32[]{:S(2)}) collective-permute-start(bf16[256,384]{0,1:T(8,128)(2,1)S(1)} %get-tuple-element.160), channel_id=1, source_target_pairs={{0,3},{1,2},{2,1},{3,0},{4,7},{5,6},{6,5},{7,4},{8,11},{9,10},{10,... | collective-permute-start | bytes 589832 | tf_op jit(solution)/shard_map/ppermute | solution.py:378
  601.4 50.4 %collective-permute-start.25 = (bf16[256,384]{0,1:T(8,128)(2,1)S(1)}, bf16[256,384]{0,1:T(8,128)(2,1)S(1)}, u32[]{:S(2)}, u32[]{:S(2)}) collective-permute-start(bf16[256,384]{0,1:T(8,128)(2,1)S(1)} %get-tuple-element.161), channel_id=1, source_target_pairs={{0,7},{1,6},{2,5},{3,4},{4,3},{5,2},{6,1},{7,0},{8,15},{9,14},{10,... | collective-permute-start | bytes 589832 | tf_op jit(solution)/shard_map/ppermute | solution.py:378
  602.7 50.5 %collective-permute-start.26 = (bf16[256,384]{0,1:T(8,128)(2,1)S(1)}, bf16[256,384]{0,1:T(8,128)(2,1)S(1)}, u32[]{:S(2)}, u32[]{:S(2)}) collective-permute-start(bf16[256,384]{0,1:T(8,128)(2,1)S(1)} %get-tuple-element.162), channel_id=1, source_target_pairs={{0,2},{1,3},{2,0},{3,1},{4,6},{5,7},{6,4},{7,5},{8,10},{9,11},{10,... | collective-permute-start | bytes 589832 | tf_op jit(solution)/shard_map/ppermute | solution.py:378
  604.4 50.4 %collective-permute-start.27 = (bf16[256,384]{0,1:T(8,128)(2,1)S(1)}, bf16[256,384]{0,1:T(8,128)(2,1)S(1)}, u32[]{:S(2)}, u32[]{:S(2)}) collective-permute-start(bf16[256,384]{0,1:T(8,128)(2,1)S(1)} %get-tuple-element.163), channel_id=1, source_target_pairs={{0,6},{1,7},{2,4},{3,5},{4,2},{5,3},{6,0},{7,1},{8,14},{9,15},{10,... | collective-permute-start | bytes 589832 | tf_op jit(solution)/shard_map/ppermute | solution.py:378
  648.2 14.1 %collective-permute-start.28 = (bf16[256,384]{0,1:T(8,128)(2,1)S(1)}, bf16[256,384]{0,1:T(8,128)(2,1)S(1)}, u32[]{:S(2)}, u32[]{:S(2)}) collective-permute-start(bf16[256,384]{0,1:T(8,128)(2,1)S(1)} %get-tuple-element.164), channel_id=1, source_target_pairs={{0,1},{1,0},{2,3},{3,2},{4,5},{5,4},{6,7},{7,6},{8,9},{9,8},{10,11... | collective-permute-start | bytes 589832 | tf_op jit(solution)/shard_map/ppermute | solution.py:378
  653.2 28.0 %collective-permute-start.48 = (bf16[256,512]{0,1:T(8,128)(2,1)S(1)}, bf16[256,512]{0,1:T(8,128)(2,1)S(1)}, u32[]{:S(2)}, u32[]{:S(2)}) collective-permute-start(bf16[256,512]{0,1:T(8,128)(2,1)S(1)} %get-tuple-element.115), channel_id=1, source_target_pairs={{0,4},{1,5},{2,6},{3,7},{4,0},{5,1},{6,2},{7,3},{8,12},{9,13},{10,... | collective-permute-start | bytes 786440 | tf_op jit(solution)/shard_map/ppermute | solution.py:378
  654.7 32.0 %collective-permute-start.47 = (bf16[256,512]{0,1:T(8,128)(2,1)S(1)}, bf16[256,512]{0,1:T(8,128)(2,1)S(1)}, u32[]{:S(2)}, u32[]{:S(2)}) collective-permute-start(bf16[256,512]{0,1:T(8,128)(2,1)S(1)} %get-tuple-element.116), channel_id=1, source_target_pairs={{0,5},{1,4},{2,7},{3,6},{4,1},{5,0},{6,3},{7,2},{8,13},{9,12},{10,... | collective-permute-start | bytes 786440 | tf_op jit(solution)/shard_map/ppermute | solution.py:378
  662.3 33.4 %collective-permute-start.46 = (bf16[256,512]{0,1:T(8,128)(2,1)S(1)}, bf16[256,512]{0,1:T(8,128)(2,1)S(1)}, u32[]{:S(2)}, u32[]{:S(2)}) collective-permute-start(bf16[256,512]{0,1:T(8,128)(2,1)S(1)} %get-tuple-element.117), channel_id=1, source_target_pairs={{0,1},{1,0},{2,3},{3,2},{4,5},{5,4},{6,7},{7,6},{8,9},{9,8},{10,11... | collective-permute-start | bytes 786440 | tf_op jit(solution)/shard_map/ppermute | solution.py:378
  662.3 37.4 %collective-permute-start.45 = (bf16[256,512]{0,1:T(8,128)(2,1)S(1)}, bf16[256,512]{0,1:T(8,128)(2,1)S(1)}, u32[]{:S(2)}, u32[]{:S(2)}) collective-permute-start(bf16[256,512]{0,1:T(8,128)(2,1)S(1)} %get-tuple-element.118), channel_id=1, source_target_pairs={{0,6},{1,7},{2,4},{3,5},{4,2},{5,3},{6,0},{7,1},{8,14},{9,15},{10,... | collective-permute-start | bytes 786440 | tf_op jit(solution)/shard_map/ppermute | solution.py:378
  663.9 35.7 %collective-permute-start.44 = (bf16[256,512]{0,1:T(8,128)(2,1)S(1)}, bf16[256,512]{0,1:T(8,128)(2,1)S(1)}, u32[]{:S(2)}, u32[]{:S(2)}) collective-permute-start(bf16[256,512]{0,1:T(8,128)(2,1)S(1)} %get-tuple-element.119), channel_id=1, source_target_pairs={{0,2},{1,3},{2,0},{3,1},{4,6},{5,7},{6,4},{7,5},{8,10},{9,11},{10,... | collective-permute-start | bytes 786440 | tf_op jit(solution)/shard_map/ppermute | solution.py:378
  681.2 30.6 %collective-permute-start.43 = (bf16[256,512]{0,1:T(8,128)(2,1)S(1)}, bf16[256,512]{0,1:T(8,128)(2,1)S(1)}, u32[]{:S(2)}, u32[]{:S(2)}) collective-permute-start(bf16[256,512]{0,1:T(8,128)(2,1)S(1)} %get-tuple-element.120), channel_id=1, source_target_pairs={{0,7},{1,6},{2,5},{3,4},{4,3},{5,2},{6,1},{7,0},{8,15},{9,14},{10,... | collective-permute-start | bytes 786440 | tf_op jit(solution)/shard_map/ppermute | solution.py:378
  686.8 68.5 %collective-permute-start.31 = (bf16[1,4,256,384]{2,3,1,0:T(8,128)(2,1)S(1)}, bf16[1,4,256,384]{2,3,1,0:T(8,128)(2,1)S(1)}, u32[]{:S(2)}, u32[]{:S(2)}) collective-permute-start(bf16[1,4,256,384]{2,3,1,0:T(8,128)(2,1)S(1)} %maximum_bitcast_fusion.5), channel_id=1, source_target_pairs={{0,16},{8,24},{16,0},{24,8},{1,17},{9,25},{17,1},{25,9},{2,18},{10... | collective-permute-start | bytes 2359304 | tf_op jit(solution)/shard_map/ppermute | solution.py:378
  695.7 20.5 %collective-permute-start.33 = (bf16[256,1024]{0,1:T(8,128)(2,1)S(1)}, bf16[256,1024]{0,1:T(8,128)(2,1)S(1)}, u32[]{:S(2)}, u32[]{:S(2)}) collective-permute-start(bf16[256,1024]{0,1:T(8,128)(2,1)S(1)} %get-tuple-element.75), channel_id=1, source_target_pairs={{0,3},{1,2},{2,1},{3,0},{4,7},{5,6},{6,5},{7,4},{8,11},{9,10},{10,... | collective-permute-start | bytes 1572872 | tf_op jit(solution)/shard_map/ppermute | solution.py:378
  699.7 52.9 %collective-permute-start.39 = (bf16[256,1024]{0,1:T(8,128)(2,1)S(1)}, bf16[256,1024]{0,1:T(8,128)(2,1)S(1)}, u32[]{:S(2)}, u32[]{:S(2)}) collective-permute-start(bf16[256,1024]{0,1:T(8,128)(2,1)S(1)} %get-tuple-element.76), channel_id=1, source_target_pairs={{0,4},{1,5},{2,6},{3,7},{4,0},{5,1},{6,2},{7,3},{8,12},{9,13},{10,... | collective-permute-start | bytes 1572872 | tf_op jit(solution)/shard_map/ppermute | solution.py:378
  699.7 64.1 %collective-permute-start.38 = (bf16[256,1024]{0,1:T(8,128)(2,1)S(1)}, bf16[256,1024]{0,1:T(8,128)(2,1)}, u32[]{:S(2)}, u32[]{:S(2)}) collective-permute-start(bf16[256,1024]{0,1:T(8,128)(2,1)S(1)} %get-tuple-element.77), channel_id=1, source_target_pairs={{0,5},{1,4},{2,7},{3,6},{4,1},{5,0},{6,3},{7,2},{8,13},{9,12},{10,... | collective-permute-start | bytes 1572872 | tf_op jit(solution)/shard_map/ppermute | solution.py:378
  711.7 54.5 %collective-permute-start.37 = (bf16[256,1024]{0,1:T(8,128)(2,1)S(1)}, bf16[256,1024]{0,1:T(8,128)(2,1)}, u32[]{:S(2)}, u32[]{:S(2)}) collective-permute-start(bf16[256,1024]{0,1:T(8,128)(2,1)S(1)} %get-tuple-element.78), channel_id=1, source_target_pairs={{0,1},{1,0},{2,3},{3,2},{4,5},{5,4},{6,7},{7,6},{8,9},{9,8},{10,11... | collective-permute-start | bytes 1572872 | tf_op jit(solution)/shard_map/ppermute | solution.py:378
  716.2 114.6 %collective-permute-start.36 = (bf16[256,1024]{0,1:T(8,128)(2,1)}, bf16[256,1024]{0,1:T(8,128)(2,1)}, u32[]{:S(2)}, u32[]{:S(2)}) collective-permute-start(bf16[256,1024]{0,1:T(8,128)(2,1)} %get-tuple-element.79), channel_id=1, source_target_pairs={{0,6},{1,7},{2,4},{3,5},{4,2},{5,3},{6,0},{7,1},{8,14},{9,15},{10,... | collective-permute-start | bytes 1572872 | tf_op jit(solution)/shard_map/ppermute | solution.py:378
  752.5 78.3 %collective-permute-start.35 = (bf16[256,1024]{0,1:T(8,128)(2,1)}, bf16[256,1024]{0,1:T(8,128)(2,1)}, u32[]{:S(2)}, u32[]{:S(2)}) collective-permute-start(bf16[256,1024]{0,1:T(8,128)(2,1)} %get-tuple-element.80), channel_id=1, source_target_pairs={{0,2},{1,3},{2,0},{3,1},{4,6},{5,7},{6,4},{7,5},{8,10},{9,11},{10,... | collective-permute-start | bytes 1572872 | tf_op jit(solution)/shard_map/ppermute | solution.py:378
  755.3 75.5 %collective-permute-start.34 = (bf16[256,1024]{0,1:T(8,128)(2,1)S(1)}, bf16[256,1024]{0,1:T(8,128)(2,1)}, u32[]{:S(2)}, u32[]{:S(2)}) collective-permute-start(bf16[256,1024]{0,1:T(8,128)(2,1)S(1)} %get-tuple-element.81), channel_id=1, source_target_pairs={{0,7},{1,6},{2,5},{3,4},{4,3},{5,2},{6,1},{7,0},{8,15},{9,14},{10,... | collective-permute-start | bytes 1572872 | tf_op jit(solution)/shard_map/ppermute | solution.py:378
  763.8 71.9 %collective-permute-start.49 = (bf16[1,4,256,512]{2,3,1,0:T(8,128)(2,1)}, bf16[1,4,256,512]{2,3,1,0:T(8,128)(2,1)}, u32[]{:S(2)}, u32[]{:S(2)}) collective-permute-start(bf16[1,4,256,512]{2,3,1,0:T(8,128)(2,1)} %maximum_bitcast_fusion.4), channel_id=1, source_target_pairs={{0,16},{8,24},{16,0},{24,8},{1,17},{9,25},{17,1},{25,9},{2,18},{10... | collective-permute-start | bytes 3145736 | tf_op jit(solution)/shard_map/ppermute | solution.py:378
  766.3 76.3 %collective-permute-start.32 = (bf16[2,4,256,384]{2,3,1,0:T(8,128)(2,1)}, bf16[2,4,256,384]{2,3,1,0:T(8,128)(2,1)}, u32[]{:S(2)}, u32[]{:S(2)}) collective-permute-start(bf16[2,4,256,384]{2,3,1,0:T(8,128)(2,1)} %maximum_bitcast_fusion.3), channel_id=1, source_target_pairs={{0,8},{8,0},{16,24},{24,16},{1,9},{9,1},{17,25},{25,17},{2,10},{10... | collective-permute-start | bytes 4718600 | tf_op jit(solution)/shard_map/ppermute | solution.py:378
  835.6 46.5 %collective-permute-start.40 = (bf16[1,4,256,1024]{2,3,1,0:T(8,128)(2,1)}, bf16[1,4,256,1024]{2,3,1,0:T(8,128)(2,1)}, u32[]{:S(2)}, u32[]{:S(2)}) collective-permute-start(bf16[1,4,256,1024]{2,3,1,0:T(8,128)(2,1)} %maximum_bitcast_fusion.1), channel_id=1, source_target_pairs={{0,16},{8,24},{16,0},{24,8},{1,17},{9,25},{17,1},{25,9},{2,18},{10... | collective-permute-start | bytes 6291464 | tf_op jit(solution)/shard_map/ppermute | solution.py:378
  839.6 49.3 %collective-permute-start.50 = (bf16[2,4,256,512]{2,3,1,0:T(8,128)(2,1)}, bf16[2,4,256,512]{2,3,1,0:T(8,128)(2,1)}, u32[]{:S(2)}, u32[]{:S(2)}) collective-permute-start(bf16[2,4,256,512]{2,3,1,0:T(8,128)(2,1)} %maximum_bitcast_fusion.2), channel_id=1, source_target_pairs={{0,8},{8,0},{16,24},{24,16},{1,9},{9,1},{17,25},{25,17},{2,10},{10... | collective-permute-start | bytes 6291464 | tf_op jit(solution)/shard_map/ppermute | solution.py:378
  887.0 26.3 %collective-permute-start.41 = (bf16[2,4,256,1024]{2,3,1,0:T(8,128)(2,1)}, bf16[2,4,256,1024]{2,3,1,0:T(8,128)(2,1)}, u32[]{:S(2)}, u32[]{:S(2)}) collective-permute-start(bf16[2,4,256,1024]{2,3,1,0:T(8,128)(2,1)} %maximum_bitcast_fusion), channel_id=1, source_target_pairs={{0,8},{8,0},{16,24},{24,16},{1,9},{9,1},{17,25},{25,17},{2,10},{10... | collective-permute-start | bytes 12582920 | tf_op jit(solution)/shard_map/ppermute | solution.py:378
  (48 other events, 914.0 us)

commit v2 on v1

--- a/solution.py
+++ b/solution.py
@@ -16,6 +16,7 @@
 MESH = pl.DeviceIdType.MESH
 PIECES = ((0, 48), (48, 48), (96, 32))
 ORDERS = ((1, 2, 3), (2, 3, 1), (3, 1, 2))
+PAIRS = (7, 6, 5, 3, 4, 2, 1, 0)
 
 
 def dot(left, right):
@@ -54,12 +55,14 @@
     def member(self):
         return lax.axis_index("seq") + self.seq * (lax.axis_index("fsdp") % self.share)
 
-    def device(self, mask):
-        low, high = mask % self.seq, mask // self.seq
+    def offset(self, low, high):
         return {
             "seq": jnp.bitwise_xor(lax.axis_index("seq"), low),
             "fsdp": jnp.bitwise_xor(lax.axis_index("fsdp"), high),
         }
+
+    def device(self, mask):
+        return self.offset(mask % self.seq, mask // self.seq)
 
 
 def span_mask(dims):
@@ -281,6 +284,565 @@
     scores = jnp.where(key_ids <= query_ids, scores, -1e30)
     shifted = jnp.exp(scores - jnp.max(scores, axis=1, keepdims=True))
     return shifted / jnp.sum(shifted, axis=1, keepdims=True)
+
+
+def rows_at(start, size):
+    return pl.ds(pl.multiple_of(start, 16), size)
+
+
+def greet_all(layout):
+    pairs = [(1 << bit, 0) for bit in range(layout.seq_bits)]
+    pairs += [(0, mask) for mask in range(1, layout.fsdp)]
+    barrier = pltpu.get_barrier_semaphore()
+    for low, high in pairs:
+        pl.semaphore_signal(
+            barrier, inc=1, device_id=layout.offset(low, high), device_id_type=MESH
+        )
+    pl.semaphore_wait(barrier, len(pairs))
+
+
+def gather_steps(layout, rows, own_ref, dst_ref, sems):
+    send, recv, relay_recv, own_sem = sems
+    me = layout.member()
+    sent, relayed = [], []
+
+    def place(mask, piece):
+        start, size = PIECES[piece]
+        block = jnp.bitwise_xor(me, mask)
+        return dst_ref.at[rows_at(block * rows + start, size)]
+
+    def source(mask, piece):
+        start, size = PIECES[piece]
+        return own_ref.at[pl.ds(start, size)] if mask == 0 else place(mask, piece)
+
+    def push(mask, piece, slot, dim):
+        copy = pltpu.make_async_remote_copy(
+            src_ref=source(mask, piece),
+            dst_ref=place(mask, piece),
+            send_sem=send,
+            recv_sem=recv.at[piece, slot],
+            device_id=layout.device(1 << dim),
+            device_id_type=MESH,
+        )
+        copy.start()
+        sent.append(copy)
+        return copy
+
+    def relay(mask, piece, slot):
+        copy = pltpu.make_async_remote_copy(
+            src_ref=source(mask, piece),
+            dst_ref=place(mask, piece),
+            send_sem=send,
+            recv_sem=relay_recv.at[piece, slot],
+            device_id=layout.device(1),
+            device_id_type=MESH,
+        )
+        copy.start()
+        relayed.append(copy)
+
+    first, second, third = {}, {}, {}
+    for piece, (a, b, c) in enumerate(ORDERS):
+        first[piece] = push(0, piece, 0, a)
+    for piece, (a, b, c) in enumerate(ORDERS):
+        second[piece] = [push(0, piece, 1, b)]
+    for piece, (a, b, c) in enumerate(ORDERS):
+        third[piece] = [push(0, piece, 3, c)]
+    local = pltpu.make_async_copy(own_ref, dst_ref.at[rows_at(me * rows, rows)], own_sem)
+    local.start()
+    for piece in range(len(ORDERS)):
+        relay(0, piece, 0)
+    yield
+    for piece, (a, b, c) in enumerate(ORDERS):
+        first[piece].wait_recv()
+        mask = span_mask((a,))
+        second[piece].append(push(mask, piece, 2, b))
+        third[piece].append(push(mask, piece, 4, c))
+        relay(mask, piece, 1)
+    yield
+    for piece, (a, b, c) in enumerate(ORDERS):
+        second[piece][0].wait_recv()
+        mask = span_mask((b,))
+        third[piece].append(push(mask, piece, 5, c))
+        relay(mask, piece, 2)
+    yield
+    for piece, (a, b, c) in enumerate(ORDERS):
+        second[piece][1].wait_recv()
+        mask = span_mask((a, b))
+        third[piece].append(push(mask, piece, 6, c))
+        relay(mask, piece, 3)
+    yield
+    for turn, dims in enumerate(((2,), (0, 2), (1, 2), (0, 1, 2))):
+        for piece, order in enumerate(ORDERS):
+            third[piece][turn].wait_recv()
+            relay(span_mask([order[d] for d in dims]), piece, 4 + turn)
+    yield
+    for copy in relayed:
+        copy.wait_recv()
+    local.wait()
+    whole = dst_ref.at[pl.ds(0, 15 * rows)]
+    pltpu.make_async_remote_copy(
+        src_ref=whole,
+        dst_ref=whole,
+        send_sem=send,
+        recv_sem=recv.at[0, 0],
+        device_id=layout.device(1),
+        device_id_type=MESH,
+    ).wait_send()
+    yield
+
+
+def gather_sems():
+    count = len(ORDERS)
+    return [
+        pltpu.SemaphoreType.DMA,
+        pltpu.SemaphoreType.DMA((count, 7)),
+        pltpu.SemaphoreType.DMA((count, 8)),
+        pltpu.SemaphoreType.DMA,
+    ]
+
+
+def finish(steps):
+    for _ in steps:
+        pass
+
+
+def scatter_steps(layout, rows, produce, total, buffers, sems):
+    stage, core_in, arrive = buffers
+    core_send, core_recv, send, recv = sems
+    me = layout.member()
+    core = me % 2
+    own = pl.multiple_of(core * rows, 16)
+    other = pl.multiple_of((1 - core) * rows, 16)
+    copies = {}
+
+    def chunked(start, size, body):
+        @pl.loop(0, size // 16)
+        def _(i):
+            body(pl.multiple_of(i * 16 + start, 16))
+
+    def push(piece, pair, dim, slot):
+        start, size = PIECES[piece]
+        copy = pltpu.make_async_remote_copy(
+            src_ref=stage.at[pair, rows_at(own + start, size)],
+            dst_ref=arrive.at[slot, pl.ds(start, size)],
+            send_sem=send.at[piece, slot],
+            recv_sem=recv.at[piece, slot],
+            device_id=layout.device(1 << dim),
+            device_id_type=MESH,
+        )
+        copy.start()
+        return copy
+
+    one, two, three = {}, {}, {}
+
+    def settle(pair):
+        copies[pair].wait_recv()
+
+        def body(r):
+            stage[pair, rows_at(own + r, 16)] = (
+                stage[pair, rows_at(own + r, 16)].astype(jnp.float32)
+                + core_in[pair, rows_at(r, 16)].astype(jnp.float32)
+            ).astype(jnp.bfloat16)
+
+        chunked(0, rows, body)
+        mask = pair * 2
+        for piece, (a, b, c) in enumerate(ORDERS):
+            if mask & (1 << a):
+                slot = (1 if mask & (1 << b) else 0) + (2 if mask & (1 << c) else 0)
+                one[piece, slot] = push(piece, pair, a, slot)
+
+    before = None
+    for pair in PAIRS:
+        produce(jnp.bitwise_xor(me // 2, pair), stage.at[pair])
+        copies[pair] = pltpu.make_async_remote_copy(
+            src_ref=stage.at[pair, rows_at(other, rows)],
+            dst_ref=core_in.at[pair],
+            send_sem=core_send.at[pair],
+            recv_sem=core_recv.at[pair],
+            device_id=layout.device(1),
+            device_id_type=MESH,
+        )
+        copies[pair].start()
+        if before is not None:
+            settle(before)
+        before = pair
+    settle(before)
+    yield
+
+    def keep(piece, pair, slots):
+        start, size = PIECES[piece]
+
+        def body(r):
+            value = stage[pair, rows_at(own + r, 16)].astype(jnp.float32)
+            for slot in slots:
+                value = value + arrive[slot, rows_at(r, 16)].astype(jnp.float32)
+            stage[pair, rows_at(own + r, 16)] = value.astype(jnp.bfloat16)
+
+        chunked(start, size, body)
+
+    for piece, (a, b, c) in enumerate(ORDERS):
+        for slot, dims in ((3, (b, c)), (1, (b,))):
+            pair = span_mask(dims) // 2
+            one[piece, slot].wait_recv()
+            keep(piece, pair, (slot,))
+            two[piece, slot] = push(piece, pair, b, 4 + slot // 2)
+    yield
+    for piece, (a, b, c) in enumerate(ORDERS):
+        pair = span_mask((c,)) // 2
+        one[piece, 2].wait_recv()
+        two[piece, 3].wait_recv()
+        keep(piece, pair, (2, 5))
+        three[piece] = push(piece, pair, c, 6)
+    yield
+    for piece, (a, b, c) in enumerate(ORDERS):
+        start, size = PIECES[piece]
+        one[piece, 0].wait_recv()
+        two[piece, 1].wait_recv()
+        three[piece].wait_recv()
+
+        def body(r):
+            value = stage[0, rows_at(own + r, 16)].astype(jnp.float32)
+            for slot in (0, 4, 6):
+                value = value + arrive[slot, rows_at(r, 16)].astype(jnp.float32)
+            total[rows_at(r, 16)] = value
+
+        chunked(start, size, body)
+    for group in (copies, one, two, three):
+        for copy in group.values():
+            copy.wait_send()
+    yield
+
+
+def scatter_scratch(rows, width):
+    return [
+        pltpu.VMEM((8, 2 * rows, width), jnp.bfloat16),
+        pltpu.VMEM((8, rows, width), jnp.bfloat16),
+        pltpu.VMEM((7, rows, width), jnp.bfloat16),
+    ]
+
+
+def scatter_sems():
+    count = len(ORDERS)
+    return [
+        pltpu.SemaphoreType.DMA((8,)),
+        pltpu.SemaphoreType.DMA((8,)),
+        pltpu.SemaphoreType.DMA((count, 7)),
+        pltpu.SemaphoreType.DMA((count, 7)),
+    ]
+
+
+def loop_rows(count, size, body):
+    @pl.loop(0, count // size)
+    def _(i):
+        body(pl.ds(pl.multiple_of(i * size, size), size))
+
+
+class Sizes:
+    def __init__(self, layout, tokens, block_ids, w_query, w_gate):
+        self.rows, self.width = tokens.shape[1], tokens.shape[2]
+        self.length = block_ids.shape[1]
+        self.depth = w_query.shape[0]
+        self.hidden = w_gate.shape[1] // GROUP
+        self.heads = H // GROUP
+        self.query = self.heads * HD
+        self.attn = 2 * self.query + 2 * HD
+        self.all_rows = GROUP * self.rows
+        self.span = min(512, self.length)
+        self.kv_share = GROUP // KVH
+
+
+def kv_half(layout, target, chunk):
+    second = (target // (GROUP // KVH)) % 2 == 1
+    return jnp.where(second, chunk[:, HD:], chunk[:, :HD])
+
+
+def attention_scores(sizes, qkv, ids, seq, start, head):
+    base = sizes.query
+    keys_rows = rows_at(seq * sizes.length, sizes.length)
+    query_rows = rows_at(seq * sizes.length + start, sizes.span)
+    query = qkv[query_rows, head * HD : (head + 1) * HD]
+    keys = qkv[keys_rows, base : base + HD]
+    values = qkv[keys_rows, base + HD : base + 2 * HD]
+    key_ids = ids[seq, 0:1, :]
+    query_ids = jnp.transpose(ids[seq, :, pl.ds(start, sizes.span)])[:, :1]
+    return query, keys, values, softmax(query, keys, query_ids, key_ids)
+
+
+def front_kernel(
+    layout,
+    sizes,
+    tok_ref,
+    cot_ref,
+    ids_ref,
+    gains_ref,
+    wq_ref,
+    wk_ref,
+    wv_ref,
+    wo_ref,
+    wg_ref,
+    wu_ref,
+    wd_ref,
+    h1_out,
+    h2_out,
+    g_out,
+    in_out,
+    down_out,
+    wa,
+    qkv,
+    attended,
+    middle,
+    gains,
+    ids,
+    x_all,
+    tok,
+    h2,
+    wq,
+    wk,
+    wv,
+    wo,
+    pack,
+    stage,
+    core_in,
+    arrive,
+    x_send,
+    x_recv,
+    x_relay,
+    x_own,
+    h_send,
+    h_recv,
+    h_relay,
+    h_own,
+    g_send,
+    g_recv,
+    g_relay,
+    g_own,
+    core_send,
+    core_recv,
+    s_send,
+    s_recv,
+    attn_send,
+    attn_recv,
+    gain_send,
+    gain_recv,
+    id_send,
+    id_recv,
+    mlp_send,
+    mlp_recv,
+    load_sem,
+):
+    share, fsdp, depth = layout.share, layout.fsdp, sizes.depth
+    seq_me, fsdp_me = lax.axis_index("seq"), lax.axis_index("fsdp")
+    query = sizes.query
+    rows, hidden = sizes.rows, sizes.hidden
+
+    loads = []
+
+    def load(src, dst):
+        copy = pltpu.make_async_copy(src, dst, load_sem.at[len(loads)])
+        copy.start()
+        loads.append(copy)
+        return copy
+
+    def columns(ref, start, size):
+        return ref.at[:, pl.ds(pl.multiple_of(start, 128), size)]
+
+    load(tok_ref, tok)
+    load(columns(wq_ref, seq_me * share * query, share * query), wq)
+    load(columns(wo_ref, seq_me * share * query, share * query), wo)
+    chunk = seq_me * share // (2 * sizes.kv_share) * 128
+    load(columns(wk_ref, chunk, 128), wk)
+    load(columns(wv_ref, chunk, 128), wv)
+    own_rows = pl.ds(pl.multiple_of(fsdp_me * depth, 128), depth)
+    load(gains_ref, gains.at[:, own_rows])
+    load(ids_ref, ids.at[fsdp_me % share])
+    greet_all(layout)
+    x_steps = gather_steps(layout, rows, tok_ref, x_all, (x_send, x_recv, x_relay, x_own))
+    next(x_steps)
+    small = []
+    for mask in range(1, fsdp):
+        copy = pltpu.make_async_remote_copy(
+            src_ref=gains_ref,
+            dst_ref=gains.at[:, own_rows],
+            send_sem=gain_send.at[mask],
+            recv_sem=gain_recv.at[mask],
+            device_id=layout.offset(0, mask),
+            device_id_type=MESH,
+        )
+        copy.start()
+        small.append(copy)
+    for mask in range(1, share):
+        copy = pltpu.make_async_remote_copy(
+            src_ref=ids_ref,
+            dst_ref=ids.at[fsdp_me % share],
+            send_sem=id_send.at[mask],
+            recv_sem=id_recv.at[mask],
+            device_id=layout.offset(0, mask),
+            device_id_type=MESH,
+        )
+        copy.start()
+        small.append(copy)
+    for copy in loads:
+        copy.wait()
+    for j in range(share):
+        target = seq_me * share + j
+        pack[j] = jnp.concatenate(
+            [
+                wq[:, j * query : (j + 1) * query],
+                kv_half(layout, target, wk[...]),
+                kv_half(layout, target, wv[...]),
+                wo[:, j * query : (j + 1) * query],
+            ],
+            axis=1,
+        )
+    attn = []
+    for mask in reversed(range(1, fsdp)):
+        copy = pltpu.make_async_remote_copy(
+            src_ref=pack.at[jnp.bitwise_xor(fsdp_me, mask) % share],
+            dst_ref=wa.at[own_rows],
+            send_sem=attn_send.at[mask],
+            recv_sem=attn_recv.at[mask],
+            device_id=layout.offset(0, mask),
+            device_id_type=MESH,
+        )
+        copy.start()
+        attn.append(copy)
+    wa[own_rows] = pack[fsdp_me % share]
+    finish(x_steps)
+    for copy in small:
+        copy.wait()
+
+    gain_one = gains[0:1].astype(jnp.float32)
+
+    def norm(r):
+        values = x_all[r].astype(jnp.float32)
+        x_all[r] = (values * rms_factor(values) * gain_one).astype(jnp.bfloat16)
+
+    loop_rows(sizes.all_rows, 64, norm)
+    h1_copy = pltpu.make_async_copy(x_all, h1_out, load_sem.at[0])
+    h1_copy.start()
+    for copy in attn:
+        copy.wait()
+
+    mlp = []
+
+    def send_mlp(ref, out, place, index):
+        def at(j):
+            return columns(ref, (seq_me * share + j) * hidden, hidden)
+
+        home = out.at[own_rows, pl.ds(place, hidden)]
+        for mask in reversed(range(1, fsdp)):
+            copy = pltpu.make_async_remote_copy(
+                src_ref=at(jnp.bitwise_xor(fsdp_me, mask) % share),
+                dst_ref=home,
+                send_sem=mlp_send.at[index, mask],
+                recv_sem=mlp_recv.at[index, mask],
+                device_id=layout.offset(0, mask),
+                device_id_type=MESH,
+            )
+            copy.start()
+            mlp.append(copy)
+        copy = pltpu.make_async_copy(at(fsdp_me % share), home, load_sem.at[1 + index])
+        copy.start()
+        mlp.append(copy)
+
+    send_mlp(wg_ref, in_out, 0, 0)
+    send_mlp(wu_ref, in_out, hidden, 1)
+    send_mlp(wd_ref, down_out, 0, 2)
+
+    def project(r):
+        qkv[r] = dot(x_all[r], wa[:, : query + 2 * HD]).astype(jnp.bfloat16)
+
+    loop_rows(sizes.all_rows, 256, project)
+
+    blocks = sizes.length // sizes.span
+
+    @pl.loop(0, share * blocks)
+    def _(i):
+        seq = i // blocks
+        start = pl.multiple_of((i % blocks) * sizes.span, sizes.span)
+        outs = []
+        for head in range(sizes.heads):
+            _, _, values, probs = attention_scores(sizes, qkv, ids, seq, start, head)
+            outs.append(dot(probs.astype(jnp.bfloat16), values))
+        attended[rows_at(seq * sizes.length + start, sizes.span)] = jnp.concatenate(
+            outs, axis=1
+        ).astype(jnp.bfloat16)
+
+    def out_rows(pair, ref):
+        block = attended[rows_at(pair * 2 * rows, 2 * rows)]
+
+        @pl.loop(0, sizes.width // 512)
+        def _(i):
+            piece = pl.ds(pl.multiple_of(i * 512, 512), 512)
+            ref[:, piece] = dot_cols(block, wa[piece, query + 2 * HD :]).astype(jnp.bfloat16)
+
+    finish(
+        scatter_steps(
+            layout, rows, out_rows, middle, (stage, core_in, arrive),
+            (core_send, core_recv, s_send, s_recv),
+        )
+    )
+    gain_two = gains[8:9].astype(jnp.float32)
+
+    def second(r):
+        values = tok[r].astype(jnp.float32) + RESIDUAL * middle[r]
+        middle[r] = values
+        h2[r] = (values * rms_factor(values) * gain_two).astype(jnp.bfloat16)
+
+    loop_rows(rows, 32, second)
+    h_steps = gather_steps(layout, rows, h2, h2_out, (h_send, h_recv, h_relay, h_own))
+    finish(h_steps)
+    g_steps = gather_steps(layout, rows, cot_ref, g_out, (g_send, g_recv, g_relay, g_own))
+    finish(g_steps)
+    for copy in mlp:
+        copy.wait()
+    h1_copy.wait()
+
+
+def front(layout, sizes, *args):
+    width, count = sizes.width, sizes.all_rows
+    hbm, vmem = pl.BlockSpec(memory_space=pl.ANY), pl.BlockSpec(memory_space=pltpu.VMEM)
+    share, depth, fsdp = layout.share, sizes.depth, layout.fsdp
+    bf16 = jnp.bfloat16
+    shapes = [
+        ((count, width), bf16, hbm),
+        ((count, width), bf16, hbm),
+        ((count, width), bf16, hbm),
+        ((width, 2 * sizes.hidden), bf16, hbm),
+        ((width, sizes.hidden), bf16, hbm),
+        ((width, sizes.attn), bf16, vmem),
+        ((count, sizes.query + 2 * HD), bf16, vmem),
+        ((count, sizes.query), bf16, vmem),
+        ((sizes.rows, width), jnp.float32, vmem),
+        ((16, width), bf16, vmem),
+        ((share, 8, sizes.length), jnp.int32, vmem),
+    ]
+    dma = pltpu.SemaphoreType.DMA
+    return pl.pallas_call(
+        functools.partial(front_kernel, layout, sizes),
+        out_shape=[jax.ShapeDtypeStruct(shape, dtype) for shape, dtype, _ in shapes],
+        in_specs=[hbm] * len(args),
+        out_specs=[spec for _, _, spec in shapes],
+        scratch_shapes=[
+            pltpu.VMEM((count, width), bf16),
+            pltpu.VMEM((sizes.rows, width), bf16),
+            pltpu.VMEM((sizes.rows, width), bf16),
+            pltpu.VMEM((depth, share * sizes.query), bf16),
+            pltpu.VMEM((depth, 128), bf16),
+            pltpu.VMEM((depth, 128), bf16),
+            pltpu.VMEM((depth, share * sizes.query), bf16),
+            pltpu.VMEM((share, depth, sizes.attn), bf16),
+        ]
+        + scatter_scratch(sizes.rows, width)
+        + gather_sems() * 3
+        + scatter_sems()
+        + [dma((fsdp,)), dma((fsdp,)), dma((fsdp,)), dma((fsdp,))]
+        + [dma((share,)), dma((share,)), dma((3, fsdp)), dma((3, fsdp)), dma((8,))],
+        compiler_params=pltpu.CompilerParams(
+            collective_id=3, has_side_effects=True, vmem_limit_bytes=56 * 1024 * 1024
+        ),
+        name="front",
+    )(*args)
 
 
 def attend_kernel(heads, q_ref, kv_ref, row_ref, col_ref, o_ref):
@@ -416,81 +978,49 @@
     heads = H // GROUP
     query_cols = heads * HD
     kv_share = GROUP // KVH
-    column_group = seq_me * share + fsdp_me % share
-
-    def attn_part(target):
-        kv = (target // kv_share) * HD
-        return jnp.concatenate(
-            [
-                slices(w_query, target * query_cols, query_cols),
-                slices(w_key, kv, HD),
-                slices(w_value, kv, HD),
-                slices(w_out, target * query_cols, query_cols),
-                jnp.broadcast_to(gain_attn[:, None], (depth, 64)),
-                jnp.broadcast_to(gain_mlp[:, None], (depth, 64)),
-            ],
-            axis=1,
-        )
-
-    def in_part(target):
-        start = target * hidden_cols
-        return jnp.concatenate(
-            [slices(w_gate, start, hidden_cols), slices(w_up, start, hidden_cols)], axis=1
-        )
-
-    def down_part(target):
-        return slices(w_down, target * hidden_cols, hidden_cols)
-
-    def collect(part, after=None):
-        whole = None
-        for mask in range(fsdp):
-            target = seq_me * share + jnp.bitwise_xor(fsdp_me, mask) % share
-            piece = part(target)
-            if mask:
-                if after is not None:
-                    piece, _ = lax.optimization_barrier((piece, after))
-                piece = swap(piece, "fsdp", fsdp, mask)
-            if whole is None:
-                whole = jnp.zeros((fsdp * piece.shape[0], piece.shape[1]), piece.dtype)
-            whole = lax.dynamic_update_slice_in_dim(
-                whole, piece, jnp.bitwise_xor(fsdp_me, mask) * depth, axis=0
-            )
-        return whole
-
-    attn_all = collect(attn_part)
-    x_all = token_gather(layout, tokens[0])
-    in_all = collect(in_part, attn_all)
-    down_all = collect(down_part, attn_all)
+    sizes = Sizes(layout, tokens, block_ids, w_query, w_gate)
+    gains_own = jnp.concatenate(
+        [jnp.broadcast_to(gain[None], (8, depth)) for gain in (gain_attn, gain_mlp)], axis=0
+    )
+    ids_own = jnp.broadcast_to(block_ids, (8, block_ids.shape[1]))
+    (
+        normed_one,
+        normed_two,
+        grad_all,
+        in_all,
+        down_all,
+        attn_all,
+        qkv,
+        attended,
+        middle,
+        gains_all,
+        ids_all,
+    ) = front(
+        layout,
+        sizes,
+        tokens[0],
+        cotangent[0],
+        ids_own,
+        gains_own,
+        w_query,
+        w_key,
+        w_value,
+        w_out,
+        w_gate,
+        w_up,
+        w_down,
+    )
     w_in = attn_all[:, : query_cols + 2 * HD]
-    w_back = attn_all[:, query_cols + 2 * HD : 2 * query_cols + 2 * HD]
-    attn_gain = attn_all[:, 2 * query_cols + 2 * HD].astype(jnp.float32)[None]
-    mlp_gain = attn_all[:, 2 * query_cols + 2 * HD + 64].astype(jnp.float32)[None]
-
-    id_rows = [block_ids]
-    for bit in range(share.bit_length() - 1):
-        id_rows = id_rows + [swap(r, "fsdp", fsdp, 1 << bit) for r in id_rows]
-    ids = jnp.zeros((share, block_ids.shape[1]), block_ids.dtype)
-    for mask, row in enumerate(id_rows):
-        ids = lax.dynamic_update_slice_in_dim(
-            ids, row, jnp.bitwise_xor(fsdp_me % share, mask), axis=0
-        )
-
-    inputs_all = x_all.astype(jnp.float32)
-    normed_one = (inputs_all * rms_factor(inputs_all) * attn_gain).astype(jnp.bfloat16)
-    qkv = dot(normed_one, w_in).astype(jnp.bfloat16)
-    attended = attend(qkv, ids, heads)
-    branch = token_scatter(layout, dot_cols(attended, w_back).astype(jnp.bfloat16))
+    w_back = attn_all[:, query_cols + 2 * HD :]
+    attn_gain = gains_all[0:1].astype(jnp.float32)
+    mlp_gain = gains_all[8:9].astype(jnp.float32)
+    ids = ids_all[:, 0]
     inputs = tokens[0].astype(jnp.float32)
-    middle = inputs + RESIDUAL * branch
     factor_two = rms_factor(middle)
-    normed_two = token_gather(
-        layout, (middle * factor_two * mlp_gain).astype(jnp.bfloat16)
-    )
     gate_up = dot(normed_two, in_all)
     gate, upward = gate_up[:, :hidden_cols], gate_up[:, hidden_cols:]
     sigma = jax.nn.sigmoid(gate)
     hidden = (gate * sigma * upward).astype(jnp.bfloat16)
-    grad_all = token_gather(layout, cotangent[0])
     grad_down_in = (RESIDUAL * grad_all.astype(jnp.float32)).astype(jnp.bfloat16)
     grad_hidden = dot(grad_down_in, down_all)
     grad_upward = (grad_hidden * gate * sigma).astype(jnp.bfloat16)

time: 960 us -> 861 us (0.90)
  waiting for transfers between devices: 204 us -> 93.2 us
  Pallas kernels: 332 us -> 436 us
  local copies, waits for them, and re-layouts: 104 us -> 51.5 us
  starting transfers between devices: 78.1 us -> 47.7 us
    pallas_call x1, Pallas kernels: 9.07 us -> 278 us  [front(): pl.pallas_call(functools.partial(front_kernel, layout, sizes), out_shape=...]
    pallas_call x4 -> x1, Pallas kernels: 157 us -> 34.1 us  [token_gather(): pl.pallas_call(functools.partial(gather_kernel, layout, rows), out_shape=...]
    ppermute x51 -> x27, waiting for transfers between devices: 204 us -> 93.2 us  [swap(): return lax.ppermute(array, axis, [(i, i ^ mask) for i in range(size)])]
    pallas_call x4 -> x3, Pallas kernels: 155 us -> 113 us  [token_scatter(): pl.pallas_call(functools.partial(scatter_kernel, layout, rows), out_shape...]
    ppermute x51 -> x27, starting transfers between devices: 78.1 us -> 47.7 us  [swap(): return lax.ppermute(array, axis, [(i, i ^ mask) for i in range(size)])]
    dynamic_update_slice x27 -> x0, local copies, waits for them, and re-layouts: 20.8 us -> none  [the longest x23 19.9 us: collect(): lax.dynamic_update_slice_in_dim(whole, piece, jnp.bitwise_xor(fsdp_me, ma...]
    ppermute x14 -> x0, local copies, waits for them, and re-layouts: 17.3 us -> none  [swap(): return lax.ppermute(array, axis, [(i, i ^ mask) for i in range(size)])]
    dynamic_slice x5 -> x0, local copies, waits for them, and re-layouts: 10.1 us -> none  [slices(): return lax.dynamic_slice_in_dim(array, start, size, axis=1)]
  transfers between devices with their start and end apart: 51 -> 27, of which waited for: 20 -> 9; matrix products, arithmetic and copies ran while one was open for 15% -> 11% of each run, Pallas kernels for 22% -> 4%
where the time goes in v2:
time: 861 us; the launch traced here: 851 us
  Pallas kernels  436 us (51%)
  waiting for transfers between devices  93.2 us (11%)
  matrix products  91.3 us (11%)
  other arithmetic  65.4 us (8%)
  blocking collectives  63.6 us (7%)
  local copies, waits for them, and re-layouts  51.5 us (6%)
  starting transfers between devices  47.7 us (6%)
    pallas_call x1, Pallas kernels, front(): pl.pallas_call(functools.partial(front_kernel, layout, sizes), out_shape=...  278 us
    pallas_call x3, Pallas kernels, token_scatter(): pl.pallas_call(functools.partial(scatter_kernel, layout, rows), out_shape...  113 us
    ppermute x27, waiting for transfers between devices, swap(): return lax.ppermute(array, axis, [(i, i ^ mask) for i in range(size)])  93.2 us
    psum x1, blocking collectives, body(): gains = lax.psum(gains, ('seq', 'fsdp'))  63.6 us
    ppermute x27, starting transfers between devices, swap(): return lax.ppermute(array, axis, [(i, i ^ mask) for i in range(size)])  47.7 us
    dot_general x4, matrix products, dot_rows(): lax.dot_general(left, right, (((0,), (0,)), ((), ())), preferred_element_...  34.3 us
    pallas_call x1, Pallas kernels, token_gather(): pl.pallas_call(functools.partial(gather_kernel, layout, rows), out_shape=...  34.1 us
    dot_general x3, matrix products, dot(): return jnp.dot(left, right, preferred_element_type=jnp.float32)  30.4 us
  transfers between devices with their start and end apart: 27, of which 9 were waited for; matrix products, arithmetic and copies ran while one was open for 11% of the time, Pallas kernels for 4%

profile of v2, /device:TPU:15, one launch (start us, length us, event | category | flops | bytes accessed | tf_op | source)
XLA Modules:
  0.0 851.0 jit_solution(3009498485688678542)
XLA Ops:
  3.9 278.0 %front.1 = (bf16[2048,2048]{1,0:T(8,128)(2,1)}, bf16[2048,2048]{1,0:T(8,128)(2,1)}, bf16[2048,2048]{1,0:T(8,128)(2,1)}, bf16[2048,1024]{1,0:T(8,128)(2,1)}, bf16...) custom-call(bf16[128,2048]{1,0:T(8,128)(2,1)} %bitcast.506, ...), custom_call_target="tpu_custom_call" | custom-call | tf_op jit(solution)/shard_map/front/pallas_call | solution.py:821
  285.3 14.8 %fusion.76 = f32[2048,1024]{0,1:T(8,128)} fusion(bf16[2048,2048]{1,0:T(8,128)(2,1)} %get-tuple-element.23, bf16[2048,1024]{1,0:T(8,128)(2,1)} %get-tuple-element.24), kind=kOutput, calls=%fused_computation.322 | convolution fusion | flops 8589934592 | bytes 20971520 | tf_op jit(solution)/shard_map/dot_general | solution.py:23
  300.1 11.3 %multiply_convert_fusion.4 = (bf16[2048,512]{0,1:T(8,128)(2,1)}, bf16[2048,512]{0,1:T(8,128)(2,1)}, bf16[2048,512]{0,1:T(8,128)(2,1)}) fusion(f32[2048,1024]{0,1:T(8,128)} %fusion.76, bf16[2048,512]{1,0:T(8,128)(2,1)} %get-tuple-element.25, bf16[2048,2048]{1,0:T(8,128)(2,1)S(1)} %bitcast.518), kind=kOutput, calls=%fused_computation.13 | convolution fusion | flops 4324327424 | bytes 25165824 | tf_op jit(solution)/shard_map/dot_general | solution.py:23
  311.4 13.5 %convolution_convert_fusion.1.p_ref = bf16[2048,2048]{1,0:T(8,128)(2,1)} fusion(bf16[2048,1024]{1,0:T(8,128)(2,1)S(1)} %copy-done.33, bf16[2048,512]{0,1:T(8,128)(2,1)} %get-tuple-element.55, bf16[2048,512]{0,1:T(8,128)(2,1)} %get-tuple-element.54), kind=kOutput, calls=%fused_computation.3 | convolution fusion | flops 8602517504 | bytes 16777216 | tf_op jit(solution)/shard_map/dot_general | solution.py:27
  325.0 37.2 %token_scatter.4 = f32[128,2048]{1,0:T(8,128)S(1)} custom-call(bf16[2048,2048]{1,0:T(8,128)(2,1)} %convolution_convert_fusion.1.p_ref), custom_call_target="tpu_custom_call" | custom-call | tf_op jit(solution)/shard_map/token_scatter/pallas_call | solution.py:261
  362.6 7.2 convolution_convert_fusion.2.p_ref
  369.8 38.3 %token_scatter.3 = f32[128,2048]{1,0:T(8,128)S(1)} custom-call(bf16[2048,2048]{1,0:T(8,128)(2,1)} %convolution_convert_fusion.2.p_ref), custom_call_target="tpu_custom_call" | custom-call | tf_op jit(solution)/shard_map/token_scatter/pallas_call | solution.py:261
  409.9 34.1 %token_gather.1 = bf16[2048,2048]{1,0:T(8,128)(2,1)} custom-call(bf16[128,2048]{1,0:T(8,128)(2,1)} %get-tuple-element.52.x_ref), custom_call_target="tpu_custom_call" | custom-call | tf_op jit(solution)/shard_map/token_gather/pallas_call | solution.py:162
  444.0 5.6 convolution_convert_fusion.5
  449.8 4.3 convolution_convert_fusion.6.g_ref
  455.2 10.8 %attend_back.1 = bf16[2048,256]{1,0:T(8,128)(2,1)S(1)} custom-call(bf16[2048,256]{1,0:T(8,128)(2,1)S(1)} %copy-done, bf16[2048,256]{1,0:T(8,128)(2,1)S(1)} %copy-done, s32[4,1,512]{2,1,0:T(1,128)S(1)} %get-tuple-element.190.row_ref, s32[4,512,1]{2,1,0:T(8,128)S(1)} %broadcast_in_dim_squeeze.4.col_ref, bf16[2048,128]{1,0:T(8,128)(2,1)S(1)} %copy-done.1), custom_call_target="tpu_custom_call" | custom-call | tf_op jit(solution)/shard_map/attend_back/pallas_call | solution.py:926
  466.1 5.8 convolution_convert_fusion.4
  472.6 2.3 collective-permute-start.6
  480.8 10.0 %fusion.2 = bf16[2048,512]{0,1:T(8,128)(2,1)} fusion(bf16[2048,512]{0,1:T(8,128)(2,1)} %get-tuple-element.62, bf16[2048,2048]{1,0:T(8,128)(2,1)} %get-tuple-element.26), kind=kOutput, calls=%fused_computation.26 | convolution fusion | flops 4308598784 | bytes 12582912 | tf_op jit(solution)/shard_map/dot_general | solution.py:33
  490.8 12.9 %convolution_convert_fusion.3 = bf16[2048,1024]{0,1:T(8,128)(2,1)} fusion(bf16[2048,2048]{1,0:T(8,128)(2,1)} %get-tuple-element.23, bf16[2048,512]{0,1:T(8,128)(2,1)S(1)} %copy-done.38, bf16[2048,512]{0,1:T(8,128)(2,1)S(1)} %copy-done.37), kind=kOutput, calls=%fused_computation.24 | convolution fusion | flops 8600420352 | bytes 16777216 | tf_op jit(solution)/shard_map/dot_general | solution.py:33
  503.7 5.8 convolution_convert_fusion.p_ref
  509.5 37.9 %token_scatter.5 = f32[128,2048]{1,0:T(8,128)S(1)} custom-call(bf16[2048,2048]{1,0:T(8,128)(2,1)} %convolution_convert_fusion.p_ref), custom_call_target="tpu_custom_call" | custom-call | tf_op jit(solution)/shard_map/token_scatter/pallas_call | solution.py:261
  550.5 2.5 constant_dynamic-slice_fusion.7
  554.3 2.4 collective-permute-start.24
  557.4 6.5 collective-permute-done.4
  565.7 2.4 collective-permute-start.20
  568.2 11.0 %collective-permute-done.24 = bf16[256,512]{0,1:T(8,128)(2,1)S(1)} collective-permute-done((bf16[256,512]{0,1:T(8,128)(2,1)S(1)}, bf16[256,512]{0,1:T(8,128)(2,1)S(1)}, u32[]{:S(2)}, u32[]{:S(2)}) %collective-permute-start.24) | collective-permute-done | bytes 262176 | tf_op jit(solution)/shard_map/ppermute | solution.py:940
  579.2 3.8 collective-permute-start.19
  583.1 2.5 collective-permute-done.23
  585.6 6.6 collective-permute-start.7
  594.1 5.3 collective-permute-start.9
  599.7 3.3 collective-permute-start.14
  603.0 7.8 collective-permute-done.19
  616.0 34.9 %collective-permute-done.15 = bf16[256,1024]{0,1:T(8,128)(2,1)S(1)} collective-permute-done((bf16[256,1024]{0,1:T(8,128)(2,1)}, bf16[256,1024]{0,1:T(8,128)(2,1)S(1)}, u32[]{:S(2)}, u32[]{:S(2)}) %collective-permute-start.15) | collective-permute-done | bytes 524320 | tf_op jit(solution)/shard_map/ppermute | solution.py:940
  650.9 4.2 collective-permute-start.11
  659.1 3.1 collective-permute-done.14
  665.7 63.6 %psum.7 = f32[2,2048]{1,0:T(2,128)S(1)} all-reduce(f32[2,2048]{1,0:T(2,128)S(1)} %pad_maximum_fusion.6), channel_id=1, replica_groups=mesh['seq'=4,'fsdp'=8] {'seq','fsdp'}, use_global_device_ids=true, to_apply=%region_6.7 | all-reduce | flops 4096 | bytes 32768 | tf_op jit(solution)/shard_map/psum | solution.py:1077
  729.9 2.8 select_bitcast_fusion.15
  738.9 2.6 collective-permute-start.26
  745.1 3.4 copy.26
  755.2 25.3 %collective-permute-done.16 = bf16[1,4,256,1024]{2,3,1,0:T(8,128)(2,1)} collective-permute-done((bf16[1,4,256,1024]{2,3,1,0:T(8,128)(2,1)}, bf16[1,4,256,1024]{2,3,1,0:T(8,128)(2,1)}, u32[]{:S(2)}, u32[]{:S(2)}) %collective-permute-start.16) | collective-permute-done | bytes 2097184 | tf_op jit(solution)/shard_map/ppermute | solution.py:940
  780.6 2.0 select_bitcast_fusion.5
  782.6 2.4 maximum_bitcast_fusion
  785.5 2.5 collective-permute-start.17
  789.8 2.4 pad_maximum_fusion.2
  792.2 7.3 copy.28
  808.0 4.4 convert_element_type.390
  812.4 5.2 select_bitcast_fusion.1
  817.6 7.6 pad_maximum_fusion
  825.2 11.4 %copy.27 = bf16[2,2,4,256,1024]{4,3,2,1,0:T(8,128)(2,1)} copy(bf16[2,2,4,256,1024]{3,4,2,0,1:T(8,128)(2,1)} %pad_maximum_fusion) | data formatting | bytes 16777216 | tf_op jit(solution)/shard_map/stack | solution.py:949
  836.5 3.9 slice_bitcast_fusion
  841.7 4.4 convert_element_type.376
  846.1 4.4 convert_element_type.375
  (212 shorter events, 67.3 us)
Async XLA Ops:
  285.0 15.1 %slice-start = ((s8[8388608]{0:T(1024)(128)(4,1)}), s8[4194304]{0:T(1024)(128)(4,1)S(1)}, s32[]{:S(2)}) async-start(s8[8388608]{0:T(1024)(128)(4,1)} %bitcast.517), calls=%async_computation | async-start | bytes 8388608
  285.3 14.8 %slice-start.1 = ((s8[8388608]{0:T(1024)(128)(4,1)}), s8[4194304]{0:T(1024)(128)(4,1)S(1)}, s32[]{:S(2)}) async-start(s8[8388608]{0:T(1024)(128)(4,1)} %bitcast.517), calls=%async_computation.1 | async-start | bytes 8388608
  300.1 11.3 %copy-start.33 = (bf16[2048,1024]{1,0:T(8,128)(2,1)S(1)}, bf16[2048,1024]{1,0:T(8,128)(2,1)}, u32[]{:S(2)}) copy-start(bf16[2048,1024]{1,0:T(8,128)(2,1)} %get-tuple-element.24) | copy-start | bytes 12582916
  325.0 37.3 %copy-start.9 = (f32[128,2048]{1,0:T(8,128)S(1)}, f32[128,2048]{1,0:T(8,128)}, u32[]{:S(2)}) copy-start(f32[128,2048]{1,0:T(8,128)} %get-tuple-element.22) | copy-start | bytes 3145732
  325.0 37.6 %copy-start.34 = (bf16[2048,512]{1,0:T(8,128)(2,1)S(1)}, bf16[2048,512]{1,0:T(8,128)(2,1)}, u32[]{:S(2)}) copy-start(bf16[2048,512]{1,0:T(8,128)(2,1)} %get-tuple-element.25) | copy-start | bytes 6291460
  325.0 37.6 %copy-start.36 = (bf16[2048,512]{0,1:T(8,128)(2,1)S(1)}, bf16[2048,512]{0,1:T(8,128)(2,1)}, u32[]{:S(2)}) copy-start(bf16[2048,512]{0,1:T(8,128)(2,1)} %get-tuple-element.62) | copy-start | bytes 6291460
  369.8 38.3 %copy-start.21 = (bf16[1,128,2048]{2,1,0:T(8,128)(2,1)S(1)}, bf16[1,128,2048]{2,1,0:T(8,128)(2,1)}, u32[]{:S(2)}) copy-start(bf16[1,128,2048]{2,1,0:T(8,128)(2,1)} %param.23) | copy-start | bytes 1572868
  409.9 34.1 %copy-start.35 = (bf16[2048,128]{1,0:T(8,128)(2,1)S(1)}, bf16[2048,128]{1,0:T(8,128)(2,1)}, u32[]{:S(2)}) copy-start(bf16[2048,128]{1,0:T(8,128)(2,1)} %get-tuple-element.32) | copy-start | bytes 1572868
  472.6 75.6 %collective-permute-start.6 = (bf16[256,384]{0,1:T(8,128)(2,1)}, bf16[256,384]{0,1:T(8,128)(2,1)S(1)}, u32[]{:S(2)}, u32[]{:S(2)}) collective-permute-start(bf16[256,384]{0,1:T(8,128)(2,1)} %fusion.63), channel_id=1, source_target_pairs={{0,4},{1,5},{2,6},{3,7},{4,0},{5,1},{6,2},{7,3},{8,12},{9,13},{10,... | collective-permute-start | bytes 589832 | tf_op jit(solution)/shard_map/ppermute | solution.py:940
  475.8 73.0 %collective-permute-start = (bf16[256,384]{0,1:T(8,128)(2,1)S(1)}, bf16[256,384]{0,1:T(8,128)(2,1)S(1)}, u32[]{:S(2)}, u32[]{:S(2)}) collective-permute-start(bf16[256,384]{0,1:T(8,128)(2,1)S(1)} %get-tuple-element.126), channel_id=1, source_target_pairs={{0,3},{1,2},{2,1},{3,0},{4,7},{5,6},{6,5},{7,4},{8,11},{9,10},{10,... | collective-permute-start | bytes 589832 | tf_op jit(solution)/shard_map/ppermute | solution.py:940
  477.0 76.0 %collective-permute-start.1 = (bf16[256,384]{0,1:T(8,128)(2,1)}, bf16[256,384]{0,1:T(8,128)(2,1)}, u32[]{:S(2)}, u32[]{:S(2)}) collective-permute-start(bf16[256,384]{0,1:T(8,128)(2,1)} %get-tuple-element.127), channel_id=1, source_target_pairs={{0,7},{1,6},{2,5},{3,4},{4,3},{5,2},{6,1},{7,0},{8,15},{9,14},{10,... | collective-permute-start | bytes 589832 | tf_op jit(solution)/shard_map/ppermute | solution.py:940
  477.1 77.2 %collective-permute-start.2 = (bf16[256,384]{0,1:T(8,128)(2,1)}, bf16[256,384]{0,1:T(8,128)(2,1)}, u32[]{:S(2)}, u32[]{:S(2)}) collective-permute-start(bf16[256,384]{0,1:T(8,128)(2,1)} %get-tuple-element.128), channel_id=1, source_target_pairs={{0,2},{1,3},{2,0},{3,1},{4,6},{5,7},{6,4},{7,5},{8,10},{9,11},{10,... | collective-permute-start | bytes 589832 | tf_op jit(solution)/shard_map/ppermute | solution.py:940
  478.8 77.9 %collective-permute-start.3 = (bf16[256,384]{0,1:T(8,128)(2,1)}, bf16[256,384]{0,1:T(8,128)(2,1)}, u32[]{:S(2)}, u32[]{:S(2)}) collective-permute-start(bf16[256,384]{0,1:T(8,128)(2,1)} %get-tuple-element.129), channel_id=1, source_target_pairs={{0,6},{1,7},{2,4},{3,5},{4,2},{5,3},{6,0},{7,1},{8,14},{9,15},{10,... | collective-permute-start | bytes 589832 | tf_op jit(solution)/shard_map/ppermute | solution.py:940
  480.7 10.0 %copy-start.37 = (bf16[2048,512]{0,1:T(8,128)(2,1)S(1)}, bf16[2048,512]{0,1:T(8,128)(2,1)}, u32[]{:S(2)}) copy-start(bf16[2048,512]{0,1:T(8,128)(2,1)} %get-tuple-element.54) | copy-start | bytes 6291460
  480.8 10.0 %copy-start.38 = (bf16[2048,512]{0,1:T(8,128)(2,1)S(1)}, bf16[2048,512]{0,1:T(8,128)(2,1)}, u32[]{:S(2)}) copy-start(bf16[2048,512]{0,1:T(8,128)(2,1)} %get-tuple-element.55) | copy-start | bytes 6291460
  490.8 12.9 %copy-start.23 = (bf16[2048,384]{1,0:T(8,128)(2,1)S(1)}, bf16[2048,384]{1,0:T(8,128)(2,1)}, u32[]{:S(2)}) copy-start(bf16[2048,384]{1,0:T(8,128)(2,1)} %get-tuple-element.30) | copy-start | bytes 4718596
  509.5 39.8 %copy-start.20 = (f32[128,2048]{1,0:T(8,128)S(1)}, f32[128,2048]{1,0:T(8,128)}, u32[]{:S(2)}) copy-start(f32[128,2048]{1,0:T(8,128)} %get-tuple-element.53) | copy-start | bytes 3145732
  548.2 15.7 %collective-permute-start.4 = (bf16[256,384]{0,1:T(8,128)(2,1)}, bf16[256,384]{0,1:T(8,128)(2,1)S(1)}, u32[]{:S(2)}, u32[]{:S(2)}) collective-permute-start(bf16[256,384]{0,1:T(8,128)(2,1)} %get-tuple-element.130), channel_id=1, source_target_pairs={{0,1},{1,0},{2,3},{3,2},{4,5},{5,4},{6,7},{7,6},{8,9},{9,8},{10,11... | collective-permute-start | bytes 589832 | tf_op jit(solution)/shard_map/ppermute | solution.py:940
  548.8 15.4 %copy-start.31 = (bf16[256,384]{0,1:T(8,128)(2,1)}, bf16[256,384]{0,1:T(8,128)(2,1)S(1)}, u32[]{:S(2)}) copy-start(bf16[256,384]{0,1:T(8,128)(2,1)S(1)} %collective-permute-done) | copy-start | bytes 589828
  548.8 15.4 %collective-permute-start.5 = (bf16[256,384]{0,1:T(8,128)(2,1)}, bf16[256,384]{0,1:T(8,128)(2,1)S(1)}, u32[]{:S(2)}, u32[]{:S(2)}) collective-permute-start(bf16[256,384]{0,1:T(8,128)(2,1)} %get-tuple-element.131), channel_id=1, source_target_pairs={{0,5},{1,4},{2,7},{3,6},{4,1},{5,0},{6,3},{7,2},{8,13},{9,12},{10,... | collective-permute-start | bytes 589832 | tf_op jit(solution)/shard_map/ppermute | solution.py:940
  553.0 39.2 %copy-start.19 = (bf16[2048,1024]{0,1:T(8,128)(2,1)S(1)}, bf16[2048,1024]{0,1:T(8,128)(2,1)}, u32[]{:S(2)}) copy-start(bf16[2048,1024]{0,1:T(8,128)(2,1)} %convolution_convert_fusion.3) | copy-start | bytes 12582916
  553.0 12.8 %collective-permute-start.18 = (bf16[256,512]{0,1:T(8,128)(2,1)S(1)}, bf16[256,512]{0,1:T(8,128)(2,1)S(1)}, u32[]{:S(2)}, u32[]{:S(2)}) collective-permute-start(bf16[256,512]{0,1:T(8,128)(2,1)S(1)} %get-tuple-element.82), channel_id=1, source_target_pairs={{0,3},{1,2},{2,1},{3,0},{4,7},{5,6},{6,5},{7,4},{8,11},{9,10},{10,... | collective-permute-start | bytes 786440 | tf_op jit(solution)/shard_map/ppermute | solution.py:940
  554.3 24.9 %collective-permute-start.24 = (bf16[256,512]{0,1:T(8,128)(2,1)S(1)}, bf16[256,512]{0,1:T(8,128)(2,1)S(1)}, u32[]{:S(2)}, u32[]{:S(2)}) collective-permute-start(bf16[256,512]{0,1:T(8,128)(2,1)S(1)} %get-tuple-element.83), channel_id=1, source_target_pairs={{0,4},{1,5},{2,6},{3,7},{4,0},{5,1},{6,2},{7,3},{8,12},{9,13},{10,... | collective-permute-start | bytes 786440 | tf_op jit(solution)/shard_map/ppermute | solution.py:940
  556.7 28.9 %collective-permute-start.23 = (bf16[256,512]{0,1:T(8,128)(2,1)S(1)}, bf16[256,512]{0,1:T(8,128)(2,1)}, u32[]{:S(2)}, u32[]{:S(2)}) collective-permute-start(bf16[256,512]{0,1:T(8,128)(2,1)S(1)} %get-tuple-element.84), channel_id=1, source_target_pairs={{0,5},{1,4},{2,7},{3,6},{4,1},{5,0},{6,3},{7,2},{8,13},{9,12},{10,... | collective-permute-start | bytes 786440 | tf_op jit(solution)/shard_map/ppermute | solution.py:940
  563.9 30.2 %collective-permute-start.22 = (bf16[256,512]{0,1:T(8,128)(2,1)}, bf16[256,512]{0,1:T(8,128)(2,1)}, u32[]{:S(2)}, u32[]{:S(2)}) collective-permute-start(bf16[256,512]{0,1:T(8,128)(2,1)} %get-tuple-element.85), channel_id=1, source_target_pairs={{0,1},{1,0},{2,3},{3,2},{4,5},{5,4},{6,7},{7,6},{8,9},{9,8},{10,11... | collective-permute-start | bytes 786440 | tf_op jit(solution)/shard_map/ppermute | solution.py:940
  564.2 35.6 %collective-permute-start.21 = (bf16[256,512]{0,1:T(8,128)(2,1)}, bf16[256,512]{0,1:T(8,128)(2,1)}, u32[]{:S(2)}, u32[]{:S(2)}) collective-permute-start(bf16[256,512]{0,1:T(8,128)(2,1)} %get-tuple-element.86), channel_id=1, source_target_pairs={{0,6},{1,7},{2,4},{3,5},{4,2},{5,3},{6,0},{7,1},{8,14},{9,15},{10,... | collective-permute-start | bytes 786440 | tf_op jit(solution)/shard_map/ppermute | solution.py:940
  565.7 17.4 %copy-start.26 = (bf16[256,512]{0,1:T(8,128)(2,1)}, bf16[256,512]{0,1:T(8,128)(2,1)S(1)}, u32[]{:S(2)}) copy-start(bf16[256,512]{0,1:T(8,128)(2,1)S(1)} %collective-permute-done.18) | copy-start | bytes 786436
  565.7 34.0 %collective-permute-start.20 = (bf16[256,512]{0,1:T(8,128)(2,1)}, bf16[256,512]{0,1:T(8,128)(2,1)S(1)}, u32[]{:S(2)}, u32[]{:S(2)}) collective-permute-start(bf16[256,512]{0,1:T(8,128)(2,1)} %get-tuple-element.87), channel_id=1, source_target_pairs={{0,2},{1,3},{2,0},{3,1},{4,6},{5,7},{6,4},{7,5},{8,10},{9,11},{10,... | collective-permute-start | bytes 786440 | tf_op jit(solution)/shard_map/ppermute | solution.py:940
  579.2 31.7 %collective-permute-start.19 = (bf16[256,512]{0,1:T(8,128)(2,1)}, bf16[256,512]{0,1:T(8,128)(2,1)S(1)}, u32[]{:S(2)}, u32[]{:S(2)}) collective-permute-start(bf16[256,512]{0,1:T(8,128)(2,1)} %get-tuple-element.88), channel_id=1, source_target_pairs={{0,7},{1,6},{2,5},{3,4},{4,3},{5,2},{6,1},{7,0},{8,15},{9,14},{10,... | collective-permute-start | bytes 786440 | tf_op jit(solution)/shard_map/ppermute | solution.py:940
  585.6 26.0 %copy-start.27 = (bf16[256,512]{0,1:T(8,128)(2,1)S(1)}, bf16[256,512]{0,1:T(8,128)(2,1)}, u32[]{:S(2)}) copy-start(bf16[256,512]{0,1:T(8,128)(2,1)} %copy-done.26) | copy-start | bytes 786436
  585.6 69.5 %collective-permute-start.7 = (bf16[1,4,256,384]{2,3,1,0:T(8,128)(2,1)S(1)}, bf16[1,4,256,384]{2,3,1,0:T(8,128)(2,1)S(1)}, u32[]{:S(2)}, u32[]{:S(2)}) collective-permute-start(bf16[1,4,256,384]{2,3,1,0:T(8,128)(2,1)S(1)} %maximum_bitcast_fusion.5), channel_id=1, source_target_pairs={{0,16},{8,24},{16,0},{24,8},{1,17},{9,25},{17,1},{25,9},{2,18},{10... | collective-permute-start | bytes 2359304 | tf_op jit(solution)/shard_map/ppermute | solution.py:940
  592.2 19.4 %copy-start.29 = (bf16[256,512]{0,1:T(8,128)(2,1)S(1)}, bf16[256,512]{0,1:T(8,128)(2,1)}, u32[]{:S(2)}) copy-start(bf16[256,512]{0,1:T(8,128)(2,1)} %copy-done.28) | copy-start | bytes 786436
  594.1 21.9 %collective-permute-start.9 = (bf16[256,1024]{0,1:T(8,128)(2,1)}, bf16[256,1024]{0,1:T(8,128)(2,1)S(1)}, u32[]{:S(2)}, u32[]{:S(2)}) collective-permute-start(bf16[256,1024]{0,1:T(8,128)(2,1)} %get-tuple-element.67), channel_id=1, source_target_pairs={{0,3},{1,2},{2,1},{3,0},{4,7},{5,6},{6,5},{7,4},{8,11},{9,10},{10,... | collective-permute-start | bytes 1572872 | tf_op jit(solution)/shard_map/ppermute | solution.py:940
  599.7 51.2 %collective-permute-start.15 = (bf16[256,1024]{0,1:T(8,128)(2,1)}, bf16[256,1024]{0,1:T(8,128)(2,1)S(1)}, u32[]{:S(2)}, u32[]{:S(2)}) collective-permute-start(bf16[256,1024]{0,1:T(8,128)(2,1)} %get-tuple-element.68), channel_id=1, source_target_pairs={{0,4},{1,5},{2,6},{3,7},{4,0},{5,1},{6,2},{7,3},{8,12},{9,13},{10,... | collective-permute-start | bytes 1572872 | tf_op jit(solution)/shard_map/ppermute | solution.py:940
  599.7 62.4 %collective-permute-start.14 = (bf16[256,1024]{0,1:T(8,128)(2,1)}, bf16[256,1024]{0,1:T(8,128)(2,1)}, u32[]{:S(2)}, u32[]{:S(2)}) collective-permute-start(bf16[256,1024]{0,1:T(8,128)(2,1)} %get-tuple-element.69), channel_id=1, source_target_pairs={{0,5},{1,4},{2,7},{3,6},{4,1},{5,0},{6,3},{7,2},{8,13},{9,12},{10,... | collective-permute-start | bytes 1572872 | tf_op jit(solution)/shard_map/ppermute | solution.py:940
  611.6 52.2 %collective-permute-start.13 = (bf16[256,1024]{0,1:T(8,128)(2,1)}, bf16[256,1024]{0,1:T(8,128)(2,1)}, u32[]{:S(2)}, u32[]{:S(2)}) collective-permute-start(bf16[256,1024]{0,1:T(8,128)(2,1)} %get-tuple-element.70), channel_id=1, source_target_pairs={{0,1},{1,0},{2,3},{3,2},{4,5},{5,4},{6,7},{7,6},{8,9},{9,8},{10,11... | collective-permute-start | bytes 1572872 | tf_op jit(solution)/shard_map/ppermute | solution.py:940
  613.3 52.4 %copy-start.32 = (f32[2048]{0:T(1024)S(1)}, f32[2048]{0:T(1024)}, u32[]{:S(2)}) copy-start(f32[2048]{0:T(1024)} %get-tuple-element.35) | copy-start | bytes 24580
  616.0 41.8 %copy-start.24 = (bf16[256,1024]{0,1:T(8,128)(2,1)}, bf16[256,1024]{0,1:T(8,128)(2,1)S(1)}, u32[]{:S(2)}) copy-start(bf16[256,1024]{0,1:T(8,128)(2,1)S(1)} %collective-permute-done.9) | copy-start | bytes 1572868
  616.0 113.9 %collective-permute-start.12 = (bf16[256,1024]{0,1:T(8,128)(2,1)}, bf16[256,1024]{0,1:T(8,128)(2,1)}, u32[]{:S(2)}, u32[]{:S(2)}) collective-permute-start(bf16[256,1024]{0,1:T(8,128)(2,1)} %get-tuple-element.71), channel_id=1, source_target_pairs={{0,6},{1,7},{2,4},{3,5},{4,2},{5,3},{6,0},{7,1},{8,14},{9,15},{10,... | collective-permute-start | bytes 1572872 | tf_op jit(solution)/shard_map/ppermute | solution.py:940
  650.9 79.0 %collective-permute-start.11 = (bf16[256,1024]{0,1:T(8,128)(2,1)}, bf16[256,1024]{0,1:T(8,128)(2,1)}, u32[]{:S(2)}, u32[]{:S(2)}) collective-permute-start(bf16[256,1024]{0,1:T(8,128)(2,1)} %get-tuple-element.72), channel_id=1, source_target_pairs={{0,2},{1,3},{2,0},{3,1},{4,6},{5,7},{6,4},{7,5},{8,10},{9,11},{10,... | collective-permute-start | bytes 1572872 | tf_op jit(solution)/shard_map/ppermute | solution.py:940
  656.0 73.9 %collective-permute-start.10 = (bf16[256,1024]{0,1:T(8,128)(2,1)}, bf16[256,1024]{0,1:T(8,128)(2,1)}, u32[]{:S(2)}, u32[]{:S(2)}) collective-permute-start(bf16[256,1024]{0,1:T(8,128)(2,1)} %get-tuple-element.73), channel_id=1, source_target_pairs={{0,7},{1,6},{2,5},{3,4},{4,3},{5,2},{6,1},{7,0},{8,15},{9,14},{10,... | collective-permute-start | bytes 1572872 | tf_op jit(solution)/shard_map/ppermute | solution.py:940
  662.2 72.9 %collective-permute-start.25 = (bf16[1,4,256,512]{2,3,1,0:T(8,128)(2,1)}, bf16[1,4,256,512]{2,3,1,0:T(8,128)(2,1)}, u32[]{:S(2)}, u32[]{:S(2)}) collective-permute-start(bf16[1,4,256,512]{2,3,1,0:T(8,128)(2,1)} %maximum_bitcast_fusion.4), channel_id=1, source_target_pairs={{0,16},{8,24},{16,0},{24,8},{1,17},{9,25},{17,1},{25,9},{2,18},{10... | collective-permute-start | bytes 3145736 | tf_op jit(solution)/shard_map/ppermute | solution.py:940
  663.7 77.8 %collective-permute-start.8 = (bf16[2,4,256,384]{2,3,1,0:T(8,128)(2,1)}, bf16[2,4,256,384]{2,3,1,0:T(8,128)(2,1)}, u32[]{:S(2)}, u32[]{:S(2)}) collective-permute-start(bf16[2,4,256,384]{2,3,1,0:T(8,128)(2,1)} %maximum_bitcast_fusion.3), channel_id=1, source_target_pairs={{0,8},{8,0},{16,24},{24,16},{1,9},{9,1},{17,25},{25,17},{2,10},{10... | collective-permute-start | bytes 4718600 | tf_op jit(solution)/shard_map/ppermute | solution.py:940
  734.7 45.9 %collective-permute-start.16 = (bf16[1,4,256,1024]{2,3,1,0:T(8,128)(2,1)}, bf16[1,4,256,1024]{2,3,1,0:T(8,128)(2,1)}, u32[]{:S(2)}, u32[]{:S(2)}) collective-permute-start(bf16[1,4,256,1024]{2,3,1,0:T(8,128)(2,1)} %maximum_bitcast_fusion.1), channel_id=1, source_target_pairs={{0,16},{8,24},{16,0},{24,8},{1,17},{9,25},{17,1},{25,9},{2,18},{10... | collective-permute-start | bytes 6291464 | tf_op jit(solution)/shard_map/ppermute | solution.py:940
  738.9 49.0 %collective-permute-start.26 = (bf16[2,4,256,512]{2,3,1,0:T(8,128)(2,1)}, bf16[2,4,256,512]{2,3,1,0:T(8,128)(2,1)}, u32[]{:S(2)}, u32[]{:S(2)}) collective-permute-start(bf16[2,4,256,512]{2,3,1,0:T(8,128)(2,1)} %maximum_bitcast_fusion.2), channel_id=1, source_target_pairs={{0,8},{8,0},{16,24},{24,16},{1,9},{9,1},{17,25},{25,17},{2,10},{10... | collective-permute-start | bytes 6291464 | tf_op jit(solution)/shard_map/ppermute | solution.py:940
  752.8 27.8 %copy-start.14 = (bf16[1,256,1024]{1,2,0:T(8,128)(2,1)S(1)}, bf16[1,256,1024]{1,2,0:T(8,128)(2,1)}, u32[]{:S(2)}) copy-start(bf16[1,256,1024]{1,2,0:T(8,128)(2,1)} %copy-done.13) | copy-start | bytes 1572868
  752.8 27.8 %copy-start.16 = (bf16[1,256,1024]{1,2,0:T(8,128)(2,1)S(1)}, bf16[1,256,1024]{1,2,0:T(8,128)(2,1)}, u32[]{:S(2)}) copy-start(bf16[1,256,1024]{1,2,0:T(8,128)(2,1)} %copy-done.15) | copy-start | bytes 1572868
  785.5 26.9 %collective-permute-start.17 = (bf16[2,4,256,1024]{2,3,1,0:T(8,128)(2,1)}, bf16[2,4,256,1024]{2,3,1,0:T(8,128)(2,1)}, u32[]{:S(2)}, u32[]{:S(2)}) collective-permute-start(bf16[2,4,256,1024]{2,3,1,0:T(8,128)(2,1)} %maximum_bitcast_fusion), channel_id=1, source_target_pairs={{0,8},{8,0},{16,24},{24,16},{1,9},{9,1},{17,25},{25,17},{2,10},{10... | collective-permute-start | bytes 12582920 | tf_op jit(solution)/shard_map/ppermute | solution.py:940
  (20 other events, 80.4 us)

commit v3 on v2

--- a/solution.py
+++ b/solution.py
@@ -67,216 +67,6 @@
 
 def span_mask(dims):
     return sum(1 << d for d in dims)
-
-
-def greet(layout):
-    barrier = pltpu.get_barrier_semaphore()
-    for bit in range(4):
-        pl.semaphore_signal(
-            barrier, inc=1, device_id=layout.device(1 << bit), device_id_type=MESH
-        )
-    pl.semaphore_wait(barrier, 4)
-
-
-def gather_kernel(layout, rows, x_ref, o_ref, send, recv, core_send, core_recv, own_sem):
-    greet(layout)
-    me = layout.member()
-
-    def place(mask, piece):
-        start, size = PIECES[piece]
-        block = jnp.bitwise_xor(me, mask)
-        return o_ref.at[pl.ds(pl.multiple_of(block * rows + start, 16), size)]
-
-    def own(piece):
-        start, size = PIECES[piece]
-        return x_ref.at[pl.ds(start, size)]
-
-    sent, relayed = [], []
-
-    def push(mask, piece, slot, dim):
-        copy = pltpu.make_async_remote_copy(
-            src_ref=own(piece) if mask == 0 else place(mask, piece),
-            dst_ref=place(mask, piece),
-            send_sem=send.at[piece, slot],
-            recv_sem=recv.at[piece, slot],
-            device_id=layout.device(1 << dim),
-            device_id_type=MESH,
-        )
-        copy.start()
-        sent.append(copy)
-        return copy
-
-    def relay(mask, piece, slot):
-        copy = pltpu.make_async_remote_copy(
-            src_ref=own(piece) if mask == 0 else place(mask, piece),
-            dst_ref=place(mask, piece),
-            send_sem=core_send.at[piece, slot],
-            recv_sem=core_recv.at[piece, slot],
-            device_id=layout.device(1),
-            device_id_type=MESH,
-        )
-        copy.start()
-        sent.append(copy)
-        relayed.append(copy)
-
-    first, second, third = {}, {}, {}
-    for piece, (a, b, c) in enumerate(ORDERS):
-        first[piece] = push(0, piece, 0, a)
-    for piece, (a, b, c) in enumerate(ORDERS):
-        second[piece] = [push(0, piece, 1, b)]
-    for piece, (a, b, c) in enumerate(ORDERS):
-        third[piece] = [push(0, piece, 3, c)]
-    local = pltpu.make_async_copy(x_ref, o_ref.at[pl.ds(pl.multiple_of(me * rows, 16), rows)], own_sem)
-    local.start()
-    for piece in range(3):
-        relay(0, piece, 0)
-    for piece, (a, b, c) in enumerate(ORDERS):
-        first[piece].wait_recv()
-        mask = span_mask((a,))
-        second[piece].append(push(mask, piece, 2, b))
-        third[piece].append(push(mask, piece, 4, c))
-        relay(mask, piece, 1)
-    for piece, (a, b, c) in enumerate(ORDERS):
-        second[piece][0].wait_recv()
-        mask = span_mask((b,))
-        third[piece].append(push(mask, piece, 5, c))
-        relay(mask, piece, 2)
-    for piece, (a, b, c) in enumerate(ORDERS):
-        second[piece][1].wait_recv()
-        mask = span_mask((a, b))
-        third[piece].append(push(mask, piece, 6, c))
-        relay(mask, piece, 3)
-    for turn, dims in enumerate(((2,), (0, 2), (1, 2), (0, 1, 2))):
-        for piece, order in enumerate(ORDERS):
-            third[piece][turn].wait_recv()
-            relay(span_mask([order[d] for d in dims]), piece, 4 + turn)
-    for copy in sent:
-        copy.wait_send()
-    for copy in relayed:
-        copy.wait_recv()
-    local.wait()
-
-
-def token_gather(layout, block):
-    rows, width = block.shape
-    return pl.pallas_call(
-        functools.partial(gather_kernel, layout, rows),
-        out_shape=jax.ShapeDtypeStruct((GROUP * rows, width), block.dtype),
-        in_specs=[pl.BlockSpec(memory_space=pl.ANY)],
-        out_specs=pl.BlockSpec(memory_space=pl.ANY),
-        scratch_shapes=[
-            pltpu.SemaphoreType.DMA((3, 7)),
-            pltpu.SemaphoreType.DMA((3, 7)),
-            pltpu.SemaphoreType.DMA((3, 8)),
-            pltpu.SemaphoreType.DMA((3, 8)),
-            pltpu.SemaphoreType.DMA,
-        ],
-        compiler_params=pltpu.CompilerParams(collective_id=1, has_side_effects=True),
-        name="token_gather",
-    )(block)
-
-
-def scatter_kernel(
-    layout, rows, p_ref, o_ref, core_in, acc, arrive, core_send, core_recv, send, recv
-):
-    greet(layout)
-    me = layout.member()
-    masks = (14, 12, 10, 6, 8, 4, 2, 0)
-
-    def rows_of(mask):
-        return pl.ds(pl.multiple_of(jnp.bitwise_xor(me, mask) * rows, 16), rows)
-
-    core = []
-    for mask in masks:
-        copy = pltpu.make_async_remote_copy(
-            src_ref=p_ref.at[rows_of(mask ^ 1)],
-            dst_ref=core_in.at[mask // 2],
-            send_sem=core_send.at[mask // 2],
-            recv_sem=core_recv.at[mask // 2],
-            device_id=layout.device(1),
-            device_id_type=MESH,
-        )
-        copy.start()
-        core.append(copy)
-
-    def push(piece, mask, dim, slot):
-        start, size = PIECES[piece]
-        copy = pltpu.make_async_remote_copy(
-            src_ref=acc.at[mask // 2, pl.ds(start, size)],
-            dst_ref=arrive.at[slot, pl.ds(start, size)],
-            send_sem=send.at[piece, slot],
-            recv_sem=recv.at[piece, slot],
-            device_id=layout.device(1 << dim),
-            device_id_type=MESH,
-        )
-        copy.start()
-        return copy
-
-    one, two, three = {}, {}, {}
-    for mask, copy in zip(masks, core):
-        copy.wait_recv()
-        acc[mask // 2] = (
-            p_ref[rows_of(mask)].astype(jnp.float32) + core_in[mask // 2].astype(jnp.float32)
-        ).astype(jnp.bfloat16)
-        for piece, (a, b, c) in enumerate(ORDERS):
-            if mask & (1 << a):
-                rest = mask ^ (1 << a)
-                slot = (1 if rest & (1 << b) else 0) + (2 if rest & (1 << c) else 0)
-                one[piece, slot] = push(piece, mask, a, slot)
-
-    def add(piece, slot, mask):
-        start, size = PIECES[piece]
-        own = acc[mask // 2, pl.ds(start, size)].astype(jnp.float32)
-        return own + arrive[slot, pl.ds(start, size)].astype(jnp.float32)
-
-    def keep(piece, slot, mask):
-        start, size = PIECES[piece]
-        acc[mask // 2, pl.ds(start, size)] = add(piece, slot, mask).astype(jnp.bfloat16)
-
-    for piece, (a, b, c) in enumerate(ORDERS):
-        for slot, mask in ((3, span_mask((b, c))), (1, span_mask((b,)))):
-            one[piece, slot].wait_recv()
-            keep(piece, slot, mask)
-            two[piece, slot] = push(piece, mask, b, 4 + slot // 2)
-    for piece, (a, b, c) in enumerate(ORDERS):
-        mask = span_mask((c,))
-        one[piece, 2].wait_recv()
-        keep(piece, 2, mask)
-        two[piece, 3].wait_recv()
-        keep(piece, 5, mask)
-        three[piece] = push(piece, mask, c, 6)
-    for piece, (a, b, c) in enumerate(ORDERS):
-        start, size = PIECES[piece]
-        one[piece, 0].wait_recv()
-        two[piece, 1].wait_recv()
-        partial = add(piece, 0, 0) + arrive[4, pl.ds(start, size)].astype(jnp.float32)
-        three[piece].wait_recv()
-        o_ref[pl.ds(start, size)] = partial + arrive[6, pl.ds(start, size)].astype(jnp.float32)
-    for copy in core + list(one.values()) + list(two.values()) + list(three.values()):
-        copy.wait_send()
-
-
-def token_scatter(layout, partial):
-    rows, width = partial.shape[0] // GROUP, partial.shape[1]
-    return pl.pallas_call(
-        functools.partial(scatter_kernel, layout, rows),
-        out_shape=jax.ShapeDtypeStruct((rows, width), jnp.float32),
-        in_specs=[pl.BlockSpec(memory_space=pltpu.VMEM)],
-        out_specs=pl.BlockSpec(memory_space=pltpu.VMEM),
-        scratch_shapes=[
-            pltpu.VMEM((8, rows, width), jnp.bfloat16),
-            pltpu.VMEM((8, rows, width), jnp.bfloat16),
-            pltpu.VMEM((7, rows, width), jnp.bfloat16),
-            pltpu.SemaphoreType.DMA((8,)),
-            pltpu.SemaphoreType.DMA((8,)),
-            pltpu.SemaphoreType.DMA((3, 7)),
-            pltpu.SemaphoreType.DMA((3, 7)),
-        ],
-        compiler_params=pltpu.CompilerParams(
-            collective_id=2, has_side_effects=True, vmem_limit_bytes=48 * 1024 * 1024
-        ),
-        name="token_scatter",
-    )(partial)
 
 
 def softmax(query, keys, query_ids, key_ids):
@@ -547,7 +337,7 @@
         self.query = self.heads * HD
         self.attn = 2 * self.query + 2 * HD
         self.all_rows = GROUP * self.rows
-        self.span = min(512, self.length)
+        self.span = max(128, min(self.length, 512 * 512 // self.length))
         self.kv_share = GROUP // KVH
 
 
@@ -845,114 +635,500 @@
     )(*args)
 
 
-def attend_kernel(heads, q_ref, kv_ref, row_ref, col_ref, o_ref):
-    base = heads * HD
-    keys = kv_ref[:, base : base + HD]
-    values = kv_ref[:, base + HD : base + 2 * HD]
-    outs = []
-    for head in range(heads):
-        query = q_ref[:, head * HD : (head + 1) * HD]
-        probs = softmax(query, keys, col_ref[0], row_ref[0])
-        outs.append(dot(probs.astype(jnp.bfloat16), values))
-    o_ref[...] = jnp.concatenate(outs, axis=1).astype(jnp.bfloat16)
-
-
-def attend_back_kernel(heads, q_ref, kv_ref, row_ref, col_ref, g_ref, o_ref, grad_kv):
-    step = pl.program_id(1)
-    span, length = q_ref.shape[0], kv_ref.shape[0]
-    base = heads * HD
-    keys = kv_ref[:, base : base + HD]
-    values = kv_ref[:, base + HD : base + 2 * HD]
-    grads, grad_keys, grad_values = [], 0.0, 0.0
-    for head in range(heads):
-        query = q_ref[:, head * HD : (head + 1) * HD]
-        grad = g_ref[:, head * HD : (head + 1) * HD]
-        probs = softmax(query, keys, col_ref[0], row_ref[0])
-        grad_probs = dot_cols(grad, values)
-        centre = jnp.sum(probs * grad_probs, axis=1, keepdims=True)
-        grad_scores = (probs * (grad_probs - centre)).astype(jnp.bfloat16)
-        grads.append(dot(grad_scores, keys) * (1.0 / HD))
-        grad_keys = grad_keys + dot_rows(grad_scores, query) * (1.0 / HD)
-        grad_values = grad_values + dot_rows(probs.astype(jnp.bfloat16), grad)
-    both = jnp.concatenate([grad_keys, grad_values], axis=1)
-
-    @pl.when(step == 0)
-    def _():
-        grad_kv[...] = both
-
-    @pl.when(step > 0)
-    def _():
-        grad_kv[...] += both
-
-    start = pl.multiple_of(step * span, span)
-    o_ref[pl.ds(start, span), :base] = jnp.concatenate(grads, axis=1).astype(jnp.bfloat16)
-
-    @pl.when(step == pl.num_programs(1) - 1)
-    def _():
-        o_ref[:, base:] = grad_kv[...].astype(jnp.bfloat16)
-
-
-def attention_specs(qkv, ids, heads):
-    count, length = ids.shape
-    span = min(512, length)
-    blocks = length // span
-    width = qkv.shape[1]
-    specs = [
-        pl.BlockSpec((span, width), lambda i, j: (i * blocks + j, 0)),
-        pl.BlockSpec((length, width), lambda i, j: (i, 0)),
-        pl.BlockSpec((1, 1, length), lambda i, j: (i, 0, 0)),
-        pl.BlockSpec((1, span, 1), lambda i, j: (i, j, 0)),
+def seq_gather(layout, own_ref, out_ref, width, sems):
+    send, recv, own_sem = sems
+    me = lax.axis_index("seq")
+    bits = [1 << bit for bit in reversed(range(layout.seq_bits))]
+
+    def block(mask):
+        start = jnp.bitwise_xor(me, mask) * width
+        return out_ref.at[:, pl.ds(pl.multiple_of(start, 128), width)]
+
+    copies = {}
+
+    def push(mask, bit):
+        copy = pltpu.make_async_remote_copy(
+            src_ref=own_ref if mask == 0 else block(mask),
+            dst_ref=block(mask),
+            send_sem=send.at[mask ^ bit],
+            recv_sem=recv.at[mask ^ bit],
+            device_id=layout.offset(bit, 0),
+            device_id_type=MESH,
+        )
+        copy.start()
+        copies[mask ^ bit] = copy
+
+    for bit in bits:
+        push(0, bit)
+    local = pltpu.make_async_copy(own_ref, block(0), own_sem)
+    local.start()
+    yield
+    held = [0]
+    for bit in bits:
+        for mask in held[1:]:
+            push(mask, bit)
+        new = [mask ^ bit for mask in held]
+        if bit != bits[-1]:
+            for mask in new:
+                copies[mask].wait_recv()
+        held = held + new
+    yield
+    for mask in held[len(held) // 2 :]:
+        copies[mask].wait_recv()
+    for copy in copies.values():
+        copy.wait_send()
+    local.wait()
+    yield
+
+
+def back_kernel(
+    layout,
+    sizes,
+    tok_ref,
+    cot_ref,
+    h1_ref,
+    h2_ref,
+    g_ref,
+    in_ref,
+    down_ref,
+    wa_ref,
+    qkv_ref,
+    att_ref,
+    mid_ref,
+    gains_ref,
+    ids_ref,
+    mixed,
+    grad_tok,
+    gain_sum,
+    gate_out,
+    up_out,
+    down_out,
+    attn_out,
+    in_recv,
+    down_recv,
+    attn_recv,
+    g_all,
+    h_all,
+    w_in,
+    w_down,
+    wa,
+    qkv,
+    attended,
+    hid,
+    grad_in,
+    middle,
+    total,
+    grad_mid,
+    tok,
+    cot,
+    grad_loc,
+    down_stage,
+    gains,
+    ids,
+    grad_kv,
+    terms,
+    gain_in,
+    gain_seq,
+    stage,
+    core_in,
+    arrive,
+    a_send,
+    a_recv,
+    a_relay,
+    a_own,
+    core_send,
+    core_recv,
+    s_send,
+    s_recv,
+    credit,
+    grad_send,
+    grad_recv,
+    join_send,
+    join_recv,
+    join_own,
+    gain_send,
+    gain_recv,
+    gs_send,
+    gs_recv,
+    load_sem,
+    pick_sem,
+):
+    share, fsdp, depth = layout.share, layout.fsdp, sizes.depth
+    seq_me, fsdp_me = lax.axis_index("seq"), lax.axis_index("fsdp")
+    query, hidden, rows = sizes.query, sizes.hidden, sizes.rows
+    base = query + 2 * HD
+    count = sizes.all_rows
+    scatter = (stage, core_in, arrive)
+    scatter_sem = (core_send, core_recv, s_send, s_recv)
+
+    loads = {}
+    for name, src, dst in (
+        ("in", in_ref, w_in),
+        ("h", h2_ref, h_all),
+        ("g", g_ref, g_all),
+        ("down", down_ref, w_down),
+        ("mid", mid_ref, middle),
+        ("tok", tok_ref, tok),
+        ("cot", cot_ref, cot),
+        ("gains", gains_ref, gains),
+        ("wa", wa_ref, wa),
+        ("qkv", qkv_ref, qkv),
+        ("att", att_ref, attended),
+        ("ids", ids_ref, ids),
+    ):
+        loads[name] = pltpu.make_async_copy(src, dst, load_sem.at[len(loads)])
+        loads[name].start()
+    greet_all(layout)
+    for name in ("in", "h", "g", "down"):
+        loads[name].wait()
+
+    def hidden_rows(r):
+        h = h_all[r]
+        gate = dot(h, w_in[:, :hidden])
+        upward = dot(h, w_in[:, hidden:])
+        grad = (RESIDUAL * g_all[r].astype(jnp.float32)).astype(jnp.bfloat16)
+        g_all[r] = grad
+        grad_hidden = dot(grad, w_down[...])
+        sigma = jax.nn.sigmoid(gate)
+        hid[r] = (gate * sigma * upward).astype(jnp.bfloat16)
+        grad_in[r, hidden:] = (grad_hidden * gate * sigma).astype(jnp.bfloat16)
+        grad_in[r, :hidden] = (
+            grad_hidden * upward * sigma * (1.0 + gate * (1.0 - sigma))
+        ).astype(jnp.bfloat16)
+
+    loop_rows(count, 256, hidden_rows)
+
+    sends = []
+    far = list(reversed(range(1, fsdp))) + [0]
+
+    def owner_columns(mask):
+        start = jnp.bitwise_xor(fsdp_me, mask) * depth
+        return pl.ds(pl.multiple_of(start, 128), depth)
+
+    def send_grad(mask, src, dst, index):
+        if mask == 0:
+            return
+        copy = pltpu.make_async_remote_copy(
+            src_ref=src,
+            dst_ref=dst.at[mask],
+            send_sem=grad_send.at[index, mask],
+            recv_sem=grad_recv.at[index, mask],
+            device_id=layout.offset(0, mask),
+            device_id_type=MESH,
+        )
+        copy.start()
+        sends.append((index, mask, copy))
+
+    def block(mask):
+        return pl.ds(mask * depth, depth)
+
+    def grad_down(mask):
+        down_stage[block(mask)] = dot_rows(g_all[:, owner_columns(mask)], hid[...]).astype(
+            jnp.bfloat16
+        )
+        send_grad(mask, down_stage.at[block(mask)], down_recv, 0)
+
+    for mask in far:
+        grad_down(mask)
+
+    def hidden_back(pair, ref):
+        left = grad_in[rows_at(pair * 2 * rows, 2 * rows)]
+
+        @pl.loop(0, sizes.width // 512)
+        def _(i):
+            piece = pl.ds(pl.multiple_of(i * 512, 512), 512)
+            ref[:, piece] = dot_cols(left, w_in[piece]).astype(jnp.bfloat16)
+
+    steps = scatter_steps(layout, rows, hidden_back, total, scatter, scatter_sem)
+    next(steps)
+
+    def grad_up(mask):
+        w_in[block(mask)] = dot_rows(h_all[:, owner_columns(mask)], grad_in[...]).astype(
+            jnp.bfloat16
+        )
+        send_grad(mask, w_in.at[block(mask)], in_recv, 1)
+
+    for turn in range(3):
+        for mask in far[turn * 3 : turn * 3 + 3]:
+            grad_up(mask)
+        next(steps)
+    finish(steps)
+    h1_copy = pltpu.make_async_copy(h1_ref, h_all, load_sem.at[len(loads)])
+    h1_copy.start()
+    for name in ("mid", "tok", "cot", "gains", "wa", "qkv", "att", "ids"):
+        loads[name].wait()
+    gain_one = gains[0:1].astype(jnp.float32)
+    gain_two = gains[8:9].astype(jnp.float32)
+    terms[...] = jnp.zeros_like(terms)
+
+    def norm_two(r):
+        values, normed = middle[r], total[r]
+        factor = rms_factor(values)
+        terms[1:2] += jnp.sum(normed * values * factor, axis=0, keepdims=True)
+        grad = cot[r].astype(jnp.float32) + norm_back(normed, values, factor, gain_two)
+        grad_mid[r] = grad
+        grad_loc[r] = (RESIDUAL * grad).astype(jnp.bfloat16)
+
+    loop_rows(rows, 32, norm_two)
+    finish(gather_steps(layout, rows, grad_loc, g_all, (a_send, a_recv, a_relay, a_own)))
+
+    def down_rows(pair, ref):
+        left = hid[rows_at(pair * 2 * rows, 2 * rows)]
+
+        @pl.loop(0, sizes.width // 512)
+        def _(i):
+            piece = pl.ds(pl.multiple_of(i * 512, 512), 512)
+            ref[:, piece] = dot_cols(left, w_down[piece]).astype(jnp.bfloat16)
+
+    steps = scatter_steps(layout, rows, down_rows, total, scatter, scatter_sem)
+    next(steps)
+
+    blocks = sizes.length // sizes.span
+
+    def attend_back_block(i):
+        seq = i // blocks
+        part = i % blocks
+        start = pl.multiple_of(part * sizes.span, sizes.span)
+        here = rows_at(seq * sizes.length + start, sizes.span)
+        grad_out = dot(g_all[here], wa[:, base:]).astype(jnp.bfloat16)
+        grads, grad_keys, grad_values = [], 0.0, 0.0
+        for head in range(sizes.heads):
+            left, keys, values, probs = attention_scores(sizes, qkv, ids, seq, start, head)
+            grad = grad_out[:, head * HD : (head + 1) * HD]
+            grad_probs = dot_cols(grad, values)
+            centre = jnp.sum(probs * grad_probs, axis=1, keepdims=True)
+            grad_scores = (probs * (grad_probs - centre)).astype(jnp.bfloat16)
+            grads.append(dot(grad_scores, keys) * (1.0 / HD))
+            grad_keys = grad_keys + dot_rows(grad_scores, left) * (1.0 / HD)
+            grad_values = grad_values + dot_rows(probs.astype(jnp.bfloat16), grad)
+        both = jnp.concatenate([grad_keys, grad_values], axis=1)
+
+        @pl.when(part == 0)
+        def _():
+            grad_kv[...] = both
+
+        @pl.when(part > 0)
+        def _():
+            grad_kv[...] += both
+
+        qkv[here, :query] = jnp.concatenate(grads, axis=1).astype(jnp.bfloat16)
+
+        @pl.when(part == blocks - 1)
+        def _():
+            qkv[rows_at(seq * sizes.length, sizes.length), query:] = grad_kv[...].astype(
+                jnp.bfloat16
+            )
+
+    turns = share * blocks
+
+    @pl.loop(0, turns // 2)
+    def _(i):
+        attend_back_block(i)
+
+    next(steps)
+
+    @pl.loop(turns // 2, turns)
+    def _(i):
+        attend_back_block(i)
+
+    finish(steps)
+    for bit in range(4):
+        pl.semaphore_signal(
+            credit, inc=1, device_id=layout.device(1 << bit), device_id_type=MESH
+        )
+
+    def mix(r):
+        mixed[r] = (middle[r] + RESIDUAL * total[r]).astype(jnp.bfloat16)
+
+    loop_rows(rows, 32, mix)
+    pl.semaphore_wait(credit, 4)
+
+    def qkv_back(pair, ref):
+        left = qkv[rows_at(pair * 2 * rows, 2 * rows)]
+
+        @pl.loop(0, sizes.width // 512)
+        def _(i):
+            piece = pl.ds(pl.multiple_of(i * 512, 512), 512)
+            ref[:, piece] = dot_cols(left, wa[piece, :base]).astype(jnp.bfloat16)
+
+    steps = scatter_steps(layout, rows, qkv_back, total, scatter, scatter_sem)
+    next(steps)
+    h1_copy.wait()
+
+    def grad_attn(mask):
+        cols = owner_columns(mask)
+        w_down[block(mask), :base] = dot_rows(h_all[:, cols], qkv[...]).astype(jnp.bfloat16)
+        w_down[block(mask), base : sizes.attn] = dot_rows(g_all[:, cols], attended[...]).astype(
+            jnp.bfloat16
+        )
+        send_grad(mask, w_down.at[block(mask), pl.ds(0, sizes.attn)], attn_recv, 2)
+
+    for turn in range(3):
+        for mask in far[turn * 3 : turn * 3 + 3]:
+            grad_attn(mask)
+        next(steps)
+    finish(steps)
+
+    def norm_one(r):
+        values, normed = tok[r].astype(jnp.float32), total[r]
+        factor = rms_factor(values)
+        terms[0:1] += jnp.sum(normed * values * factor, axis=0, keepdims=True)
+        grad = grad_mid[r] + norm_back(normed, values, factor, gain_one)
+        grad_tok[r] = grad.astype(jnp.bfloat16)
+
+    loop_rows(rows, 32, norm_one)
+    gain_copies = []
+    for mask in range(1, fsdp):
+        copy = pltpu.make_async_remote_copy(
+            src_ref=terms.at[:, owner_columns(mask)],
+            dst_ref=gain_in.at[mask],
+            send_sem=gain_send.at[mask],
+            recv_sem=gain_recv.at[mask],
+            device_id=layout.offset(0, mask),
+            device_id_type=MESH,
+        )
+        copy.start()
+        gain_copies.append(copy)
+
+    picks = []
+
+    def fetch(index, src, width, place):
+        for number, mask, copy in sends:
+            if number == index:
+                copy.wait_recv()
+                pick = pltpu.make_async_copy(
+                    src.at[mask],
+                    h_all.at[block(mask), pl.ds(place, width)],
+                    pick_sem.at[index, mask],
+                )
+                pick.start()
+                picks.append((index, pick))
+
+    def combine(index, own_ref, own_at, width, place, slot):
+        for number, pick in picks:
+            if number == index:
+                pick.wait()
+        mine = fsdp_me % share
+        for low in range(share):
+            value = 0.0
+            for mask in range(low, fsdp, share):
+                if mask:
+                    piece = h_all[block(mask), place : place + width]
+                else:
+                    piece = own_ref[block(0), own_at : own_at + width]
+                value = value + piece.astype(jnp.float32)
+            start = pl.multiple_of(jnp.bitwise_xor(mine, low) * width, 128)
+            stage[slot, :, pl.ds(start, width)] = value.astype(jnp.bfloat16)
+
+    def join(index, width, out):
+        sems = (join_send.at[index], join_recv.at[index], join_own.at[index])
+        return seq_gather(
+            layout, stage.at[index, :, pl.ds(0, share * width)], out, share * width, sems
+        )
+
+    fetch(0, down_recv, hidden, 2 * hidden)
+    combine(0, down_stage, 0, hidden, 2 * hidden, 0)
+    joins = [join(0, hidden, down_out)]
+    next(joins[0])
+    fetch(1, in_recv, 2 * hidden, 0)
+    for pick_index in (1, 2):
+        combine(1, w_in, (pick_index - 1) * hidden, hidden, (pick_index - 1) * hidden, pick_index)
+        picks.clear()
+        joins.append(join(pick_index, hidden, gate_out if pick_index == 1 else up_out))
+        next(joins[-1])
+    fetch(2, attn_recv, sizes.attn, 3 * hidden)
+    combine(2, w_down, 0, sizes.attn, 3 * hidden, 3)
+    joins.append(join(3, sizes.attn, attn_out))
+    next(joins[-1])
+
+    value = terms[:, owner_columns(0)]
+    for copy in gain_copies:
+        copy.wait()
+    for mask in range(1, fsdp):
+        value = value + gain_in[mask]
+    for bit in range(layout.seq_bits):
+        gain_seq[2 * bit] = value
+        copy = pltpu.make_async_remote_copy(
+            src_ref=gain_seq.at[2 * bit],
+            dst_ref=gain_seq.at[2 * bit + 1],
+            send_sem=gs_send.at[bit],
+            recv_sem=gs_recv.at[bit],
+            device_id=layout.offset(1 << bit, 0),
+            device_id_type=MESH,
+        )
+        copy.start()
+        copy.wait()
+        value = value + gain_seq[2 * bit + 1]
+    gain_sum[...] = value
+    for steps in joins:
+        next(steps)
+    for steps in joins:
+        finish(steps)
+    for _, _, copy in sends:
+        copy.wait_send()
+
+
+def back(layout, sizes, *args):
+    width, count = sizes.width, sizes.all_rows
+    hbm, vmem = pl.BlockSpec(memory_space=pl.ANY), pl.BlockSpec(memory_space=pltpu.VMEM)
+    share, depth, fsdp = layout.share, sizes.depth, layout.fsdp
+    rows, hidden, base = sizes.rows, sizes.hidden, sizes.query + 2 * HD
+    bf16, f32 = jnp.bfloat16, jnp.float32
+    shapes = [
+        ((rows, width), bf16, vmem),
+        ((rows, width), bf16, vmem),
+        ((8, depth), f32, vmem),
+        ((depth, GROUP * hidden), bf16, hbm),
+        ((depth, GROUP * hidden), bf16, hbm),
+        ((depth, GROUP * hidden), bf16, hbm),
+        ((depth, GROUP * sizes.attn), bf16, hbm),
+        ((fsdp, depth, 2 * hidden), bf16, hbm),
+        ((fsdp, depth, hidden), bf16, hbm),
+        ((fsdp, depth, sizes.attn), bf16, hbm),
     ]
-    args = (qkv, qkv, ids[:, None, :], ids[:, :, None])
-    return (count, blocks), span, length, specs, args
-
-
-def attend(qkv, ids, heads):
-    grid, span, length, specs, args = attention_specs(qkv, ids, heads)
+    dma = pltpu.SemaphoreType.DMA
+    seq = layout.seq
     return pl.pallas_call(
-        functools.partial(attend_kernel, heads),
-        grid=grid,
-        in_specs=specs,
-        out_specs=pl.BlockSpec((span, heads * HD), lambda i, j: (i * grid[1] + j, 0)),
-        out_shape=jax.ShapeDtypeStruct((qkv.shape[0], heads * HD), jnp.bfloat16),
-        compiler_params=pltpu.CompilerParams(vmem_limit_bytes=48 * 1024 * 1024),
-        name="attend",
+        functools.partial(back_kernel, layout, sizes),
+        out_shape=[jax.ShapeDtypeStruct(shape, dtype) for shape, dtype, _ in shapes],
+        in_specs=[hbm] * len(args),
+        out_specs=[spec for _, _, spec in shapes],
+        scratch_shapes=[
+            pltpu.VMEM((count, width), bf16),
+            pltpu.VMEM((count, width), bf16),
+            pltpu.VMEM((width, 2 * hidden), bf16),
+            pltpu.VMEM((width, hidden), bf16),
+            pltpu.VMEM((width, sizes.attn), bf16),
+            pltpu.VMEM((count, base), bf16),
+            pltpu.VMEM((count, sizes.query), bf16),
+            pltpu.VMEM((count, hidden), bf16),
+            pltpu.VMEM((count, 2 * hidden), bf16),
+            pltpu.VMEM((rows, width), f32),
+            pltpu.VMEM((rows, width), f32),
+            pltpu.VMEM((rows, width), f32),
+            pltpu.VMEM((rows, width), bf16),
+            pltpu.VMEM((rows, width), bf16),
+            pltpu.VMEM((rows, width), bf16),
+            pltpu.VMEM((width, hidden), bf16),
+            pltpu.VMEM((16, width), bf16),
+            pltpu.VMEM((share, 8, sizes.length), jnp.int32),
+            pltpu.VMEM((sizes.length, 2 * HD), f32),
+            pltpu.VMEM((8, width), f32),
+            pltpu.VMEM((fsdp, 8, depth), f32),
+            pltpu.VMEM((2 * layout.seq_bits, 8, depth), f32),
+        ]
+        + scatter_scratch(rows, width)
+        + gather_sems()
+        + scatter_sems()
+        + [pltpu.SemaphoreType.REGULAR]
+        + [dma((3, fsdp)), dma((3, fsdp)), dma((4, seq)), dma((4, seq)), dma((4,))]
+        + [dma((fsdp,)), dma((fsdp,)), dma((layout.seq_bits,)), dma((layout.seq_bits,))]
+        + [dma((16,)), dma((3, fsdp))],
+        compiler_params=pltpu.CompilerParams(
+            collective_id=4, has_side_effects=True, vmem_limit_bytes=62 * 1024 * 1024
+        ),
+        name="back",
     )(*args)
-
-
-def attend_back(qkv, ids, grad, heads):
-    grid, span, length, specs, args = attention_specs(qkv, ids, heads)
-    width = qkv.shape[1]
-    return pl.pallas_call(
-        functools.partial(attend_back_kernel, heads),
-        grid=grid,
-        in_specs=specs
-        + [pl.BlockSpec((span, heads * HD), lambda i, j: (i * grid[1] + j, 0))],
-        out_specs=pl.BlockSpec((length, width), lambda i, j: (i, 0)),
-        out_shape=jax.ShapeDtypeStruct(qkv.shape, jnp.bfloat16),
-        scratch_shapes=[pltpu.VMEM((length, 2 * HD), jnp.float32)],
-        compiler_params=pltpu.CompilerParams(vmem_limit_bytes=48 * 1024 * 1024),
-        name="attend_back",
-    )(*args, grad)
-
-
-def swap(array, axis, size, mask):
-    return lax.ppermute(array, axis, [(i, i ^ mask) for i in range(size)])
-
-
-def gather_seq(layout, array):
-    me = lax.axis_index("seq")
-    stack = array[None]
-    for bit in reversed(range(layout.seq_bits)):
-        other = swap(stack, "seq", layout.seq, 1 << bit)
-        upper = (me >> bit) % 2 == 1
-        pair = jnp.stack([jnp.where(upper, other, stack), jnp.where(upper, stack, other)], axis=1)
-        stack = pair.reshape((-1,) + array.shape)
-    return stack
-
-
-def slices(array, start, size):
-    return lax.dynamic_slice_in_dim(array, start, size, axis=1)
 
 
 def body(
@@ -970,14 +1146,7 @@
     cotangent,
 ):
     layout = Layout(lax.axis_size("seq"), lax.axis_size("fsdp"))
-    fsdp, share = layout.fsdp, layout.share
-    seq_me, fsdp_me = lax.axis_index("seq"), lax.axis_index("fsdp")
-    rows, width = tokens.shape[1], tokens.shape[2]
     depth = w_gate.shape[0]
-    hidden_cols = w_gate.shape[1] // GROUP
-    heads = H // GROUP
-    query_cols = heads * HD
-    kv_share = GROUP // KVH
     sizes = Sizes(layout, tokens, block_ids, w_query, w_gate)
     gains_own = jnp.concatenate(
         [jnp.broadcast_to(gain[None], (8, depth)) for gain in (gain_attn, gain_mlp)], axis=0
@@ -1010,109 +1179,45 @@
         w_up,
         w_down,
     )
-    w_in = attn_all[:, : query_cols + 2 * HD]
-    w_back = attn_all[:, query_cols + 2 * HD :]
-    attn_gain = gains_all[0:1].astype(jnp.float32)
-    mlp_gain = gains_all[8:9].astype(jnp.float32)
-    ids = ids_all[:, 0]
-    inputs = tokens[0].astype(jnp.float32)
-    factor_two = rms_factor(middle)
-    gate_up = dot(normed_two, in_all)
-    gate, upward = gate_up[:, :hidden_cols], gate_up[:, hidden_cols:]
-    sigma = jax.nn.sigmoid(gate)
-    hidden = (gate * sigma * upward).astype(jnp.bfloat16)
-    grad_down_in = (RESIDUAL * grad_all.astype(jnp.float32)).astype(jnp.bfloat16)
-    grad_hidden = dot(grad_down_in, down_all)
-    grad_upward = (grad_hidden * gate * sigma).astype(jnp.bfloat16)
-    grad_gate_in = (grad_hidden * upward * sigma * (1.0 + gate * (1.0 - sigma))).astype(
-        jnp.bfloat16
+    mixed, grad_tokens, gain_sum, grad_gate, grad_up, grad_down, grad_attn, _, _, _ = back(
+        layout,
+        sizes,
+        tokens[0],
+        cotangent[0],
+        normed_one,
+        normed_two,
+        grad_all,
+        in_all,
+        down_all,
+        attn_all,
+        qkv,
+        attended,
+        middle,
+        gains_all,
+        ids_all,
     )
-    grad_in = jnp.concatenate([grad_gate_in, grad_upward], axis=1)
-    grad_normed_two = token_scatter(layout, dot_cols(grad_in, in_all).astype(jnp.bfloat16))
-    down = token_scatter(layout, dot_cols(hidden, down_all).astype(jnp.bfloat16))
-    mixed = (middle + RESIDUAL * down).astype(jnp.bfloat16)
-
-    def spread(partials):
-        held = {}
-        for mask in range(fsdp):
-            piece = lax.dynamic_slice_in_dim(
-                partials, jnp.bitwise_xor(fsdp_me, mask) * depth, depth, axis=0
-            )
-            held[mask] = swap(piece, "fsdp", fsdp, mask) if mask else piece
-        sums = []
-        for low in range(share):
-            total = 0.0
-            for high in range(0, fsdp, share):
-                total = total + held[low + high].astype(jnp.float32)
-            sums.append(total.astype(jnp.bfloat16))
-        ordered = []
-        mine = fsdp_me % share
-        for column in range(share):
-            pick = sums[0]
-            for mask in range(1, share):
-                pick = jnp.where(jnp.bitwise_xor(mine, mask) == column, sums[mask], pick)
-            ordered.append(pick)
-        return gather_seq(layout, jnp.stack(ordered))
-
-    down_parts = spread(dot_rows(grad_down_in, hidden).astype(jnp.bfloat16))
-    in_parts = spread(dot_rows(normed_two, grad_in).astype(jnp.bfloat16))
-
-    grad_output = cotangent[0].astype(jnp.float32)
-    gain_two_term = jnp.sum(grad_normed_two * middle * factor_two, axis=0)
-    grad_middle = grad_output + norm_back(grad_normed_two, middle, factor_two, mlp_gain)
-    grad_branch = token_gather(layout, (RESIDUAL * grad_middle).astype(jnp.bfloat16))
-    grad_attended = dot(grad_branch, w_back).astype(jnp.bfloat16)
-    grad_qkv = attend_back(qkv, ids, grad_attended, heads)
-    grad_normed_one = token_scatter(layout, dot_cols(grad_qkv, w_in).astype(jnp.bfloat16))
-    attn_parts = spread(
-        jnp.concatenate(
-            [dot_rows(normed_one, grad_qkv), dot_rows(grad_branch, attended)], axis=1
-        ).astype(jnp.bfloat16)
-    )
-    factor_one = rms_factor(inputs)
-    gain_one_term = jnp.sum(grad_normed_one * inputs * factor_one, axis=0)
-    grad_inputs = grad_middle + norm_back(grad_normed_one, inputs, factor_one, attn_gain)
-
-    gains = jnp.stack([gain_one_term, gain_two_term])
-    gains = lax.psum(gains, ("seq", "fsdp"))
-    gains = lax.dynamic_slice_in_dim(gains, fsdp_me * depth, depth, axis=1)
-
-    def join(parts, start, size):
-        return jnp.concatenate(
-            [
-                parts[i][j, :, start : start + size]
-                for i in range(layout.seq)
-                for j in range(share)
-            ],
-            axis=1,
-        ).astype(jnp.float32)
-
-    def join_shared(parts, start, size):
-        columns = [
-            parts[i][j, :, start : start + size].astype(jnp.float32)
-            for i in range(layout.seq)
-            for j in range(share)
-        ]
-        return jnp.concatenate(
-            [
-                sum(columns[i : i + kv_share][1:], columns[i])
-                for i in range(0, GROUP, kv_share)
-            ],
-            axis=1,
-        )
+    parts = grad_attn.reshape(depth, GROUP, sizes.attn)
+    query, base = sizes.query, sizes.query + 2 * HD
+
+    def flat(columns):
+        return columns.astype(jnp.float32).reshape(depth, -1)
+
+    def shared(columns):
+        pairs = columns.astype(jnp.float32).reshape(depth, KVH, sizes.kv_share, HD)
+        return jnp.sum(pairs, axis=2).reshape(depth, -1)
 
     return (
         mixed[None],
-        grad_inputs.astype(jnp.bfloat16)[None],
-        gains[0],
-        join(attn_parts, 0, query_cols),
-        join_shared(attn_parts, query_cols, HD),
-        join_shared(attn_parts, query_cols + HD, HD),
-        join(attn_parts, query_cols + 2 * HD, query_cols),
-        gains[1],
-        join(in_parts, 0, hidden_cols),
-        join(in_parts, hidden_cols, hidden_cols),
-        join(down_parts, 0, hidden_cols),
+        grad_tokens[None],
+        gain_sum[0],
+        flat(parts[:, :, :query]),
+        shared(parts[:, :, query : query + HD]),
+        shared(parts[:, :, query + HD : base]),
+        flat(parts[:, :, base:]),
+        gain_sum[1],
+        flat(grad_gate),
+        flat(grad_up),
+        flat(grad_down),
     )
 
 

time: 861 us -> 737 us (0.86)
  Pallas kernels: 436 us -> 677 us
  waiting for transfers between devices: 93.2 us -> 0 us
  matrix products: 91.3 us -> 0 us
  blocking collectives: 63.6 us -> 0 us
  starting transfers between devices: 47.7 us -> 0 us
  other arithmetic: 65.4 us -> 23 us
  local copies, waits for them, and re-layouts: 51.5 us -> 22.3 us
    pallas_call x5 -> x1, Pallas kernels: 158 us -> 399 us  [back(): pl.pallas_call(functools.partial(back_kernel, layout, sizes), out_shape=[...]
    ppermute x27 -> x0, waiting for transfers between devices: 93.2 us -> none  [swap(): return lax.ppermute(array, axis, [(i, i ^ mask) for i in range(size)])]
    dot_general x10 -> x0, matrix products: 91.3 us -> none  [the longest x4 34.3 us: dot_rows(): lax.dot_general(left, right, (((0,), (0,)), ((), ())), preferred_element_...]
    psum x1 -> x0, blocking collectives: 63.6 us -> none  [body(): gains = lax.psum(gains, ('seq', 'fsdp'))]
    ppermute x27 -> x0, starting transfers between devices: 47.7 us -> none  [swap(): return lax.ppermute(array, axis, [(i, i ^ mask) for i in range(size)])]
    another operation x16 -> x0, other arithmetic: 31.6 us -> none  [the longest x9 25.4 us: gather_seq(): jnp.stack([jnp.where(upper, other, stack), jnp.where(upper, stack, other)...]
    another operation x4 -> x0, local copies, waits for them, and re-layouts: 22.4 us -> none  [the longest x3 22 us: gather_seq(): jnp.stack([jnp.where(upper, other, stack), jnp.where(upper, stack, other)...]
    convert_element_type x6 -> x3, other arithmetic: 18.1 us -> 13.1 us  [flat(): return columns.astype(jnp.float32).reshape(depth, -1)]
  transfers between devices with their start and end apart: 27 -> 0, of which waited for: 9 -> 0; matrix products, arithmetic and copies ran while one was open for 11% -> 0% of each run, Pallas kernels for 4% -> 0%
where the time goes in v3:
time: 737 us; the launch traced here: 724 us
  Pallas kernels  677 us (92%)
  other arithmetic  23 us (3%)
  local copies, waits for them, and re-layouts  22.3 us (3%)
    pallas_call x1, Pallas kernels, back(): pl.pallas_call(functools.partial(back_kernel, layout, sizes), out_shape=[...  399 us
    pallas_call x1, Pallas kernels, front(): pl.pallas_call(functools.partial(front_kernel, layout, sizes), out_shape=...  278 us

profile of v3, /device:TPU:15, one launch (start us, length us, event | category | flops | bytes accessed | tf_op | source)
XLA Modules:
  0.0 723.6 jit_solution(15745668394325103370)
XLA Ops:
  0.6 0.7 broadcast_in_dim.27
  1.3 0.7 broadcast_in_dim.28
  2.0 0.6 pad_maximum_fusion.gains_ref
  2.6 1.3 broadcast_in_dim.26.ids_ref
  3.9 278.0 %front.1 = (bf16[2048,2048]{1,0:T(8,128)(2,1)}, bf16[2048,2048]{1,0:T(8,128)(2,1)}, bf16[2048,2048]{1,0:T(8,128)(2,1)}, bf16[2048,1024]{1,0:T(8,128)(2,1)}, bf16...) custom-call(bf16[128,2048]{1,0:T(8,128)(2,1)} %bitcast.28, ...), custom_call_target="tpu_custom_call" | custom-call | tf_op jit(solution)/shard_map/front/pallas_call | solution.py:611
  281.9 399.2 %back.1 = (bf16[128,2048]{1,0:T(8,128)(2,1)}, bf16[128,2048]{1,0:T(8,128)(2,1)}, f32[8,256]{1,0:T(8,128)}, bf16[256,8192]{1,0:T(8,128)(2,1)}, bf16[256,8192]{1,0...) custom-call(bf16[128,2048]{1,0:T(8,128)(2,1)} %bitcast.29, ...), custom_call_target="tpu_custom_call" | custom-call | tf_op jit(solution)/shard_map/back/pallas_call | solution.py:1091
  681.1 1.3 fusion.1
  682.4 2.6 copy.29
  685.0 1.5 fusion
  686.4 3.9 convert_reduce_fusion
  690.3 2.3 copy.26
  692.7 2.0 copy.28
  694.7 5.1 convert_reduce_fusion.1
  699.8 2.3 copy.25
  702.1 2.0 copy.27
  704.1 0.3 slice_convert_fusion
  704.5 0.0 copy-start.2
  704.5 4.0 copy_bitcast_fusion
  708.5 0.0 copy-done.2
  708.5 0.0 copy-start.1
  708.5 4.4 convert_element_type.6
  712.9 0.0 copy-done.1
  712.9 0.0 copy-start
  712.9 4.4 convert_element_type.14
  717.3 0.0 copy-done
  717.3 0.0 copy-start.4
  717.3 0.0 copy-start.3
  717.3 4.4 convert_element_type.15
  721.7 0.0 copy-done.4
  721.7 0.8 copy.36
  722.5 0.0 copy-done.3
  722.5 0.8 copy.37
Async XLA Ops:
  704.5 4.0 copy-start.2
  708.5 4.4 copy-start.1
  712.9 4.4 copy-start
  717.3 4.4 copy-start.4
  717.3 5.2 copy-start.3

commit v4 on v3

--- a/solution.py
+++ b/solution.py
@@ -14,8 +14,15 @@
 RESIDUAL = 0.22
 GROUP = 16
 MESH = pl.DeviceIdType.MESH
-PIECES = ((0, 48), (48, 48), (96, 32))
-ORDERS = ((1, 2, 3), (2, 3, 1), (3, 1, 2))
+FIRST_PLAN = ((0, 48, (3, 2, 1)), (48, 48, (3, 1, 2)), (96, 32, (3, 2, 1)))
+COTANGENT_PLAN = ((0, 48, (3, 2, 1)), (48, 48, (3, 1, 2)), (96, 32, (3, 2, 1)))
+BRANCH_PLAN = ((0, 48, (1, 2, 3)), (48, 48, (2, 1, 3)), (96, 32, (1, 2, 3)))
+SECOND_PLAN = ((0, 48, (3, 2, 1)), (48, 48, (3, 1, 2)), (96, 32, (3, 2, 1)))
+HIDDEN_PLAN = ((0, 48, (1, 2, 3)), (48, 48, (2, 1, 3)), (96, 32, (1, 2, 3)))
+MIDDLE_PLAN = ((0, 48, (3, 2, 1)), (48, 48, (3, 1, 2)), (96, 32, (3, 2, 1)))
+DOWN_PLAN = ((0, 48, (1, 2, 3)), (48, 48, (2, 3, 1)), (96, 32, (3, 1, 2)))
+LAST_PLAN = ((0, 48, (1, 2, 3)), (48, 48, (2, 3, 1)), (96, 32, (3, 1, 2)))
+PLAN_PIECES = 4
 PAIRS = (7, 6, 5, 3, 4, 2, 1, 0)
 
 
@@ -91,18 +98,18 @@
     pl.semaphore_wait(barrier, len(pairs))
 
 
-def gather_steps(layout, rows, own_ref, dst_ref, sems):
+def gather_steps(layout, rows, plan, own_ref, dst_ref, sems):
     send, recv, relay_recv, own_sem = sems
     me = layout.member()
     sent, relayed = [], []
 
     def place(mask, piece):
-        start, size = PIECES[piece]
+        start, size, _ = plan[piece]
         block = jnp.bitwise_xor(me, mask)
         return dst_ref.at[rows_at(block * rows + start, size)]
 
     def source(mask, piece):
-        start, size = PIECES[piece]
+        start, size, _ = plan[piece]
         return own_ref.at[pl.ds(start, size)] if mask == 0 else place(mask, piece)
 
     def push(mask, piece, slot, dim):
@@ -131,38 +138,38 @@
         relayed.append(copy)
 
     first, second, third = {}, {}, {}
-    for piece, (a, b, c) in enumerate(ORDERS):
+    for piece, (_, _, (a, b, c)) in enumerate(plan):
         first[piece] = push(0, piece, 0, a)
-    for piece, (a, b, c) in enumerate(ORDERS):
+    for piece, (_, _, (a, b, c)) in enumerate(plan):
         second[piece] = [push(0, piece, 1, b)]
-    for piece, (a, b, c) in enumerate(ORDERS):
+    for piece, (_, _, (a, b, c)) in enumerate(plan):
         third[piece] = [push(0, piece, 3, c)]
     local = pltpu.make_async_copy(own_ref, dst_ref.at[rows_at(me * rows, rows)], own_sem)
     local.start()
-    for piece in range(len(ORDERS)):
+    for piece in range(len(plan)):
         relay(0, piece, 0)
     yield
-    for piece, (a, b, c) in enumerate(ORDERS):
+    for piece, (_, _, (a, b, c)) in enumerate(plan):
         first[piece].wait_recv()
         mask = span_mask((a,))
         second[piece].append(push(mask, piece, 2, b))
         third[piece].append(push(mask, piece, 4, c))
         relay(mask, piece, 1)
     yield
-    for piece, (a, b, c) in enumerate(ORDERS):
+    for piece, (_, _, (a, b, c)) in enumerate(plan):
         second[piece][0].wait_recv()
         mask = span_mask((b,))
         third[piece].append(push(mask, piece, 5, c))
         relay(mask, piece, 2)
     yield
-    for piece, (a, b, c) in enumerate(ORDERS):
+    for piece, (_, _, (a, b, c)) in enumerate(plan):
         second[piece][1].wait_recv()
         mask = span_mask((a, b))
         third[piece].append(push(mask, piece, 6, c))
         relay(mask, piece, 3)
     yield
     for turn, dims in enumerate(((2,), (0, 2), (1, 2), (0, 1, 2))):
-        for piece, order in enumerate(ORDERS):
+        for piece, (_, _, order) in enumerate(plan):
             third[piece][turn].wait_recv()
             relay(span_mask([order[d] for d in dims]), piece, 4 + turn)
     yield
@@ -182,7 +189,7 @@
 
 
 def gather_sems():
-    count = len(ORDERS)
+    count = PLAN_PIECES
     return [
         pltpu.SemaphoreType.DMA,
         pltpu.SemaphoreType.DMA((count, 7)),
@@ -196,9 +203,10 @@
         pass
 
 
-def scatter_steps(layout, rows, produce, total, buffers, sems):
+def scatter_steps(layout, rows, plan, produce, total, buffers, tail, sems):
     stage, core_in, arrive = buffers
-    core_send, core_recv, send, recv = sems
+    last_out, last_in = tail
+    core_send, core_recv, send, recv, last_send, last_recv = sems
     me = layout.member()
     core = me % 2
     own = pl.multiple_of(core * rows, 16)
@@ -211,7 +219,7 @@
             body(pl.multiple_of(i * 16 + start, 16))
 
     def push(piece, pair, dim, slot):
-        start, size = PIECES[piece]
+        start, size, _ = plan[piece]
         copy = pltpu.make_async_remote_copy(
             src_ref=stage.at[pair, rows_at(own + start, size)],
             dst_ref=arrive.at[slot, pl.ds(start, size)],
@@ -236,7 +244,7 @@
 
         chunked(0, rows, body)
         mask = pair * 2
-        for piece, (a, b, c) in enumerate(ORDERS):
+        for piece, (_, _, (a, b, c)) in enumerate(plan):
             if mask & (1 << a):
                 slot = (1 if mask & (1 << b) else 0) + (2 if mask & (1 << c) else 0)
                 one[piece, slot] = push(piece, pair, a, slot)
@@ -260,7 +268,7 @@
     yield
 
     def keep(piece, pair, slots):
-        start, size = PIECES[piece]
+        start, size, _ = plan[piece]
 
         def body(r):
             value = stage[pair, rows_at(own + r, 16)].astype(jnp.float32)
@@ -270,36 +278,58 @@
 
         chunked(start, size, body)
 
-    for piece, (a, b, c) in enumerate(ORDERS):
+    for piece, (_, _, (a, b, c)) in enumerate(plan):
         for slot, dims in ((3, (b, c)), (1, (b,))):
             pair = span_mask(dims) // 2
             one[piece, slot].wait_recv()
             keep(piece, pair, (slot,))
             two[piece, slot] = push(piece, pair, b, 4 + slot // 2)
     yield
-    for piece, (a, b, c) in enumerate(ORDERS):
+    for piece, (start, size, (a, b, c)) in enumerate(plan):
         pair = span_mask((c,)) // 2
         one[piece, 2].wait_recv()
         two[piece, 3].wait_recv()
-        keep(piece, pair, (2, 5))
-        three[piece] = push(piece, pair, c, 6)
-    yield
-    for piece, (a, b, c) in enumerate(ORDERS):
-        start, size = PIECES[piece]
+
+        def onward(r):
+            value = stage[pair, rows_at(own + r, 16)].astype(jnp.float32)
+            for slot in (2, 5):
+                value = value + arrive[slot, rows_at(r, 16)].astype(jnp.float32)
+            last_out[rows_at(r, 16)] = value.astype(jnp.bfloat16)
+
+        chunked(start, size, onward)
+        three[piece] = pltpu.make_async_remote_copy(
+            src_ref=last_out.at[pl.ds(start, size)],
+            dst_ref=last_in.at[pl.ds(start, size)],
+            send_sem=last_send.at[piece],
+            recv_sem=last_recv.at[piece],
+            device_id=layout.device(1 << c),
+            device_id_type=MESH,
+        )
+        three[piece].start()
+    for piece, (start, size, (a, b, c)) in enumerate(plan):
         one[piece, 0].wait_recv()
         two[piece, 1].wait_recv()
-        three[piece].wait_recv()
-
-        def body(r):
+
+        def gathered(r):
             value = stage[0, rows_at(own + r, 16)].astype(jnp.float32)
-            for slot in (0, 4, 6):
+            for slot in (0, 4):
                 value = value + arrive[slot, rows_at(r, 16)].astype(jnp.float32)
             total[rows_at(r, 16)] = value
 
-        chunked(start, size, body)
-    for group in (copies, one, two, three):
+        chunked(start, size, gathered)
+    for group in (copies, one, two):
         for copy in group.values():
             copy.wait_send()
+    yield
+    for piece, (start, size, _) in enumerate(plan):
+        three[piece].wait_recv()
+
+        def finished(r):
+            total[rows_at(r, 16)] += last_in[rows_at(r, 16)].astype(jnp.float32)
+
+        chunked(start, size, finished)
+    for copy in three.values():
+        copy.wait_send()
     yield
 
 
@@ -307,17 +337,21 @@
     return [
         pltpu.VMEM((8, 2 * rows, width), jnp.bfloat16),
         pltpu.VMEM((8, rows, width), jnp.bfloat16),
-        pltpu.VMEM((7, rows, width), jnp.bfloat16),
+        pltpu.VMEM((6, rows, width), jnp.bfloat16),
+        pltpu.VMEM((rows, width), jnp.bfloat16),
+        pltpu.VMEM((rows, width), jnp.bfloat16),
     ]
 
 
 def scatter_sems():
-    count = len(ORDERS)
+    count = PLAN_PIECES
     return [
         pltpu.SemaphoreType.DMA((8,)),
         pltpu.SemaphoreType.DMA((8,)),
-        pltpu.SemaphoreType.DMA((count, 7)),
-        pltpu.SemaphoreType.DMA((count, 7)),
+        pltpu.SemaphoreType.DMA((count, 6)),
+        pltpu.SemaphoreType.DMA((count, 6)),
+        pltpu.SemaphoreType.DMA((count,)),
+        pltpu.SemaphoreType.DMA((count,)),
     ]
 
 
@@ -339,6 +373,12 @@
         self.all_rows = GROUP * self.rows
         self.span = max(128, min(self.length, 512 * 512 // self.length))
         self.kv_share = GROUP // KVH
+
+    def kv_columns(self, layout):
+        return max(1, layout.share // self.kv_share) * HD
+
+    def attn_joined(self, layout):
+        return 2 * layout.share * self.query + 2 * self.kv_columns(layout)
 
 
 def kv_half(layout, target, chunk):
@@ -394,6 +434,8 @@
     stage,
     core_in,
     arrive,
+    last_out,
+    last_in,
     x_send,
     x_recv,
     x_relay,
@@ -410,6 +452,8 @@
     core_recv,
     s_send,
     s_recv,
+    last_send,
+    last_recv,
     attn_send,
     attn_recv,
     gain_send,
@@ -437,17 +481,15 @@
         return ref.at[:, pl.ds(pl.multiple_of(start, 128), size)]
 
     load(tok_ref, tok)
+    own_rows = pl.ds(pl.multiple_of(fsdp_me * depth, 128), depth)
+    load(gains_ref, gains.at[:, own_rows])
     load(columns(wq_ref, seq_me * share * query, share * query), wq)
     load(columns(wo_ref, seq_me * share * query, share * query), wo)
     chunk = seq_me * share // (2 * sizes.kv_share) * 128
     load(columns(wk_ref, chunk, 128), wk)
     load(columns(wv_ref, chunk, 128), wv)
-    own_rows = pl.ds(pl.multiple_of(fsdp_me * depth, 128), depth)
-    load(gains_ref, gains.at[:, own_rows])
     load(ids_ref, ids.at[fsdp_me % share])
     greet_all(layout)
-    x_steps = gather_steps(layout, rows, tok_ref, x_all, (x_send, x_recv, x_relay, x_own))
-    next(x_steps)
     small = []
     for mask in range(1, fsdp):
         copy = pltpu.make_async_remote_copy(
@@ -455,17 +497,6 @@
             dst_ref=gains.at[:, own_rows],
             send_sem=gain_send.at[mask],
             recv_sem=gain_recv.at[mask],
-            device_id=layout.offset(0, mask),
-            device_id_type=MESH,
-        )
-        copy.start()
-        small.append(copy)
-    for mask in range(1, share):
-        copy = pltpu.make_async_remote_copy(
-            src_ref=ids_ref,
-            dst_ref=ids.at[fsdp_me % share],
-            send_sem=id_send.at[mask],
-            recv_sem=id_recv.at[mask],
             device_id=layout.offset(0, mask),
             device_id_type=MESH,
         )
@@ -497,21 +528,34 @@
         copy.start()
         attn.append(copy)
     wa[own_rows] = pack[fsdp_me % share]
-    finish(x_steps)
     for copy in small:
         copy.wait()
-
     gain_one = gains[0:1].astype(jnp.float32)
 
     def norm(r):
-        values = x_all[r].astype(jnp.float32)
-        x_all[r] = (values * rms_factor(values) * gain_one).astype(jnp.bfloat16)
-
-    loop_rows(sizes.all_rows, 64, norm)
-    h1_copy = pltpu.make_async_copy(x_all, h1_out, load_sem.at[0])
-    h1_copy.start()
-    for copy in attn:
-        copy.wait()
+        values = tok[r].astype(jnp.float32)
+        h2[r] = (values * rms_factor(values) * gain_one).astype(jnp.bfloat16)
+
+    loop_rows(rows, 32, norm)
+    x_steps = gather_steps(layout, rows, FIRST_PLAN, h2, x_all, (x_send, x_recv, x_relay, x_own))
+    next(x_steps)
+    id_copies = []
+    for mask in range(1, share):
+        copy = pltpu.make_async_remote_copy(
+            src_ref=ids_ref,
+            dst_ref=ids.at[fsdp_me % share],
+            send_sem=id_send.at[mask],
+            recv_sem=id_recv.at[mask],
+            device_id=layout.offset(0, mask),
+            device_id_type=MESH,
+        )
+        copy.start()
+        id_copies.append(copy)
+    g_steps = gather_steps(
+        layout, rows, COTANGENT_PLAN, cot_ref, g_out, (g_send, g_recv, g_relay, g_own)
+    )
+    next(g_steps)
+    next(x_steps)
 
     mlp = []
 
@@ -537,12 +581,20 @@
 
     send_mlp(wg_ref, in_out, 0, 0)
     send_mlp(wu_ref, in_out, hidden, 1)
-    send_mlp(wd_ref, down_out, 0, 2)
+    finish(x_steps)
+    h1_copy = pltpu.make_async_copy(x_all, h1_out, load_sem.at[0])
+    h1_copy.start()
+    next(g_steps)
+    for copy in attn:
+        copy.wait()
 
     def project(r):
         qkv[r] = dot(x_all[r], wa[:, : query + 2 * HD]).astype(jnp.bfloat16)
 
     loop_rows(sizes.all_rows, 256, project)
+    next(g_steps)
+    for copy in id_copies:
+        copy.wait()
 
     blocks = sizes.length // sizes.span
 
@@ -566,12 +618,15 @@
             piece = pl.ds(pl.multiple_of(i * 512, 512), 512)
             ref[:, piece] = dot_cols(block, wa[piece, query + 2 * HD :]).astype(jnp.bfloat16)
 
-    finish(
-        scatter_steps(
-            layout, rows, out_rows, middle, (stage, core_in, arrive),
-            (core_send, core_recv, s_send, s_recv),
-        )
-    )
+    next(g_steps)
+    next(g_steps)
+    steps = scatter_steps(
+        layout, rows, BRANCH_PLAN, out_rows, middle, (stage, core_in, arrive),
+        (last_out, last_in), (core_send, core_recv, s_send, s_recv, last_send, last_recv),
+    )
+    next(steps)
+    next(g_steps)
+    finish(steps)
     gain_two = gains[8:9].astype(jnp.float32)
 
     def second(r):
@@ -580,10 +635,14 @@
         h2[r] = (values * rms_factor(values) * gain_two).astype(jnp.bfloat16)
 
     loop_rows(rows, 32, second)
-    h_steps = gather_steps(layout, rows, h2, h2_out, (h_send, h_recv, h_relay, h_own))
+    h_steps = gather_steps(
+        layout, rows, SECOND_PLAN, h2, h2_out, (h_send, h_recv, h_relay, h_own)
+    )
+    next(h_steps)
+    next(h_steps)
+    send_mlp(wd_ref, down_out, 0, 2)
+    finish(g_steps)
     finish(h_steps)
-    g_steps = gather_steps(layout, rows, cot_ref, g_out, (g_send, g_recv, g_relay, g_own))
-    finish(g_steps)
     for copy in mlp:
         copy.wait()
     h1_copy.wait()
@@ -635,8 +694,8 @@
     )(*args)
 
 
-def seq_gather(layout, own_ref, out_ref, width, sems):
-    send, recv, own_sem = sems
+def seq_gather(layout, out_ref, width, sems):
+    send, recv = sems
     me = lax.axis_index("seq")
     bits = [1 << bit for bit in reversed(range(layout.seq_bits))]
 
@@ -648,7 +707,7 @@
 
     def push(mask, bit):
         copy = pltpu.make_async_remote_copy(
-            src_ref=own_ref if mask == 0 else block(mask),
+            src_ref=block(mask),
             dst_ref=block(mask),
             send_sem=send.at[mask ^ bit],
             recv_sem=recv.at[mask ^ bit],
@@ -660,8 +719,6 @@
 
     for bit in bits:
         push(0, bit)
-    local = pltpu.make_async_copy(own_ref, block(0), own_sem)
-    local.start()
     yield
     held = [0]
     for bit in bits:
@@ -677,7 +734,6 @@
         copies[mask].wait_recv()
     for copy in copies.values():
         copy.wait_send()
-    local.wait()
     yield
 
 
@@ -704,7 +760,8 @@
     up_out,
     down_out,
     attn_out,
-    in_recv,
+    gate_recv,
+    up_recv,
     down_recv,
     attn_recv,
     g_all,
@@ -720,8 +777,6 @@
     total,
     grad_mid,
     tok,
-    cot,
-    grad_loc,
     down_stage,
     gains,
     ids,
@@ -729,9 +784,15 @@
     terms,
     gain_in,
     gain_seq,
+    own_sum,
     stage,
     core_in,
     arrive,
+    last_out,
+    last_in,
+    down_total,
+    down_last_out,
+    down_last_in,
     a_send,
     a_recv,
     a_relay,
@@ -740,12 +801,16 @@
     core_recv,
     s_send,
     s_recv,
+    last_send,
+    last_recv,
+    down_last_send,
+    down_last_recv,
     credit,
     grad_send,
     grad_recv,
     join_send,
     join_recv,
-    join_own,
+    own_sem,
     gain_send,
     gain_recv,
     gs_send,
@@ -759,7 +824,8 @@
     base = query + 2 * HD
     count = sizes.all_rows
     scatter = (stage, core_in, arrive)
-    scatter_sem = (core_send, core_recv, s_send, s_recv)
+    sems = (core_send, core_recv, s_send, s_recv)
+    scatter_sem = sems + (last_send, last_recv)
 
     loads = {}
     for name, src, dst in (
@@ -769,7 +835,7 @@
         ("down", down_ref, w_down),
         ("mid", mid_ref, middle),
         ("tok", tok_ref, tok),
-        ("cot", cot_ref, cot),
+        ("cot", cot_ref, down_last_out),
         ("gains", gains_ref, gains),
         ("wa", wa_ref, wa),
         ("qkv", qkv_ref, qkv),
@@ -839,14 +905,13 @@
             piece = pl.ds(pl.multiple_of(i * 512, 512), 512)
             ref[:, piece] = dot_cols(left, w_in[piece]).astype(jnp.bfloat16)
 
-    steps = scatter_steps(layout, rows, hidden_back, total, scatter, scatter_sem)
+    steps = scatter_steps(layout, rows, HIDDEN_PLAN, hidden_back, total, scatter, (last_out, last_in), scatter_sem)
     next(steps)
 
     def grad_up(mask):
         w_in[block(mask)] = dot_rows(h_all[:, owner_columns(mask)], grad_in[...]).astype(
             jnp.bfloat16
         )
-        send_grad(mask, w_in.at[block(mask)], in_recv, 1)
 
     for turn in range(3):
         for mask in far[turn * 3 : turn * 3 + 3]:
@@ -865,12 +930,21 @@
         values, normed = middle[r], total[r]
         factor = rms_factor(values)
         terms[1:2] += jnp.sum(normed * values * factor, axis=0, keepdims=True)
-        grad = cot[r].astype(jnp.float32) + norm_back(normed, values, factor, gain_two)
+        grad = down_last_out[r].astype(jnp.float32) + norm_back(normed, values, factor, gain_two)
         grad_mid[r] = grad
-        grad_loc[r] = (RESIDUAL * grad).astype(jnp.bfloat16)
+        last_out[r] = (RESIDUAL * grad).astype(jnp.bfloat16)
 
     loop_rows(rows, 32, norm_two)
-    finish(gather_steps(layout, rows, grad_loc, g_all, (a_send, a_recv, a_relay, a_own)))
+    a_steps = gather_steps(
+        layout, rows, MIDDLE_PLAN, last_out, g_all, (a_send, a_recv, a_relay, a_own)
+    )
+    next(a_steps)
+    next(a_steps)
+    for mask in far:
+        send_grad(mask, w_in.at[block(mask), pl.ds(0, hidden)], gate_recv, 1)
+    for mask in far:
+        send_grad(mask, w_in.at[block(mask), pl.ds(hidden, hidden)], up_recv, 2)
+    finish(a_steps)
 
     def down_rows(pair, ref):
         left = hid[rows_at(pair * 2 * rows, 2 * rows)]
@@ -880,8 +954,81 @@
             piece = pl.ds(pl.multiple_of(i * 512, 512), 512)
             ref[:, piece] = dot_cols(left, w_down[piece]).astype(jnp.bfloat16)
 
-    steps = scatter_steps(layout, rows, down_rows, total, scatter, scatter_sem)
-    next(steps)
+    steps_low = scatter_steps(
+        layout, rows, DOWN_PLAN, down_rows, down_total, scatter, (down_last_out, down_last_in),
+        sems + (down_last_send, down_last_recv),
+    )
+    next(steps_low)
+
+    mine = fsdp_me % share
+
+    def collect(index, src, width, own_piece, landing, combine, out, out_width):
+        picks = []
+        for number, mask, copy in sends:
+            if number == index:
+                copy.wait_recv()
+                pick = pltpu.make_async_copy(
+                    src.at[mask], landing.at[block(mask)], pick_sem.at[index, mask]
+                )
+                pick.start()
+                picks.append(pick)
+        yield
+        for pick in picks:
+            pick.wait()
+
+        def terms_of(low, start, size):
+            cols = pl.ds(start, size)
+            value = own_piece[:, cols] if low == 0 else landing[block(low), cols]
+            value = value.astype(jnp.float32)
+            for mask in range(low + share, fsdp, share):
+                value = value + landing[block(mask), cols].astype(jnp.float32)
+            return value
+
+        combine(terms_of, width)
+        home = pl.multiple_of(seq_me * out_width, 128)
+        local = pltpu.make_async_copy(
+            own_sum.at[:, pl.ds(0, out_width)], out.at[:, pl.ds(home, out_width)], own_sem.at[index]
+        )
+        local.start()
+        local.wait()
+        yield from seq_gather(layout, out, out_width, (join_send.at[index], join_recv.at[index]))
+
+    def place_columns(terms_of, width):
+        for low in range(share):
+            start = pl.multiple_of(jnp.bitwise_xor(mine, low) * width, 128)
+            own_sum[:, pl.ds(start, width)] = terms_of(low, 0, width).astype(jnp.bfloat16)
+
+    def place_attn(terms_of, width):
+        for low in range(share):
+            for source, target in ((0, 0), (base, share * query)):
+                start = pl.multiple_of(target + jnp.bitwise_xor(mine, low) * query, 128)
+                own_sum[:, pl.ds(start, query)] = terms_of(low, source, query).astype(
+                    jnp.bfloat16
+                )
+        both = sizes.kv_columns(layout)
+        at = 2 * share * query
+        for source in (query, query + HD):
+            heads = []
+            for first in range(0, share, sizes.kv_share):
+                value = terms_of(first, source, HD)
+                for low in range(first + 1, min(share, first + sizes.kv_share)):
+                    value = value + terms_of(low, source, HD)
+                heads.append(value)
+            value = heads[0]
+            if len(heads) == 2:
+                upper = mine // sizes.kv_share == 1
+                value = jnp.concatenate(
+                    [jnp.where(upper, heads[1], heads[0]), jnp.where(upper, heads[0], heads[1])],
+                    axis=1,
+                )
+            own_sum[:, at : at + both] = value.astype(jnp.bfloat16)
+            at += both
+
+    joined = share * hidden
+    steps_down = collect(
+        0, down_recv, hidden, down_stage.at[block(0)], hid, place_columns, down_out, joined
+    )
+    next(steps_down)
 
     blocks = sizes.length // sizes.span
 
@@ -925,22 +1072,20 @@
     def _(i):
         attend_back_block(i)
 
-    next(steps)
+    next(steps_down)
+    next(steps_low)
 
     @pl.loop(turns // 2, turns)
     def _(i):
         attend_back_block(i)
 
-    finish(steps)
+    next(steps_low)
     for bit in range(4):
         pl.semaphore_signal(
             credit, inc=1, device_id=layout.device(1 << bit), device_id_type=MESH
         )
 
-    def mix(r):
-        mixed[r] = (middle[r] + RESIDUAL * total[r]).astype(jnp.bfloat16)
-
-    loop_rows(rows, 32, mix)
+    next(steps_down)
     pl.semaphore_wait(credit, 4)
 
     def qkv_back(pair, ref):
@@ -951,8 +1096,6 @@
             piece = pl.ds(pl.multiple_of(i * 512, 512), 512)
             ref[:, piece] = dot_cols(left, wa[piece, :base]).astype(jnp.bfloat16)
 
-    steps = scatter_steps(layout, rows, qkv_back, total, scatter, scatter_sem)
-    next(steps)
     h1_copy.wait()
 
     def grad_attn(mask):
@@ -961,12 +1104,22 @@
         w_down[block(mask), base : sizes.attn] = dot_rows(g_all[:, cols], attended[...]).astype(
             jnp.bfloat16
         )
-        send_grad(mask, w_down.at[block(mask), pl.ds(0, sizes.attn)], attn_recv, 2)
-
-    for turn in range(3):
-        for mask in far[turn * 3 : turn * 3 + 3]:
-            grad_attn(mask)
-        next(steps)
+        send_grad(mask, w_down.at[block(mask), pl.ds(0, sizes.attn)], attn_recv, 3)
+
+    for mask in far[: fsdp // 2]:
+        grad_attn(mask)
+    steps = scatter_steps(layout, rows, LAST_PLAN, qkv_back, total, scatter, (last_out, last_in), scatter_sem)
+    next(steps)
+    for mask in far[fsdp // 2 :]:
+        grad_attn(mask)
+    steps_gate = collect(
+        1, gate_recv, hidden, w_in.at[block(0), pl.ds(0, hidden)], grad_in.at[:, pl.ds(0, hidden)],
+        place_columns, gate_out, joined,
+    )
+    next(steps_gate)
+    next(steps)
+    next(steps_gate)
+    next(steps)
     finish(steps)
 
     def norm_one(r):
@@ -977,6 +1130,12 @@
         grad_tok[r] = grad.astype(jnp.bfloat16)
 
     loop_rows(rows, 32, norm_one)
+    finish(steps_low)
+
+    def mix(r):
+        mixed[r] = (middle[r] + RESIDUAL * down_total[r]).astype(jnp.bfloat16)
+
+    loop_rows(rows, 32, mix)
     gain_copies = []
     for mask in range(1, fsdp):
         copy = pltpu.make_async_remote_copy(
@@ -990,56 +1149,20 @@
         copy.start()
         gain_copies.append(copy)
 
-    picks = []
-
-    def fetch(index, src, width, place):
-        for number, mask, copy in sends:
-            if number == index:
-                copy.wait_recv()
-                pick = pltpu.make_async_copy(
-                    src.at[mask],
-                    h_all.at[block(mask), pl.ds(place, width)],
-                    pick_sem.at[index, mask],
-                )
-                pick.start()
-                picks.append((index, pick))
-
-    def combine(index, own_ref, own_at, width, place, slot):
-        for number, pick in picks:
-            if number == index:
-                pick.wait()
-        mine = fsdp_me % share
-        for low in range(share):
-            value = 0.0
-            for mask in range(low, fsdp, share):
-                if mask:
-                    piece = h_all[block(mask), place : place + width]
-                else:
-                    piece = own_ref[block(0), own_at : own_at + width]
-                value = value + piece.astype(jnp.float32)
-            start = pl.multiple_of(jnp.bitwise_xor(mine, low) * width, 128)
-            stage[slot, :, pl.ds(start, width)] = value.astype(jnp.bfloat16)
-
-    def join(index, width, out):
-        sems = (join_send.at[index], join_recv.at[index], join_own.at[index])
-        return seq_gather(
-            layout, stage.at[index, :, pl.ds(0, share * width)], out, share * width, sems
-        )
-
-    fetch(0, down_recv, hidden, 2 * hidden)
-    combine(0, down_stage, 0, hidden, 2 * hidden, 0)
-    joins = [join(0, hidden, down_out)]
-    next(joins[0])
-    fetch(1, in_recv, 2 * hidden, 0)
-    for pick_index in (1, 2):
-        combine(1, w_in, (pick_index - 1) * hidden, hidden, (pick_index - 1) * hidden, pick_index)
-        picks.clear()
-        joins.append(join(pick_index, hidden, gate_out if pick_index == 1 else up_out))
-        next(joins[-1])
-    fetch(2, attn_recv, sizes.attn, 3 * hidden)
-    combine(2, w_down, 0, sizes.attn, 3 * hidden, 3)
-    joins.append(join(3, sizes.attn, attn_out))
-    next(joins[-1])
+    steps_up = collect(
+        2, up_recv, hidden, w_in.at[block(0), pl.ds(hidden, hidden)], grad_in.at[:, pl.ds(hidden, hidden)],
+        place_columns, up_out, joined,
+    )
+    next(steps_up)
+    next(steps_up)
+    next(steps_gate)
+    steps_attn = collect(
+        3, attn_recv, sizes.attn, w_down.at[block(0), pl.ds(0, sizes.attn)], h_all.at[:, pl.ds(0, sizes.attn)],
+        place_attn, attn_out, sizes.attn_joined(layout),
+    )
+    next(steps_attn)
+    next(steps_attn)
+    next(steps_up)
 
     value = terms[:, owner_columns(0)]
     for copy in gain_copies:
@@ -1060,9 +1183,7 @@
         copy.wait()
         value = value + gain_seq[2 * bit + 1]
     gain_sum[...] = value
-    for steps in joins:
-        next(steps)
-    for steps in joins:
+    for steps in (steps_attn, steps_down, steps_gate, steps_up):
         finish(steps)
     for _, _, copy in sends:
         copy.wait_send()
@@ -1081,8 +1202,9 @@
         ((depth, GROUP * hidden), bf16, hbm),
         ((depth, GROUP * hidden), bf16, hbm),
         ((depth, GROUP * hidden), bf16, hbm),
-        ((depth, GROUP * sizes.attn), bf16, hbm),
-        ((fsdp, depth, 2 * hidden), bf16, hbm),
+        ((depth, layout.seq * sizes.attn_joined(layout)), bf16, hbm),
+        ((fsdp, depth, hidden), bf16, hbm),
+        ((fsdp, depth, hidden), bf16, hbm),
         ((fsdp, depth, hidden), bf16, hbm),
         ((fsdp, depth, sizes.attn), bf16, hbm),
     ]
@@ -1107,8 +1229,6 @@
             pltpu.VMEM((rows, width), f32),
             pltpu.VMEM((rows, width), f32),
             pltpu.VMEM((rows, width), bf16),
-            pltpu.VMEM((rows, width), bf16),
-            pltpu.VMEM((rows, width), bf16),
             pltpu.VMEM((width, hidden), bf16),
             pltpu.VMEM((16, width), bf16),
             pltpu.VMEM((share, 8, sizes.length), jnp.int32),
@@ -1116,14 +1236,21 @@
             pltpu.VMEM((8, width), f32),
             pltpu.VMEM((fsdp, 8, depth), f32),
             pltpu.VMEM((2 * layout.seq_bits, 8, depth), f32),
+            pltpu.VMEM((depth, share * max(hidden, 2 * sizes.query + 2 * HD)), bf16),
         ]
         + scatter_scratch(rows, width)
+        + [
+            pltpu.VMEM((rows, width), f32),
+            pltpu.VMEM((rows, width), bf16),
+            pltpu.VMEM((rows, width), bf16),
+        ]
         + gather_sems()
         + scatter_sems()
+        + [dma((PLAN_PIECES,)), dma((PLAN_PIECES,))]
         + [pltpu.SemaphoreType.REGULAR]
-        + [dma((3, fsdp)), dma((3, fsdp)), dma((4, seq)), dma((4, seq)), dma((4,))]
+        + [dma((4, fsdp)), dma((4, fsdp)), dma((4, seq)), dma((4, seq)), dma((4,))]
         + [dma((fsdp,)), dma((fsdp,)), dma((layout.seq_bits,)), dma((layout.seq_bits,))]
-        + [dma((16,)), dma((3, fsdp))],
+        + [dma((16,)), dma((4, fsdp))],
         compiler_params=pltpu.CompilerParams(
             collective_id=4, has_side_effects=True, vmem_limit_bytes=62 * 1024 * 1024
         ),
@@ -1179,7 +1306,7 @@
         w_up,
         w_down,
     )
-    mixed, grad_tokens, gain_sum, grad_gate, grad_up, grad_down, grad_attn, _, _, _ = back(
+    mixed, grad_tokens, gain_sum, grad_gate, grad_up, grad_down, grad_attn, *_ = back(
         layout,
         sizes,
         tokens[0],
@@ -1196,24 +1323,26 @@
         gains_all,
         ids_all,
     )
-    parts = grad_attn.reshape(depth, GROUP, sizes.attn)
-    query, base = sizes.query, sizes.query + 2 * HD
+    parts = grad_attn.reshape(depth, layout.seq, sizes.attn_joined(layout))
+    wide, narrow = layout.share * sizes.query, sizes.kv_columns(layout)
 
     def flat(columns):
         return columns.astype(jnp.float32).reshape(depth, -1)
 
-    def shared(columns):
-        pairs = columns.astype(jnp.float32).reshape(depth, KVH, sizes.kv_share, HD)
-        return jnp.sum(pairs, axis=2).reshape(depth, -1)
+    def heads(columns):
+        columns = columns.astype(jnp.float32)
+        if layout.seq * narrow > KVH * HD:
+            columns = jnp.sum(columns.reshape(depth, KVH, -1, HD), axis=2)
+        return columns.reshape(depth, -1)
 
     return (
         mixed[None],
         grad_tokens[None],
         gain_sum[0],
-        flat(parts[:, :, :query]),
-        shared(parts[:, :, query : query + HD]),
-        shared(parts[:, :, query + HD : base]),
-        flat(parts[:, :, base:]),
+        flat(parts[:, :, :wide]),
+        heads(parts[:, :, 2 * wide : 2 * wide + narrow]),
+        heads(parts[:, :, 2 * wide + narrow :]),
+        flat(parts[:, :, wide : 2 * wide]),
         gain_sum[1],
         flat(grad_gate),
         flat(grad_up),

time: 737 us -> 612 us (0.83)
  the two profiles are of different devices: /device:TPU:15 before, /device:TPU:0 now
where the time goes in v4:
time: 612 us; the launch traced here: 602 us
  Pallas kernels  570 us (93%)
  local copies, waits for them, and re-layouts  16.5 us (3%)
  other arithmetic  14.7 us (2%)
    pallas_call x1, Pallas kernels, back(): pl.pallas_call(functools.partial(back_kernel, layout, sizes), out_shape=[...  318 us
    pallas_call x1, Pallas kernels, front(): pl.pallas_call(functools.partial(front_kernel, layout, sizes), out_shape=...  252 us
    convert_element_type x3, other arithmetic, flat(): return columns.astype(jnp.float32).reshape(depth, -1)  13.1 us

profile of v4, /device:TPU:0, one launch (start us, length us, event | category | flops | bytes accessed | tf_op | source)
XLA Modules:
  0.0 602.5 jit_solution(9133246180720421124)
XLA Ops:
  0.6 0.7 broadcast_in_dim.27
  1.3 0.7 broadcast_in_dim.28
  2.0 0.6 pad_maximum_fusion.gains_ref
  2.6 1.3 broadcast_in_dim.26.ids_ref
  3.9 252.5 %front.1 = (bf16[2048,2048]{1,0:T(8,128)(2,1)}, bf16[2048,2048]{1,0:T(8,128)(2,1)}, bf16[2048,2048]{1,0:T(8,128)(2,1)}, bf16[2048,1024]{1,0:T(8,128)(2,1)}, bf16...) custom-call(bf16[128,2048]{1,0:T(8,128)(2,1)} %bitcast.19, ...), custom_call_target="tpu_custom_call" | custom-call | tf_op jit(solution)/shard_map/front/pallas_call | solution.py:670
  256.3 317.9 %back.1 = (bf16[128,2048]{1,0:T(8,128)(2,1)}, bf16[128,2048]{1,0:T(8,128)(2,1)}, f32[8,256]{1,0:T(8,128)}, bf16[256,8192]{1,0:T(8,128)(2,1)}, bf16[256,8192]{1,0...) custom-call(bf16[128,2048]{1,0:T(8,128)(2,1)} %bitcast.20, ...), custom_call_target="tpu_custom_call" | custom-call | tf_op jit(solution)/shard_map/back/pallas_call | solution.py:1213
  574.2 1.3 fusion
  575.5 4.8 reshape.51
  580.4 0.1 slice_convert_fusion.2
  580.5 1.0 copy_bitcast_fusion
  581.6 0.8 slice_convert_fusion
  582.4 2.2 copy.26
  584.6 0.0 copy-start.2
  584.6 2.2 copy.23
  586.8 0.7 copy-done.2
  587.5 0.0 copy-start.1
  587.5 4.4 convert_element_type.6
  591.9 0.0 copy-done.1
  591.9 0.0 copy-start
  591.9 4.4 convert_element_type.14
  596.3 0.0 copy-done
  596.3 0.0 copy-start.4
  596.3 0.0 copy-start.3
  596.3 4.4 convert_element_type.15
  600.7 0.0 copy-done.4
  600.7 0.8 copy.31
  601.5 0.0 copy-done.3
  601.5 0.8 copy.32
Async XLA Ops:
  584.6 2.9 copy-start.2
  587.5 4.4 copy-start.1
  591.9 4.4 copy-start
  596.3 4.4 copy-start.4
  596.3 5.2 copy-start.3

commit v5 on v4

--- a/solution.py
+++ b/solution.py
@@ -12,18 +12,28 @@
 HD = 64
 EPSILON = 1e-05
 RESIDUAL = 0.22
-GROUP = 16
+MLP_GROUP = 16
+ATTN_GROUP = 8
 MESH = pl.DeviceIdType.MESH
-FIRST_PLAN = ((0, 48, (3, 2, 1)), (48, 48, (3, 1, 2)), (96, 32, (3, 2, 1)))
-COTANGENT_PLAN = ((0, 48, (3, 2, 1)), (48, 48, (3, 1, 2)), (96, 32, (3, 2, 1)))
-BRANCH_PLAN = ((0, 48, (1, 2, 3)), (48, 48, (2, 1, 3)), (96, 32, (1, 2, 3)))
-SECOND_PLAN = ((0, 48, (3, 2, 1)), (48, 48, (3, 1, 2)), (96, 32, (3, 2, 1)))
-HIDDEN_PLAN = ((0, 48, (1, 2, 3)), (48, 48, (2, 1, 3)), (96, 32, (1, 2, 3)))
-MIDDLE_PLAN = ((0, 48, (3, 2, 1)), (48, 48, (3, 1, 2)), (96, 32, (3, 2, 1)))
-DOWN_PLAN = ((0, 48, (1, 2, 3)), (48, 48, (2, 3, 1)), (96, 32, (3, 1, 2)))
-LAST_PLAN = ((0, 48, (1, 2, 3)), (48, 48, (2, 3, 1)), (96, 32, (3, 1, 2)))
-PLAN_PIECES = 4
-PAIRS = (7, 6, 5, 3, 4, 2, 1, 0)
+EVEN = ((0, 64), (64, 64))
+THIRDS = ((0, 48), (48, 48), (96, 32))
+
+
+def plan_of(pieces, orders):
+    return tuple((start, size, order) for (start, size), order in zip(pieces, orders))
+
+
+MLP_GATHER = plan_of(THIRDS, ((3, 2, 1), (3, 1, 2), (3, 2, 1)))
+MLP_SCATTER = plan_of(THIRDS, ((1, 2, 3), (2, 1, 3), (1, 2, 3)))
+
+
+def attn_plan(group):
+    if group.bits == 3:
+        return plan_of(EVEN, ((1, 2), (2, 1)))
+    return plan_of(THIRDS, ((1, 2, 3), (2, 3, 1), (3, 1, 2)))
+
+
+PLAN_PIECES = 3
 
 
 def dot(left, right):
@@ -52,28 +62,39 @@
     return factor * weighted - values * (factor * factor * factor) * centre
 
 
+class Group:
+    def __init__(self, seq, share):
+        self.seq = seq
+        self.share = share
+        self.count = seq * share
+        self.bits = self.count.bit_length() - 1
+
+    def member(self):
+        return lax.axis_index("seq") + self.seq * (lax.axis_index("fsdp") % self.share)
+
+    def partner(self, bit):
+        mask = 1 << bit
+        return offset(mask % self.seq, mask // self.seq)
+
+
 class Layout:
     def __init__(self, seq_count, fsdp_count):
         self.seq = seq_count
         self.fsdp = fsdp_count
-        self.share = GROUP // seq_count
         self.seq_bits = seq_count.bit_length() - 1
-
-    def member(self):
-        return lax.axis_index("seq") + self.seq * (lax.axis_index("fsdp") % self.share)
-
-    def offset(self, low, high):
-        return {
-            "seq": jnp.bitwise_xor(lax.axis_index("seq"), low),
-            "fsdp": jnp.bitwise_xor(lax.axis_index("fsdp"), high),
-        }
-
-    def device(self, mask):
-        return self.offset(mask % self.seq, mask // self.seq)
-
-
-def span_mask(dims):
-    return sum(1 << d for d in dims)
+        self.mlp = Group(seq_count, max(1, MLP_GROUP // seq_count))
+        self.attn = Group(seq_count, max(1, ATTN_GROUP // seq_count))
+
+
+def offset(low, high):
+    return {
+        "seq": jnp.bitwise_xor(lax.axis_index("seq"), low),
+        "fsdp": jnp.bitwise_xor(lax.axis_index("fsdp"), high),
+    }
+
+
+def place_of(order, index):
+    return sum(1 << bit for position, bit in enumerate(order) if index >> position & 1)
 
 
 def softmax(query, keys, query_ids, key_ids):
@@ -93,15 +114,16 @@
     barrier = pltpu.get_barrier_semaphore()
     for low, high in pairs:
         pl.semaphore_signal(
-            barrier, inc=1, device_id=layout.offset(low, high), device_id_type=MESH
+            barrier, inc=1, device_id=offset(low, high), device_id_type=MESH
         )
     pl.semaphore_wait(barrier, len(pairs))
 
 
-def gather_steps(layout, rows, plan, own_ref, dst_ref, sems):
+def gather_steps(group, rows, plan, own_ref, dst_ref, sems):
     send, recv, relay_recv, own_sem = sems
-    me = layout.member()
-    sent, relayed = [], []
+    me = group.member()
+    depth = group.bits - 1
+    pushed, relayed = {}, []
 
     def place(mask, piece):
         start, size, _ = plan[piece]
@@ -112,77 +134,50 @@
         start, size, _ = plan[piece]
         return own_ref.at[pl.ds(start, size)] if mask == 0 else place(mask, piece)
 
-    def push(mask, piece, slot, dim):
+    def copy_to(mask, piece, recv_sem, bit):
         copy = pltpu.make_async_remote_copy(
             src_ref=source(mask, piece),
             dst_ref=place(mask, piece),
             send_sem=send,
-            recv_sem=recv.at[piece, slot],
-            device_id=layout.device(1 << dim),
+            recv_sem=recv_sem,
+            device_id=group.partner(bit),
             device_id_type=MESH,
         )
         copy.start()
-        sent.append(copy)
         return copy
 
-    def relay(mask, piece, slot):
-        copy = pltpu.make_async_remote_copy(
-            src_ref=source(mask, piece),
-            dst_ref=place(mask, piece),
-            send_sem=send,
-            recv_sem=relay_recv.at[piece, slot],
-            device_id=layout.device(1),
-            device_id_type=MESH,
-        )
-        copy.start()
-        relayed.append(copy)
-
-    first, second, third = {}, {}, {}
-    for piece, (_, _, (a, b, c)) in enumerate(plan):
-        first[piece] = push(0, piece, 0, a)
-    for piece, (_, _, (a, b, c)) in enumerate(plan):
-        second[piece] = [push(0, piece, 1, b)]
-    for piece, (_, _, (a, b, c)) in enumerate(plan):
-        third[piece] = [push(0, piece, 3, c)]
+    def forward(index, piece):
+        order = plan[piece][2]
+        mask = place_of(order, index)
+        for position in range(index.bit_length(), depth):
+            number = index | 1 << position
+            pushed[piece, number] = copy_to(
+                mask, piece, recv.at[piece, number], order[position]
+            )
+        relayed.append(copy_to(mask, piece, relay_recv.at[piece, index], 0))
+
+    for piece in range(len(plan)):
+        forward(0, piece)
     local = pltpu.make_async_copy(own_ref, dst_ref.at[rows_at(me * rows, rows)], own_sem)
     local.start()
-    for piece in range(len(plan)):
-        relay(0, piece, 0)
     yield
-    for piece, (_, _, (a, b, c)) in enumerate(plan):
-        first[piece].wait_recv()
-        mask = span_mask((a,))
-        second[piece].append(push(mask, piece, 2, b))
-        third[piece].append(push(mask, piece, 4, c))
-        relay(mask, piece, 1)
-    yield
-    for piece, (_, _, (a, b, c)) in enumerate(plan):
-        second[piece][0].wait_recv()
-        mask = span_mask((b,))
-        third[piece].append(push(mask, piece, 5, c))
-        relay(mask, piece, 2)
-    yield
-    for piece, (_, _, (a, b, c)) in enumerate(plan):
-        second[piece][1].wait_recv()
-        mask = span_mask((a, b))
-        third[piece].append(push(mask, piece, 6, c))
-        relay(mask, piece, 3)
-    yield
-    for turn, dims in enumerate(((2,), (0, 2), (1, 2), (0, 1, 2))):
-        for piece, (_, _, order) in enumerate(plan):
-            third[piece][turn].wait_recv()
-            relay(span_mask([order[d] for d in dims]), piece, 4 + turn)
+    for index in range(1, 1 << depth):
+        for piece in range(len(plan)):
+            pushed[piece, index].wait_recv()
+            forward(index, piece)
+        if index < 4:
+            yield
     yield
     for copy in relayed:
         copy.wait_recv()
     local.wait()
-    whole = dst_ref.at[pl.ds(0, 15 * rows)]
+    whole = dst_ref.at[pl.ds(0, (group.count - 1) * rows)]
     pltpu.make_async_remote_copy(
         src_ref=whole,
         dst_ref=whole,
         send_sem=send,
         recv_sem=recv.at[0, 0],
-        device_id=layout.device(1),
+        device_id=group.partner(0),
         device_id_type=MESH,
     ).wait_send()
     yield
@@ -192,7 +187,7 @@
     count = PLAN_PIECES
     return [
         pltpu.SemaphoreType.DMA,
-        pltpu.SemaphoreType.DMA((count, 7)),
+        pltpu.SemaphoreType.DMA((count, 8)),
         pltpu.SemaphoreType.DMA((count, 8)),
         pltpu.SemaphoreType.DMA,
     ]
@@ -203,35 +198,46 @@
         pass
 
 
-def scatter_steps(layout, rows, plan, produce, total, buffers, tail, sems):
+def scatter_steps(group, rows, plan, produce, total, buffers, tail, sems):
     stage, core_in, arrive = buffers
     last_out, last_in = tail
     core_send, core_recv, send, recv, last_send, last_recv = sems
-    me = layout.member()
+    me = group.member()
     core = me % 2
     own = pl.multiple_of(core * rows, 16)
     other = pl.multiple_of((1 - core) * rows, 16)
-    copies = {}
+    depth = group.bits - 1
+    top = 1 << depth
+    copies, pushed = {}, {}
 
     def chunked(start, size, body):
         @pl.loop(0, size // 16)
         def _(i):
             body(pl.multiple_of(i * 16 + start, 16))
 
-    def push(piece, pair, dim, slot):
-        start, size, _ = plan[piece]
+    def slot(position, index):
+        return top - (top >> position) + (index >> position + 1)
+
+    def push(piece, position, index):
+        start, size, order = plan[piece]
+        rest = index ^ 1 << position
+        number = slot(position, rest)
         copy = pltpu.make_async_remote_copy(
-            src_ref=stage.at[pair, rows_at(own + start, size)],
-            dst_ref=arrive.at[slot, pl.ds(start, size)],
-            send_sem=send.at[piece, slot],
-            recv_sem=recv.at[piece, slot],
-            device_id=layout.device(1 << dim),
+            src_ref=stage.at[place_of(order, index) // 2, rows_at(own + start, size)],
+            dst_ref=arrive.at[number, pl.ds(start, size)],
+            send_sem=send.at[piece, number],
+            recv_sem=recv.at[piece, number],
+            device_id=group.partner(order[position]),
             device_id_type=MESH,
         )
         copy.start()
-        return copy
-
-    one, two, three = {}, {}, {}
+        pushed[piece, position, rest] = copy
+
+    def summed(pair, r, slots):
+        value = stage[pair, rows_at(own + r, 16)].astype(jnp.float32)
+        for number in slots:
+            value = value + arrive[number, rows_at(r, 16)].astype(jnp.float32)
+        return value
 
     def settle(pair):
         copies[pair].wait_recv()
@@ -243,21 +249,20 @@
             ).astype(jnp.bfloat16)
 
         chunked(0, rows, body)
-        mask = pair * 2
-        for piece, (_, _, (a, b, c)) in enumerate(plan):
-            if mask & (1 << a):
-                slot = (1 if mask & (1 << b) else 0) + (2 if mask & (1 << c) else 0)
-                one[piece, slot] = push(piece, pair, a, slot)
+        for piece, (_, _, order) in enumerate(plan):
+            for index in range(1, top, 2):
+                if place_of(order, index) == 2 * pair:
+                    push(piece, 0, index)
 
     before = None
-    for pair in PAIRS:
+    for pair in sorted(range(top), key=lambda pair: (-pair.bit_count(), -pair)):
         produce(jnp.bitwise_xor(me // 2, pair), stage.at[pair])
         copies[pair] = pltpu.make_async_remote_copy(
             src_ref=stage.at[pair, rows_at(other, rows)],
             dst_ref=core_in.at[pair],
             send_sem=core_send.at[pair],
             recv_sem=core_recv.at[pair],
-            device_id=layout.device(1),
+            device_id=group.partner(0),
             device_id_type=MESH,
         )
         copies[pair].start()
@@ -266,69 +271,61 @@
         before = pair
     settle(before)
     yield
-
-    def keep(piece, pair, slots):
-        start, size, _ = plan[piece]
-
-        def body(r):
-            value = stage[pair, rows_at(own + r, 16)].astype(jnp.float32)
-            for slot in slots:
-                value = value + arrive[slot, rows_at(r, 16)].astype(jnp.float32)
-            stage[pair, rows_at(own + r, 16)] = value.astype(jnp.bfloat16)
-
-        chunked(start, size, body)
-
-    for piece, (_, _, (a, b, c)) in enumerate(plan):
-        for slot, dims in ((3, (b, c)), (1, (b,))):
-            pair = span_mask(dims) // 2
-            one[piece, slot].wait_recv()
-            keep(piece, pair, (slot,))
-            two[piece, slot] = push(piece, pair, b, 4 + slot // 2)
-    yield
-    for piece, (start, size, (a, b, c)) in enumerate(plan):
-        pair = span_mask((c,)) // 2
-        one[piece, 2].wait_recv()
-        two[piece, 3].wait_recv()
-
-        def onward(r):
-            value = stage[pair, rows_at(own + r, 16)].astype(jnp.float32)
-            for slot in (2, 5):
-                value = value + arrive[slot, rows_at(r, 16)].astype(jnp.float32)
-            last_out[rows_at(r, 16)] = value.astype(jnp.bfloat16)
-
-        chunked(start, size, onward)
-        three[piece] = pltpu.make_async_remote_copy(
-            src_ref=last_out.at[pl.ds(start, size)],
-            dst_ref=last_in.at[pl.ds(start, size)],
-            send_sem=last_send.at[piece],
-            recv_sem=last_recv.at[piece],
-            device_id=layout.device(1 << c),
-            device_id_type=MESH,
-        )
-        three[piece].start()
-    for piece, (start, size, (a, b, c)) in enumerate(plan):
-        one[piece, 0].wait_recv()
-        two[piece, 1].wait_recv()
+    final = {}
+    for position in range(1, depth):
+        for index in reversed(range(1 << position, top, 2 << position)):
+            for piece, (start, size, order) in enumerate(plan):
+                pair = place_of(order, index) // 2
+                slots = [slot(p, index) for p in range(position)]
+                for p in range(position):
+                    pushed[piece, p, index].wait_recv()
+                if position < depth - 1:
+
+                    def keep(r):
+                        stage[pair, rows_at(own + r, 16)] = summed(pair, r, slots).astype(
+                            jnp.bfloat16
+                        )
+
+                    chunked(start, size, keep)
+                    push(piece, position, index)
+                else:
+
+                    def onward(r):
+                        last_out[rows_at(r, 16)] = summed(pair, r, slots).astype(jnp.bfloat16)
+
+                    chunked(start, size, onward)
+                    final[piece] = pltpu.make_async_remote_copy(
+                        src_ref=last_out.at[pl.ds(start, size)],
+                        dst_ref=last_in.at[pl.ds(start, size)],
+                        send_sem=last_send.at[piece],
+                        recv_sem=last_recv.at[piece],
+                        device_id=group.partner(order[position]),
+                        device_id_type=MESH,
+                    )
+                    final[piece].start()
+        if position < depth - 1:
+            yield
+    slots = [slot(p, 0) for p in range(depth - 1)]
+    for piece, (start, size, _) in enumerate(plan):
+        for p in range(depth - 1):
+            pushed[piece, p, 0].wait_recv()
 
         def gathered(r):
-            value = stage[0, rows_at(own + r, 16)].astype(jnp.float32)
-            for slot in (0, 4):
-                value = value + arrive[slot, rows_at(r, 16)].astype(jnp.float32)
-            total[rows_at(r, 16)] = value
+            total[rows_at(r, 16)] = summed(0, r, slots)
 
         chunked(start, size, gathered)
-    for group in (copies, one, two):
-        for copy in group.values():
+    for some in (copies, pushed):
+        for copy in some.values():
             copy.wait_send()
     yield
     for piece, (start, size, _) in enumerate(plan):
-        three[piece].wait_recv()
+        final[piece].wait_recv()
 
         def finished(r):
             total[rows_at(r, 16)] += last_in[rows_at(r, 16)].astype(jnp.float32)
 
         chunked(start, size, finished)
-    for copy in three.values():
+    for copy in final.values():
         copy.wait_send()
     yield
 
@@ -366,23 +363,20 @@
         self.rows, self.width = tokens.shape[1], tokens.shape[2]
         self.length = block_ids.shape[1]
         self.depth = w_query.shape[0]
-        self.hidden = w_gate.shape[1] // GROUP
-        self.heads = H // GROUP
+        self.hidden = w_gate.shape[1] // layout.mlp.count
+        self.heads = H // layout.attn.count
         self.query = self.heads * HD
         self.attn = 2 * self.query + 2 * HD
-        self.all_rows = GROUP * self.rows
-        self.span = max(128, min(self.length, 512 * 512 // self.length))
-        self.kv_share = GROUP // KVH
-
-    def kv_columns(self, layout):
-        return max(1, layout.share // self.kv_share) * HD
-
-    def attn_joined(self, layout):
-        return 2 * layout.share * self.query + 2 * self.kv_columns(layout)
-
-
-def kv_half(layout, target, chunk):
-    second = (target // (GROUP // KVH)) % 2 == 1
+        self.mlp_rows = layout.mlp.count * self.rows
+        self.attn_rows = layout.attn.count * self.rows
+        self.span = max(128, min(self.length, 256 * 512 // self.length))
+        self.kv_share = max(1, layout.attn.count // KVH)
+        self.kv_columns = max(1, layout.attn.share // self.kv_share) * HD
+        self.attn_joined = 2 * layout.attn.share * self.query + 2 * self.kv_columns
+
+
+def kv_half(sizes, target, chunk):
+    second = (target // sizes.kv_share) % 2 == 1
     return jnp.where(second, chunk[:, HD:], chunk[:, :HD])
 
 
@@ -464,7 +458,8 @@
     mlp_recv,
     load_sem,
 ):
-    share, fsdp, depth = layout.share, layout.fsdp, sizes.depth
+    share, fsdp, depth = layout.attn.share, layout.fsdp, sizes.depth
+    mlp_share = layout.mlp.share
     seq_me, fsdp_me = lax.axis_index("seq"), lax.axis_index("fsdp")
     query = sizes.query
     rows, hidden = sizes.rows, sizes.hidden
@@ -497,7 +492,7 @@
             dst_ref=gains.at[:, own_rows],
             send_sem=gain_send.at[mask],
             recv_sem=gain_recv.at[mask],
-            device_id=layout.offset(0, mask),
+            device_id=offset(0, mask),
             device_id_type=MESH,
         )
         copy.start()
@@ -509,8 +504,8 @@
         pack[j] = jnp.concatenate(
             [
                 wq[:, j * query : (j + 1) * query],
-                kv_half(layout, target, wk[...]),
-                kv_half(layout, target, wv[...]),
+                kv_half(sizes, target, wk[...]),
+                kv_half(sizes, target, wv[...]),
                 wo[:, j * query : (j + 1) * query],
             ],
             axis=1,
@@ -522,7 +517,7 @@
             dst_ref=wa.at[own_rows],
             send_sem=attn_send.at[mask],
             recv_sem=attn_recv.at[mask],
-            device_id=layout.offset(0, mask),
+            device_id=offset(0, mask),
             device_id_type=MESH,
         )
         copy.start()
@@ -537,7 +532,7 @@
         h2[r] = (values * rms_factor(values) * gain_one).astype(jnp.bfloat16)
 
     loop_rows(rows, 32, norm)
-    x_steps = gather_steps(layout, rows, FIRST_PLAN, h2, x_all, (x_send, x_recv, x_relay, x_own))
+    x_steps = gather_steps(layout.attn, rows, attn_plan(layout.attn), h2, x_all, (x_send, x_recv, x_relay, x_own))
     next(x_steps)
     id_copies = []
     for mask in range(1, share):
@@ -546,13 +541,13 @@
             dst_ref=ids.at[fsdp_me % share],
             send_sem=id_send.at[mask],
             recv_sem=id_recv.at[mask],
-            device_id=layout.offset(0, mask),
+            device_id=offset(0, mask),
             device_id_type=MESH,
         )
         copy.start()
         id_copies.append(copy)
     g_steps = gather_steps(
-        layout, rows, COTANGENT_PLAN, cot_ref, g_out, (g_send, g_recv, g_relay, g_own)
+        layout.mlp, rows, MLP_GATHER, cot_ref, g_out, (g_send, g_recv, g_relay, g_own)
     )
     next(g_steps)
     next(x_steps)
@@ -561,21 +556,21 @@
 
     def send_mlp(ref, out, place, index):
         def at(j):
-            return columns(ref, (seq_me * share + j) * hidden, hidden)
+            return columns(ref, (seq_me * mlp_share + j) * hidden, hidden)
 
         home = out.at[own_rows, pl.ds(place, hidden)]
         for mask in reversed(range(1, fsdp)):
             copy = pltpu.make_async_remote_copy(
-                src_ref=at(jnp.bitwise_xor(fsdp_me, mask) % share),
+                src_ref=at(jnp.bitwise_xor(fsdp_me, mask) % mlp_share),
                 dst_ref=home,
                 send_sem=mlp_send.at[index, mask],
                 recv_sem=mlp_recv.at[index, mask],
-                device_id=layout.offset(0, mask),
+                device_id=offset(0, mask),
                 device_id_type=MESH,
             )
             copy.start()
             mlp.append(copy)
-        copy = pltpu.make_async_copy(at(fsdp_me % share), home, load_sem.at[1 + index])
+        copy = pltpu.make_async_copy(at(fsdp_me % mlp_share), home, load_sem.at[1 + index])
         copy.start()
         mlp.append(copy)
 
@@ -591,7 +586,7 @@
     def project(r):
         qkv[r] = dot(x_all[r], wa[:, : query + 2 * HD]).astype(jnp.bfloat16)
 
-    loop_rows(sizes.all_rows, 256, project)
+    loop_rows(sizes.attn_rows, 256, project)
     next(g_steps)
     for copy in id_copies:
         copy.wait()
@@ -621,7 +616,7 @@
     next(g_steps)
     next(g_steps)
     steps = scatter_steps(
-        layout, rows, BRANCH_PLAN, out_rows, middle, (stage, core_in, arrive),
+        layout.attn, rows, attn_plan(layout.attn), out_rows, middle, (stage, core_in, arrive),
         (last_out, last_in), (core_send, core_recv, s_send, s_recv, last_send, last_recv),
     )
     next(steps)
@@ -636,7 +631,7 @@
 
     loop_rows(rows, 32, second)
     h_steps = gather_steps(
-        layout, rows, SECOND_PLAN, h2, h2_out, (h_send, h_recv, h_relay, h_own)
+        layout.mlp, rows, MLP_GATHER, h2, h2_out, (h_send, h_recv, h_relay, h_own)
     )
     next(h_steps)
     next(h_steps)
@@ -649,19 +644,19 @@
 
 
 def front(layout, sizes, *args):
-    width, count = sizes.width, sizes.all_rows
+    width, count, few = sizes.width, sizes.mlp_rows, sizes.attn_rows
     hbm, vmem = pl.BlockSpec(memory_space=pl.ANY), pl.BlockSpec(memory_space=pltpu.VMEM)
-    share, depth, fsdp = layout.share, sizes.depth, layout.fsdp
+    share, depth, fsdp = layout.attn.share, sizes.depth, layout.fsdp
     bf16 = jnp.bfloat16
     shapes = [
-        ((count, width), bf16, hbm),
+        ((few, width), bf16, hbm),
         ((count, width), bf16, hbm),
         ((count, width), bf16, hbm),
         ((width, 2 * sizes.hidden), bf16, hbm),
         ((width, sizes.hidden), bf16, hbm),
         ((width, sizes.attn), bf16, vmem),
-        ((count, sizes.query + 2 * HD), bf16, vmem),
-        ((count, sizes.query), bf16, vmem),
+        ((few, sizes.query + 2 * HD), bf16, vmem),
+        ((few, sizes.query), bf16, vmem),
         ((sizes.rows, width), jnp.float32, vmem),
         ((16, width), bf16, vmem),
         ((share, 8, sizes.length), jnp.int32, vmem),
@@ -673,7 +668,7 @@
         in_specs=[hbm] * len(args),
         out_specs=[spec for _, _, spec in shapes],
         scratch_shapes=[
-            pltpu.VMEM((count, width), bf16),
+            pltpu.VMEM((few, width), bf16),
             pltpu.VMEM((sizes.rows, width), bf16),
             pltpu.VMEM((sizes.rows, width), bf16),
             pltpu.VMEM((depth, share * sizes.query), bf16),
@@ -711,7 +706,7 @@
             dst_ref=block(mask),
             send_sem=send.at[mask ^ bit],
             recv_sem=recv.at[mask ^ bit],
-            device_id=layout.offset(bit, 0),
+            device_id=offset(bit, 0),
             device_id_type=MESH,
         )
         copy.start()
@@ -818,11 +813,25 @@
     load_sem,
     pick_sem,
 ):
-    share, fsdp, depth = layout.share, layout.fsdp, sizes.depth
+    fsdp, depth = layout.fsdp, sizes.depth
     seq_me, fsdp_me = lax.axis_index("seq"), lax.axis_index("fsdp")
     query, hidden, rows = sizes.query, sizes.hidden, sizes.rows
     base = query + 2 * HD
-    count = sizes.all_rows
+    count, few = sizes.mlp_rows, sizes.attn_rows
+    near = pl.ds(0, few)
+    spare = few < count
+
+    def piece_at(ref, mask):
+        column = pl.ds(mask // 4 * sizes.attn, sizes.attn)
+        return ref.at[pl.ds(mask % 4 * depth, depth), column]
+
+    def staged(mask):
+        if spare:
+            return piece_at(h_all.at[pl.ds(few, few)], mask)
+        return w_down.at[block(mask), pl.ds(0, sizes.attn)]
+
+    if spare:
+        own_sum = g_all.at[pl.ds(few, depth)]
     scatter = (stage, core_in, arrive)
     sems = (core_send, core_recv, s_send, s_recv)
     scatter_sem = sems + (last_send, last_recv)
@@ -879,7 +888,7 @@
             dst_ref=dst.at[mask],
             send_sem=grad_send.at[index, mask],
             recv_sem=grad_recv.at[index, mask],
-            device_id=layout.offset(0, mask),
+            device_id=offset(0, mask),
             device_id_type=MESH,
         )
         copy.start()
@@ -905,7 +914,7 @@
             piece = pl.ds(pl.multiple_of(i * 512, 512), 512)
             ref[:, piece] = dot_cols(left, w_in[piece]).astype(jnp.bfloat16)
 
-    steps = scatter_steps(layout, rows, HIDDEN_PLAN, hidden_back, total, scatter, (last_out, last_in), scatter_sem)
+    steps = scatter_steps(layout.mlp, rows, MLP_SCATTER, hidden_back, total, scatter, (last_out, last_in), scatter_sem)
     next(steps)
 
     def grad_up(mask):
@@ -918,7 +927,7 @@
             grad_up(mask)
         next(steps)
     finish(steps)
-    h1_copy = pltpu.make_async_copy(h1_ref, h_all, load_sem.at[len(loads)])
+    h1_copy = pltpu.make_async_copy(h1_ref, h_all.at[near], load_sem.at[len(loads)])
     h1_copy.start()
     for name in ("mid", "tok", "cot", "gains", "wa", "qkv", "att", "ids"):
         loads[name].wait()
@@ -936,7 +945,7 @@
 
     loop_rows(rows, 32, norm_two)
     a_steps = gather_steps(
-        layout, rows, MIDDLE_PLAN, last_out, g_all, (a_send, a_recv, a_relay, a_own)
+        layout.attn, rows, attn_plan(layout.attn), last_out, g_all.at[near], (a_send, a_recv, a_relay, a_own)
     )
     next(a_steps)
     next(a_steps)
@@ -955,20 +964,19 @@
             ref[:, piece] = dot_cols(left, w_down[piece]).astype(jnp.bfloat16)
 
     steps_low = scatter_steps(
-        layout, rows, DOWN_PLAN, down_rows, down_total, scatter, (down_last_out, down_last_in),
+        layout.mlp, rows, MLP_SCATTER, down_rows, down_total, scatter, (down_last_out, down_last_in),
         sems + (down_last_send, down_last_recv),
     )
     next(steps_low)
 
-    mine = fsdp_me % share
-
-    def collect(index, src, width, own_piece, landing, combine, out, out_width):
+
+    def collect(index, share, src, width, own_piece, landing, combine, out, out_width):
         picks = []
         for number, mask, copy in sends:
             if number == index:
                 copy.wait_recv()
                 pick = pltpu.make_async_copy(
-                    src.at[mask], landing.at[block(mask)], pick_sem.at[index, mask]
+                    src.at[mask], landing(mask), pick_sem.at[index, mask]
                 )
                 pick.start()
                 picks.append(pick)
@@ -978,13 +986,13 @@
 
         def terms_of(low, start, size):
             cols = pl.ds(start, size)
-            value = own_piece[:, cols] if low == 0 else landing[block(low), cols]
+            value = own_piece[:, cols] if low == 0 else landing(low)[:, cols]
             value = value.astype(jnp.float32)
             for mask in range(low + share, fsdp, share):
-                value = value + landing[block(mask), cols].astype(jnp.float32)
+                value = value + landing(mask)[:, cols].astype(jnp.float32)
             return value
 
-        combine(terms_of, width)
+        combine(terms_of, share, width)
         home = pl.multiple_of(seq_me * out_width, 128)
         local = pltpu.make_async_copy(
             own_sum.at[:, pl.ds(0, out_width)], out.at[:, pl.ds(home, out_width)], own_sem.at[index]
@@ -993,19 +1001,21 @@
         local.wait()
         yield from seq_gather(layout, out, out_width, (join_send.at[index], join_recv.at[index]))
 
-    def place_columns(terms_of, width):
+    def place_columns(terms_of, share, width):
+        mine = fsdp_me % share
         for low in range(share):
             start = pl.multiple_of(jnp.bitwise_xor(mine, low) * width, 128)
             own_sum[:, pl.ds(start, width)] = terms_of(low, 0, width).astype(jnp.bfloat16)
 
-    def place_attn(terms_of, width):
+    def place_attn(terms_of, share, width):
+        mine = fsdp_me % share
         for low in range(share):
             for source, target in ((0, 0), (base, share * query)):
                 start = pl.multiple_of(target + jnp.bitwise_xor(mine, low) * query, 128)
                 own_sum[:, pl.ds(start, query)] = terms_of(low, source, query).astype(
                     jnp.bfloat16
                 )
-        both = sizes.kv_columns(layout)
+        both = sizes.kv_columns
         at = 2 * share * query
         for source in (query, query + HD):
             heads = []
@@ -1024,9 +1034,10 @@
             own_sum[:, at : at + both] = value.astype(jnp.bfloat16)
             at += both
 
-    joined = share * hidden
+    mlp_share, attn_share = layout.mlp.share, layout.attn.share
+    joined = mlp_share * hidden
     steps_down = collect(
-        0, down_recv, hidden, down_stage.at[block(0)], hid, place_columns, down_out, joined
+        0, mlp_share, down_recv, hidden, down_stage.at[block(0)], lambda mask: hid.at[block(mask)], place_columns, down_out, joined
     )
     next(steps_down)
 
@@ -1066,7 +1077,7 @@
                 jnp.bfloat16
             )
 
-    turns = share * blocks
+    turns = layout.attn.share * blocks
 
     @pl.loop(0, turns // 2)
     def _(i):
@@ -1080,13 +1091,13 @@
         attend_back_block(i)
 
     next(steps_low)
-    for bit in range(4):
+    for bit in range(layout.mlp.bits):
         pl.semaphore_signal(
-            credit, inc=1, device_id=layout.device(1 << bit), device_id_type=MESH
+            credit, inc=1, device_id=layout.mlp.partner(bit), device_id_type=MESH
         )
 
     next(steps_down)
-    pl.semaphore_wait(credit, 4)
+    pl.semaphore_wait(credit, layout.mlp.bits)
 
     def qkv_back(pair, ref):
         left = qkv[rows_at(pair * 2 * rows, 2 * rows)]
@@ -1100,20 +1111,20 @@
 
     def grad_attn(mask):
         cols = owner_columns(mask)
-        w_down[block(mask), :base] = dot_rows(h_all[:, cols], qkv[...]).astype(jnp.bfloat16)
-        w_down[block(mask), base : sizes.attn] = dot_rows(g_all[:, cols], attended[...]).astype(
+        staged(mask)[:, :base] = dot_rows(h_all[near, cols], qkv[...]).astype(jnp.bfloat16)
+        staged(mask)[:, base:] = dot_rows(g_all[near, cols], attended[...]).astype(
             jnp.bfloat16
         )
-        send_grad(mask, w_down.at[block(mask), pl.ds(0, sizes.attn)], attn_recv, 3)
+        send_grad(mask, staged(mask), attn_recv, 3)
 
     for mask in far[: fsdp // 2]:
         grad_attn(mask)
-    steps = scatter_steps(layout, rows, LAST_PLAN, qkv_back, total, scatter, (last_out, last_in), scatter_sem)
+    steps = scatter_steps(layout.attn, rows, attn_plan(layout.attn), qkv_back, total, scatter, (last_out, last_in), scatter_sem)
     next(steps)
     for mask in far[fsdp // 2 :]:
         grad_attn(mask)
     steps_gate = collect(
-        1, gate_recv, hidden, w_in.at[block(0), pl.ds(0, hidden)], grad_in.at[:, pl.ds(0, hidden)],
+        1, mlp_share, gate_recv, hidden, w_in.at[block(0), pl.ds(0, hidden)], lambda mask: grad_in.at[block(mask), pl.ds(0, hidden)],
         place_columns, gate_out, joined,
     )
     next(steps_gate)
@@ -1143,22 +1154,22 @@
             dst_ref=gain_in.at[mask],
             send_sem=gain_send.at[mask],
             recv_sem=gain_recv.at[mask],
-            device_id=layout.offset(0, mask),
+            device_id=offset(0, mask),
             device_id_type=MESH,
         )
         copy.start()
         gain_copies.append(copy)
 
     steps_up = collect(
-        2, up_recv, hidden, w_in.at[block(0), pl.ds(hidden, hidden)], grad_in.at[:, pl.ds(hidden, hidden)],
+        2, mlp_share, up_recv, hidden, w_in.at[block(0), pl.ds(hidden, hidden)], lambda mask: grad_in.at[block(mask), pl.ds(hidden, hidden)],
         place_columns, up_out, joined,
     )
     next(steps_up)
     next(steps_up)
     next(steps_gate)
     steps_attn = collect(
-        3, attn_recv, sizes.attn, w_down.at[block(0), pl.ds(0, sizes.attn)], h_all.at[:, pl.ds(0, sizes.attn)],
-        place_attn, attn_out, sizes.attn_joined(layout),
+        3, attn_share, attn_recv, sizes.attn, staged(0), functools.partial(piece_at, g_all),
+        place_attn, attn_out, sizes.attn_joined,
     )
     next(steps_attn)
     next(steps_attn)
@@ -1176,7 +1187,7 @@
             dst_ref=gain_seq.at[2 * bit + 1],
             send_sem=gs_send.at[bit],
             recv_sem=gs_recv.at[bit],
-            device_id=layout.offset(1 << bit, 0),
+            device_id=offset(1 << bit, 0),
             device_id_type=MESH,
         )
         copy.start()
@@ -1190,19 +1201,20 @@
 
 
 def back(layout, sizes, *args):
-    width, count = sizes.width, sizes.all_rows
+    width, count, few = sizes.width, sizes.mlp_rows, sizes.attn_rows
     hbm, vmem = pl.BlockSpec(memory_space=pl.ANY), pl.BlockSpec(memory_space=pltpu.VMEM)
-    share, depth, fsdp = layout.share, sizes.depth, layout.fsdp
+    share, depth, fsdp = layout.attn.share, sizes.depth, layout.fsdp
+    joined = layout.mlp.share * sizes.hidden
     rows, hidden, base = sizes.rows, sizes.hidden, sizes.query + 2 * HD
     bf16, f32 = jnp.bfloat16, jnp.float32
     shapes = [
         ((rows, width), bf16, vmem),
         ((rows, width), bf16, vmem),
         ((8, depth), f32, vmem),
-        ((depth, GROUP * hidden), bf16, hbm),
-        ((depth, GROUP * hidden), bf16, hbm),
-        ((depth, GROUP * hidden), bf16, hbm),
-        ((depth, layout.seq * sizes.attn_joined(layout)), bf16, hbm),
+        ((depth, layout.seq * joined), bf16, hbm),
+        ((depth, layout.seq * joined), bf16, hbm),
+        ((depth, layout.seq * joined), bf16, hbm),
+        ((depth, layout.seq * sizes.attn_joined), bf16, hbm),
         ((fsdp, depth, hidden), bf16, hbm),
         ((fsdp, depth, hidden), bf16, hbm),
         ((fsdp, depth, hidden), bf16, hbm),
@@ -1221,8 +1233,8 @@
             pltpu.VMEM((width, 2 * hidden), bf16),
             pltpu.VMEM((width, hidden), bf16),
             pltpu.VMEM((width, sizes.attn), bf16),
-            pltpu.VMEM((count, base), bf16),
-            pltpu.VMEM((count, sizes.query), bf16),
+            pltpu.VMEM((few, base), bf16),
+            pltpu.VMEM((few, sizes.query), bf16),
             pltpu.VMEM((count, hidden), bf16),
             pltpu.VMEM((count, 2 * hidden), bf16),
             pltpu.VMEM((rows, width), f32),
@@ -1236,7 +1248,7 @@
             pltpu.VMEM((8, width), f32),
             pltpu.VMEM((fsdp, 8, depth), f32),
             pltpu.VMEM((2 * layout.seq_bits, 8, depth), f32),
-            pltpu.VMEM((depth, share * max(hidden, 2 * sizes.query + 2 * HD)), bf16),
+            pltpu.VMEM((depth, max(joined, sizes.attn_joined) if few == count else 128), bf16),
         ]
         + scatter_scratch(rows, width)
         + [
@@ -1323,8 +1335,8 @@
         gains_all,
         ids_all,
     )
-    parts = grad_attn.reshape(depth, layout.seq, sizes.attn_joined(layout))
-    wide, narrow = layout.share * sizes.query, sizes.kv_columns(layout)
+    parts = grad_attn.reshape(depth, layout.seq, sizes.attn_joined)
+    wide, narrow = layout.attn.share * sizes.query, sizes.kv_columns
 
     def flat(columns):
         return columns.astype(jnp.float32).reshape(depth, -1)

time: 612 us -> 552 us (0.902)
  the two profiles are of different devices: /device:TPU:0 before, /device:TPU:15 now
where the time goes in v5:
time: 552 us; the launch traced here: 543 us
  Pallas kernels  511 us (93%)
  local copies, waits for them, and re-layouts  16.5 us (3%)
  other arithmetic  14.7 us (3%)
    pallas_call x1, Pallas kernels, back(): pl.pallas_call(functools.partial(back_kernel, layout, sizes), out_shape=[...  286 us
    pallas_call x1, Pallas kernels, front(): pl.pallas_call(functools.partial(front_kernel, layout, sizes), out_shape=...  225 us
    convert_element_type x3, other arithmetic, flat(): return columns.astype(jnp.float32).reshape(depth, -1)  13.1 us

profile of v5, /device:TPU:15, one launch (start us, length us, event | category | flops | bytes accessed | tf_op | source)
XLA Modules:
  0.0 543.4 jit_solution(15550722093818501077)
XLA Ops:
  0.6 0.7 broadcast_in_dim.27
  1.3 0.7 broadcast_in_dim.28
  2.0 0.6 pad_maximum_fusion.gains_ref
  2.6 1.3 broadcast_in_dim.26.ids_ref
  3.9 224.8 %front.1 = (bf16[1024,2048]{1,0:T(8,128)(2,1)}, bf16[2048,2048]{1,0:T(8,128)(2,1)}, bf16[2048,2048]{1,0:T(8,128)(2,1)}, bf16[2048,1024]{1,0:T(8,128)(2,1)}, bf16...) custom-call(bf16[128,2048]{1,0:T(8,128)(2,1)} %bitcast.19, ...), custom_call_target="tpu_custom_call" | custom-call | tf_op jit(solution)/shard_map/front/pallas_call | solution.py:665
  228.6 286.3 %back.1 = (bf16[128,2048]{1,0:T(8,128)(2,1)}, bf16[128,2048]{1,0:T(8,128)(2,1)}, f32[8,256]{1,0:T(8,128)}, bf16[256,8192]{1,0:T(8,128)(2,1)}, bf16[256,8192]{1,0...) custom-call(bf16[128,2048]{1,0:T(8,128)(2,1)} %bitcast.20, ...), custom_call_target="tpu_custom_call" | custom-call | tf_op jit(solution)/shard_map/back/pallas_call | solution.py:1225
  514.9 1.3 fusion
  516.2 4.8 reshape.51
  521.1 0.1 slice_convert_fusion.2
  521.2 1.0 copy_bitcast_fusion
  522.2 0.8 slice_convert_fusion
  523.1 2.2 copy.26
  525.3 0.0 copy-start.2
  525.3 2.2 copy.23
  527.5 0.7 copy-done.2
  528.2 0.0 copy-start.1
  528.2 4.4 convert_element_type.6
  532.6 0.0 copy-done.1
  532.6 0.0 copy-start
  532.6 4.4 convert_element_type.14
  537.0 0.0 copy-done
  537.0 0.0 copy-start.4
  537.0 0.0 copy-start.3
  537.0 4.4 convert_element_type.15
  541.3 0.0 copy-done.4
  541.3 0.8 copy.31
  542.1 0.0 copy-done.3
  542.1 0.8 copy.32
Async XLA Ops:
  525.3 2.9 copy-start.2
  528.2 4.4 copy-start.1
  532.6 4.4 copy-start
  537.0 4.4 copy-start.4
  537.0 5.2 copy-start.3

commit v6 on v5

--- a/solution.py
+++ b/solution.py
@@ -34,6 +34,7 @@
 
 
 PLAN_PIECES = 3
+FIRST_STAGES = 3
 
 
 def dot(left, right):
@@ -392,303 +393,6 @@
     return query, keys, values, softmax(query, keys, query_ids, key_ids)
 
 
-def front_kernel(
-    layout,
-    sizes,
-    tok_ref,
-    cot_ref,
-    ids_ref,
-    gains_ref,
-    wq_ref,
-    wk_ref,
-    wv_ref,
-    wo_ref,
-    wg_ref,
-    wu_ref,
-    wd_ref,
-    h1_out,
-    h2_out,
-    g_out,
-    in_out,
-    down_out,
-    wa,
-    qkv,
-    attended,
-    middle,
-    gains,
-    ids,
-    x_all,
-    tok,
-    h2,
-    wq,
-    wk,
-    wv,
-    wo,
-    pack,
-    stage,
-    core_in,
-    arrive,
-    last_out,
-    last_in,
-    x_send,
-    x_recv,
-    x_relay,
-    x_own,
-    h_send,
-    h_recv,
-    h_relay,
-    h_own,
-    g_send,
-    g_recv,
-    g_relay,
-    g_own,
-    core_send,
-    core_recv,
-    s_send,
-    s_recv,
-    last_send,
-    last_recv,
-    attn_send,
-    attn_recv,
-    gain_send,
-    gain_recv,
-    id_send,
-    id_recv,
-    mlp_send,
-    mlp_recv,
-    load_sem,
-):
-    share, fsdp, depth = layout.attn.share, layout.fsdp, sizes.depth
-    mlp_share = layout.mlp.share
-    seq_me, fsdp_me = lax.axis_index("seq"), lax.axis_index("fsdp")
-    query = sizes.query
-    rows, hidden = sizes.rows, sizes.hidden
-
-    loads = []
-
-    def load(src, dst):
-        copy = pltpu.make_async_copy(src, dst, load_sem.at[len(loads)])
-        copy.start()
-        loads.append(copy)
-        return copy
-
-    def columns(ref, start, size):
-        return ref.at[:, pl.ds(pl.multiple_of(start, 128), size)]
-
-    load(tok_ref, tok)
-    own_rows = pl.ds(pl.multiple_of(fsdp_me * depth, 128), depth)
-    load(gains_ref, gains.at[:, own_rows])
-    load(columns(wq_ref, seq_me * share * query, share * query), wq)
-    load(columns(wo_ref, seq_me * share * query, share * query), wo)
-    chunk = seq_me * share // (2 * sizes.kv_share) * 128
-    load(columns(wk_ref, chunk, 128), wk)
-    load(columns(wv_ref, chunk, 128), wv)
-    load(ids_ref, ids.at[fsdp_me % share])
-    greet_all(layout)
-    small = []
-    for mask in range(1, fsdp):
-        copy = pltpu.make_async_remote_copy(
-            src_ref=gains_ref,
-            dst_ref=gains.at[:, own_rows],
-            send_sem=gain_send.at[mask],
-            recv_sem=gain_recv.at[mask],
-            device_id=offset(0, mask),
-            device_id_type=MESH,
-        )
-        copy.start()
-        small.append(copy)
-    for copy in loads:
-        copy.wait()
-    for j in range(share):
-        target = seq_me * share + j
-        pack[j] = jnp.concatenate(
-            [
-                wq[:, j * query : (j + 1) * query],
-                kv_half(sizes, target, wk[...]),
-                kv_half(sizes, target, wv[...]),
-                wo[:, j * query : (j + 1) * query],
-            ],
-            axis=1,
-        )
-    attn = []
-    for mask in reversed(range(1, fsdp)):
-        copy = pltpu.make_async_remote_copy(
-            src_ref=pack.at[jnp.bitwise_xor(fsdp_me, mask) % share],
-            dst_ref=wa.at[own_rows],
-            send_sem=attn_send.at[mask],
-            recv_sem=attn_recv.at[mask],
-            device_id=offset(0, mask),
-            device_id_type=MESH,
-        )
-        copy.start()
-        attn.append(copy)
-    wa[own_rows] = pack[fsdp_me % share]
-    for copy in small:
-        copy.wait()
-    gain_one = gains[0:1].astype(jnp.float32)
-
-    def norm(r):
-        values = tok[r].astype(jnp.float32)
-        h2[r] = (values * rms_factor(values) * gain_one).astype(jnp.bfloat16)
-
-    loop_rows(rows, 32, norm)
-    x_steps = gather_steps(layout.attn, rows, attn_plan(layout.attn), h2, x_all, (x_send, x_recv, x_relay, x_own))
-    next(x_steps)
-    id_copies = []
-    for mask in range(1, share):
-        copy = pltpu.make_async_remote_copy(
-            src_ref=ids_ref,
-            dst_ref=ids.at[fsdp_me % share],
-            send_sem=id_send.at[mask],
-            recv_sem=id_recv.at[mask],
-            device_id=offset(0, mask),
-            device_id_type=MESH,
-        )
-        copy.start()
-        id_copies.append(copy)
-    g_steps = gather_steps(
-        layout.mlp, rows, MLP_GATHER, cot_ref, g_out, (g_send, g_recv, g_relay, g_own)
-    )
-    next(g_steps)
-    next(x_steps)
-
-    mlp = []
-
-    def send_mlp(ref, out, place, index):
-        def at(j):
-            return columns(ref, (seq_me * mlp_share + j) * hidden, hidden)
-
-        home = out.at[own_rows, pl.ds(place, hidden)]
-        for mask in reversed(range(1, fsdp)):
-            copy = pltpu.make_async_remote_copy(
-                src_ref=at(jnp.bitwise_xor(fsdp_me, mask) % mlp_share),
-                dst_ref=home,
-                send_sem=mlp_send.at[index, mask],
-                recv_sem=mlp_recv.at[index, mask],
-                device_id=offset(0, mask),
-                device_id_type=MESH,
-            )
-            copy.start()
-            mlp.append(copy)
-        copy = pltpu.make_async_copy(at(fsdp_me % mlp_share), home, load_sem.at[1 + index])
-        copy.start()
-        mlp.append(copy)
-
-    send_mlp(wg_ref, in_out, 0, 0)
-    send_mlp(wu_ref, in_out, hidden, 1)
-    finish(x_steps)
-    h1_copy = pltpu.make_async_copy(x_all, h1_out, load_sem.at[0])
-    h1_copy.start()
-    next(g_steps)
-    for copy in attn:
-        copy.wait()
-
-    def project(r):
-        qkv[r] = dot(x_all[r], wa[:, : query + 2 * HD]).astype(jnp.bfloat16)
-
-    loop_rows(sizes.attn_rows, 256, project)
-    next(g_steps)
-    for copy in id_copies:
-        copy.wait()
-
-    blocks = sizes.length // sizes.span
-
-    @pl.loop(0, share * blocks)
-    def _(i):
-        seq = i // blocks
-        start = pl.multiple_of((i % blocks) * sizes.span, sizes.span)
-        outs = []
-        for head in range(sizes.heads):
-            _, _, values, probs = attention_scores(sizes, qkv, ids, seq, start, head)
-            outs.append(dot(probs.astype(jnp.bfloat16), values))
-        attended[rows_at(seq * sizes.length + start, sizes.span)] = jnp.concatenate(
-            outs, axis=1
-        ).astype(jnp.bfloat16)
-
-    def out_rows(pair, ref):
-        block = attended[rows_at(pair * 2 * rows, 2 * rows)]
-
-        @pl.loop(0, sizes.width // 512)
-        def _(i):
-            piece = pl.ds(pl.multiple_of(i * 512, 512), 512)
-            ref[:, piece] = dot_cols(block, wa[piece, query + 2 * HD :]).astype(jnp.bfloat16)
-
-    next(g_steps)
-    next(g_steps)
-    steps = scatter_steps(
-        layout.attn, rows, attn_plan(layout.attn), out_rows, middle, (stage, core_in, arrive),
-        (last_out, last_in), (core_send, core_recv, s_send, s_recv, last_send, last_recv),
-    )
-    next(steps)
-    next(g_steps)
-    finish(steps)
-    gain_two = gains[8:9].astype(jnp.float32)
-
-    def second(r):
-        values = tok[r].astype(jnp.float32) + RESIDUAL * middle[r]
-        middle[r] = values
-        h2[r] = (values * rms_factor(values) * gain_two).astype(jnp.bfloat16)
-
-    loop_rows(rows, 32, second)
-    h_steps = gather_steps(
-        layout.mlp, rows, MLP_GATHER, h2, h2_out, (h_send, h_recv, h_relay, h_own)
-    )
-    next(h_steps)
-    next(h_steps)
-    send_mlp(wd_ref, down_out, 0, 2)
-    finish(g_steps)
-    finish(h_steps)
-    for copy in mlp:
-        copy.wait()
-    h1_copy.wait()
-
-
-def front(layout, sizes, *args):
-    width, count, few = sizes.width, sizes.mlp_rows, sizes.attn_rows
-    hbm, vmem = pl.BlockSpec(memory_space=pl.ANY), pl.BlockSpec(memory_space=pltpu.VMEM)
-    share, depth, fsdp = layout.attn.share, sizes.depth, layout.fsdp
-    bf16 = jnp.bfloat16
-    shapes = [
-        ((few, width), bf16, hbm),
-        ((count, width), bf16, hbm),
-        ((count, width), bf16, hbm),
-        ((width, 2 * sizes.hidden), bf16, hbm),
-        ((width, sizes.hidden), bf16, hbm),
-        ((width, sizes.attn), bf16, vmem),
-        ((few, sizes.query + 2 * HD), bf16, vmem),
-        ((few, sizes.query), bf16, vmem),
-        ((sizes.rows, width), jnp.float32, vmem),
-        ((16, width), bf16, vmem),
-        ((share, 8, sizes.length), jnp.int32, vmem),
-    ]
-    dma = pltpu.SemaphoreType.DMA
-    return pl.pallas_call(
-        functools.partial(front_kernel, layout, sizes),
-        out_shape=[jax.ShapeDtypeStruct(shape, dtype) for shape, dtype, _ in shapes],
-        in_specs=[hbm] * len(args),
-        out_specs=[spec for _, _, spec in shapes],
-        scratch_shapes=[
-            pltpu.VMEM((few, width), bf16),
-            pltpu.VMEM((sizes.rows, width), bf16),
-            pltpu.VMEM((sizes.rows, width), bf16),
-            pltpu.VMEM((depth, share * sizes.query), bf16),
-            pltpu.VMEM((depth, 128), bf16),
-            pltpu.VMEM((depth, 128), bf16),
-            pltpu.VMEM((depth, share * sizes.query), bf16),
-            pltpu.VMEM((share, depth, sizes.attn), bf16),
-        ]
-        + scatter_scratch(sizes.rows, width)
-        + gather_sems() * 3
-        + scatter_sems()
-        + [dma((fsdp,)), dma((fsdp,)), dma((fsdp,)), dma((fsdp,))]
-        + [dma((share,)), dma((share,)), dma((3, fsdp)), dma((3, fsdp)), dma((8,))],
-        compiler_params=pltpu.CompilerParams(
-            collective_id=3, has_side_effects=True, vmem_limit_bytes=56 * 1024 * 1024
-        ),
-        name="front",
-    )(*args)
-
-
 def seq_gather(layout, out_ref, width, sems):
     send, recv = sems
     me = lax.axis_index("seq")
@@ -732,22 +436,20 @@
     yield
 
 
-def back_kernel(
+def layer_kernel(
     layout,
     sizes,
     tok_ref,
     cot_ref,
-    h1_ref,
-    h2_ref,
-    g_ref,
-    in_ref,
-    down_ref,
-    wa_ref,
-    qkv_ref,
-    att_ref,
-    mid_ref,
+    ids_ref,
     gains_ref,
-    ids_ref,
+    wq_ref,
+    wk_ref,
+    wv_ref,
+    wo_ref,
+    wg_ref,
+    wu_ref,
+    wd_ref,
     mixed,
     grad_tok,
     gain_sum,
@@ -758,7 +460,8 @@
     gate_recv,
     up_recv,
     down_recv,
-    attn_recv,
+    attn_recv_hbm,
+    h1_out,
     g_all,
     h_all,
     w_in,
@@ -788,10 +491,18 @@
     down_total,
     down_last_out,
     down_last_in,
-    a_send,
-    a_recv,
-    a_relay,
-    a_own,
+    x_send,
+    x_recv,
+    x_relay,
+    x_own,
+    h_send,
+    h_recv,
+    h_relay,
+    h_own,
+    g_send,
+    g_recv,
+    g_relay,
+    g_own,
     core_send,
     core_recv,
     s_send,
@@ -801,24 +512,254 @@
     down_last_send,
     down_last_recv,
     credit,
+    ready,
+    attn_send,
+    attn_recv,
+    gain_send,
+    gain_recv,
+    id_send,
+    id_recv,
+    mlp_send,
+    mlp_recv,
+    load_sem,
     grad_send,
     grad_recv,
     join_send,
     join_recv,
     own_sem,
-    gain_send,
-    gain_recv,
+    sum_send,
+    sum_recv,
     gs_send,
     gs_recv,
-    load_sem,
     pick_sem,
 ):
-    fsdp, depth = layout.fsdp, sizes.depth
+    share, fsdp, depth = layout.attn.share, layout.fsdp, sizes.depth
+    mlp_share = layout.mlp.share
     seq_me, fsdp_me = lax.axis_index("seq"), lax.axis_index("fsdp")
-    query, hidden, rows = sizes.query, sizes.hidden, sizes.rows
-    base = query + 2 * HD
+    query = sizes.query
+    rows, hidden = sizes.rows, sizes.hidden
+
     count, few = sizes.mlp_rows, sizes.attn_rows
     near = pl.ds(0, few)
+    wq = grad_in.at[pl.ds(0, depth), pl.ds(0, share * query)]
+    wo = grad_in.at[pl.ds(depth, depth), pl.ds(0, share * query)]
+    wk = grad_in.at[pl.ds(0, depth), pl.ds(hidden, 128)]
+    wv = grad_in.at[pl.ds(depth, depth), pl.ds(hidden, 128)]
+    pack = [grad_in.at[pl.ds((2 + j) * depth, depth), pl.ds(0, sizes.attn)] for j in range(share)]
+
+    def tell(sem):
+        for bit in range(layout.mlp.bits):
+            pl.semaphore_signal(
+                sem, inc=1, device_id=layout.mlp.partner(bit), device_id_type=MESH
+            )
+
+    loads = []
+
+    def load(src, dst):
+        copy = pltpu.make_async_copy(src, dst, load_sem.at[len(loads)])
+        copy.start()
+        loads.append(copy)
+        return copy
+
+    def columns(ref, start, size):
+        return ref.at[:, pl.ds(pl.multiple_of(start, 128), size)]
+
+    load(tok_ref, tok)
+    own_rows = pl.ds(pl.multiple_of(fsdp_me * depth, 128), depth)
+    load(gains_ref, gains.at[:, own_rows])
+    load(columns(wq_ref, seq_me * share * query, share * query), wq)
+    load(columns(wo_ref, seq_me * share * query, share * query), wo)
+    chunk = seq_me * share // (2 * sizes.kv_share) * 128
+    load(columns(wk_ref, chunk, 128), wk)
+    load(columns(wv_ref, chunk, 128), wv)
+    load(ids_ref, ids.at[fsdp_me % share])
+    load(cot_ref, down_last_out)
+    greet_all(layout)
+    small = []
+    for mask in range(1, fsdp):
+        copy = pltpu.make_async_remote_copy(
+            src_ref=gains_ref,
+            dst_ref=gains.at[:, own_rows],
+            send_sem=gain_send.at[mask],
+            recv_sem=gain_recv.at[mask],
+            device_id=offset(0, mask),
+            device_id_type=MESH,
+        )
+        copy.start()
+        small.append(copy)
+    for copy in loads:
+        copy.wait()
+    for j in range(share):
+        target = seq_me * share + j
+        pack[j][...] = jnp.concatenate(
+            [
+                wq[:, j * query : (j + 1) * query],
+                kv_half(sizes, target, wk[...]),
+                kv_half(sizes, target, wv[...]),
+                wo[:, j * query : (j + 1) * query],
+            ],
+            axis=1,
+        )
+    def packed(j):
+        start = pl.multiple_of((2 + j) * depth, 128)
+        return grad_in.at[pl.ds(start, depth), pl.ds(0, sizes.attn)]
+
+    attn = {}
+
+    def send_attn(number, src, place, hop):
+        attn[number] = pltpu.make_async_remote_copy(
+            src_ref=src,
+            dst_ref=wa.at[place],
+            send_sem=attn_send.at[number],
+            recv_sem=attn_recv.at[number],
+            device_id=offset(0, hop),
+            device_id_type=MESH,
+        )
+        attn[number].start()
+
+    for mask in (4, 5, 3, 2, 1):
+        send_attn(mask, packed(jnp.bitwise_xor(fsdp_me, mask) % share), own_rows, mask)
+    wa[own_rows] = packed(fsdp_me % share)[...]
+    for copy in small:
+        copy.wait()
+    gain_one = gains[0:1].astype(jnp.float32)
+
+    def norm(r):
+        values = tok[r].astype(jnp.float32)
+        grad_tok[r] = (values * rms_factor(values) * gain_one).astype(jnp.bfloat16)
+
+    loop_rows(rows, 32, norm)
+    x_steps = gather_steps(
+        layout.attn, rows, attn_plan(layout.attn), grad_tok, h_all.at[near], (x_send, x_recv, x_relay, x_own)
+    )
+    next(x_steps)
+    id_copies = []
+    for mask in range(1, share):
+        copy = pltpu.make_async_remote_copy(
+            src_ref=ids_ref,
+            dst_ref=ids.at[fsdp_me % share],
+            send_sem=id_send.at[mask],
+            recv_sem=id_recv.at[mask],
+            device_id=offset(0, mask),
+            device_id_type=MESH,
+        )
+        copy.start()
+        id_copies.append(copy)
+    g_steps = gather_steps(
+        layout.mlp, rows, MLP_GATHER, cot_ref, g_all, (g_send, g_recv, g_relay, g_own)
+    )
+    next(g_steps)
+    for _ in range(FIRST_STAGES):
+        next(x_steps)
+    for mask in (4, 5):
+        attn[mask].wait_recv()
+        start = jnp.bitwise_xor(fsdp_me, mask) * depth
+        far_rows = pl.ds(pl.multiple_of(start, 128), depth)
+        send_attn(mask ^ 2, wa.at[far_rows], far_rows, 2)
+
+    mlp = []
+
+    def send_mlp(ref, out, place, index, masks):
+        def at(j):
+            return columns(ref, (seq_me * mlp_share + j) * hidden, hidden)
+
+        home = out.at[own_rows, pl.ds(place, hidden)]
+        for mask in masks:
+            if mask:
+                copy = pltpu.make_async_remote_copy(
+                    src_ref=at(jnp.bitwise_xor(fsdp_me, mask) % mlp_share),
+                    dst_ref=home,
+                    send_sem=mlp_send.at[index, mask],
+                    recv_sem=mlp_recv.at[index, mask],
+                    device_id=offset(0, mask),
+                    device_id_type=MESH,
+                )
+            else:
+                copy = pltpu.make_async_copy(at(fsdp_me % mlp_share), home, load_sem.at[1 + index])
+            copy.start()
+            mlp.append(copy)
+
+    def send_weights(masks):
+        masks = list(masks)
+        send_mlp(wg_ref, w_in, 0, 0, masks)
+        send_mlp(wu_ref, w_in, hidden, 1, masks)
+        send_mlp(wd_ref, w_down, 0, 2, masks)
+
+    send_weights(reversed(range(fsdp)))
+    finish(x_steps)
+    h1_copy = pltpu.make_async_copy(h_all.at[near], h1_out, load_sem.at[0])
+    h1_copy.start()
+    next(g_steps)
+    for mask, copy in attn.items():
+        copy.wait_send()
+        if mask not in (4, 5):
+            copy.wait_recv()
+
+    def project(r):
+        qkv[r] = dot(h_all[r], wa[:, : query + 2 * HD]).astype(jnp.bfloat16)
+
+    loop_rows(sizes.attn_rows, 256, project)
+    next(g_steps)
+    for copy in id_copies:
+        copy.wait()
+
+    blocks = sizes.length // sizes.span
+
+    @pl.loop(0, share * blocks)
+    def _(i):
+        seq = i // blocks
+        start = pl.multiple_of((i % blocks) * sizes.span, sizes.span)
+        outs = []
+        for head in range(sizes.heads):
+            _, _, values, probs = attention_scores(sizes, qkv, ids, seq, start, head)
+            outs.append(dot(probs.astype(jnp.bfloat16), values))
+        attended[rows_at(seq * sizes.length + start, sizes.span)] = jnp.concatenate(
+            outs, axis=1
+        ).astype(jnp.bfloat16)
+
+    h1_copy.wait()
+    tell(ready)
+
+    def out_rows(pair, ref):
+        block = attended[rows_at(pair * 2 * rows, 2 * rows)]
+
+        @pl.loop(0, sizes.width // 512)
+        def _(i):
+            piece = pl.ds(pl.multiple_of(i * 512, 512), 512)
+            ref[:, piece] = dot_cols(block, wa[piece, query + 2 * HD :]).astype(jnp.bfloat16)
+
+    next(g_steps)
+    next(g_steps)
+    steps = scatter_steps(
+        layout.attn, rows, attn_plan(layout.attn), out_rows, middle, (stage, core_in, arrive),
+        (last_out, last_in), (core_send, core_recv, s_send, s_recv, last_send, last_recv),
+    )
+    next(steps)
+    next(g_steps)
+    finish(steps)
+    gain_two = gains[8:9].astype(jnp.float32)
+
+    def second(r):
+        values = tok[r].astype(jnp.float32) + RESIDUAL * middle[r]
+        middle[r] = values
+        grad_tok[r] = (values * rms_factor(values) * gain_two).astype(jnp.bfloat16)
+
+    loop_rows(rows, 32, second)
+    pl.semaphore_wait(ready, layout.mlp.bits)
+    h_steps = gather_steps(
+        layout.mlp, rows, MLP_GATHER, grad_tok, h_all, (h_send, h_recv, h_relay, h_own)
+    )
+    next(h_steps)
+    next(h_steps)
+    finish(g_steps)
+    finish(h_steps)
+    for copy in mlp:
+        copy.wait()
+
+    base = query + 2 * HD
+    scatter = (stage, core_in, arrive)
+    sems = (core_send, core_recv, s_send, s_recv)
+    scatter_sem = sems + (last_send, last_recv)
     spare = few < count
 
     def piece_at(ref, mask):
@@ -832,30 +773,6 @@
 
     if spare:
         own_sum = g_all.at[pl.ds(few, depth)]
-    scatter = (stage, core_in, arrive)
-    sems = (core_send, core_recv, s_send, s_recv)
-    scatter_sem = sems + (last_send, last_recv)
-
-    loads = {}
-    for name, src, dst in (
-        ("in", in_ref, w_in),
-        ("h", h2_ref, h_all),
-        ("g", g_ref, g_all),
-        ("down", down_ref, w_down),
-        ("mid", mid_ref, middle),
-        ("tok", tok_ref, tok),
-        ("cot", cot_ref, down_last_out),
-        ("gains", gains_ref, gains),
-        ("wa", wa_ref, wa),
-        ("qkv", qkv_ref, qkv),
-        ("att", att_ref, attended),
-        ("ids", ids_ref, ids),
-    ):
-        loads[name] = pltpu.make_async_copy(src, dst, load_sem.at[len(loads)])
-        loads[name].start()
-    greet_all(layout)
-    for name in ("in", "h", "g", "down"):
-        loads[name].wait()
 
     def hidden_rows(r):
         h = h_all[r]
@@ -927,12 +844,8 @@
             grad_up(mask)
         next(steps)
     finish(steps)
-    h1_copy = pltpu.make_async_copy(h1_ref, h_all.at[near], load_sem.at[len(loads)])
+    h1_copy = pltpu.make_async_copy(h1_out, h_all.at[near], load_sem.at[0])
     h1_copy.start()
-    for name in ("mid", "tok", "cot", "gains", "wa", "qkv", "att", "ids"):
-        loads[name].wait()
-    gain_one = gains[0:1].astype(jnp.float32)
-    gain_two = gains[8:9].astype(jnp.float32)
     terms[...] = jnp.zeros_like(terms)
 
     def norm_two(r):
@@ -944,32 +857,6 @@
         last_out[r] = (RESIDUAL * grad).astype(jnp.bfloat16)
 
     loop_rows(rows, 32, norm_two)
-    a_steps = gather_steps(
-        layout.attn, rows, attn_plan(layout.attn), last_out, g_all.at[near], (a_send, a_recv, a_relay, a_own)
-    )
-    next(a_steps)
-    next(a_steps)
-    for mask in far:
-        send_grad(mask, w_in.at[block(mask), pl.ds(0, hidden)], gate_recv, 1)
-    for mask in far:
-        send_grad(mask, w_in.at[block(mask), pl.ds(hidden, hidden)], up_recv, 2)
-    finish(a_steps)
-
-    def down_rows(pair, ref):
-        left = hid[rows_at(pair * 2 * rows, 2 * rows)]
-
-        @pl.loop(0, sizes.width // 512)
-        def _(i):
-            piece = pl.ds(pl.multiple_of(i * 512, 512), 512)
-            ref[:, piece] = dot_cols(left, w_down[piece]).astype(jnp.bfloat16)
-
-    steps_low = scatter_steps(
-        layout.mlp, rows, MLP_SCATTER, down_rows, down_total, scatter, (down_last_out, down_last_in),
-        sems + (down_last_send, down_last_recv),
-    )
-    next(steps_low)
-
-
     def collect(index, share, src, width, own_piece, landing, combine, out, out_width):
         picks = []
         for number, mask, copy in sends:
@@ -1037,9 +924,36 @@
     mlp_share, attn_share = layout.mlp.share, layout.attn.share
     joined = mlp_share * hidden
     steps_down = collect(
-        0, mlp_share, down_recv, hidden, down_stage.at[block(0)], lambda mask: hid.at[block(mask)], place_columns, down_out, joined
-    )
+        0, mlp_share, down_recv, hidden, down_stage.at[block(0)],
+        lambda mask: grad_in.at[block(mask), pl.ds(0, hidden)],
+        place_columns, down_out, joined,
+    )
+    a_steps = gather_steps(
+        layout.attn, rows, attn_plan(layout.attn), last_out, g_all.at[near], (x_send, x_recv, x_relay, x_own)
+    )
+    next(a_steps)
+    next(a_steps)
+    for mask in far:
+        send_grad(mask, w_in.at[block(mask), pl.ds(0, hidden)], gate_recv, 1)
+    for mask in far:
+        send_grad(mask, w_in.at[block(mask), pl.ds(hidden, hidden)], up_recv, 2)
     next(steps_down)
+    finish(a_steps)
+
+    def down_rows(pair, ref):
+        left = hid[rows_at(pair * 2 * rows, 2 * rows)]
+
+        @pl.loop(0, sizes.width // 512)
+        def _(i):
+            piece = pl.ds(pl.multiple_of(i * 512, 512), 512)
+            ref[:, piece] = dot_cols(left, w_down[piece]).astype(jnp.bfloat16)
+
+    steps_low = scatter_steps(
+        layout.mlp, rows, MLP_SCATTER, down_rows, down_total, scatter, (down_last_out, down_last_in),
+        sems + (down_last_send, down_last_recv),
+    )
+    next(steps_low)
+
 
     blocks = sizes.length // sizes.span
 
@@ -1091,12 +1005,15 @@
         attend_back_block(i)
 
     next(steps_low)
-    for bit in range(layout.mlp.bits):
-        pl.semaphore_signal(
-            credit, inc=1, device_id=layout.mlp.partner(bit), device_id_type=MESH
-        )
-
+    tell(credit)
     next(steps_down)
+    steps_gate = collect(
+        1, mlp_share, gate_recv, hidden, w_in.at[block(0), pl.ds(0, hidden)],
+        lambda mask: grad_in.at[block(mask), pl.ds(0, hidden)],
+        place_columns, gate_out, joined,
+    )
+    next(steps_gate)
+    next(steps_gate)
     pl.semaphore_wait(credit, layout.mlp.bits)
 
     def qkv_back(pair, ref):
@@ -1115,7 +1032,7 @@
         staged(mask)[:, base:] = dot_rows(g_all[near, cols], attended[...]).astype(
             jnp.bfloat16
         )
-        send_grad(mask, staged(mask), attn_recv, 3)
+        send_grad(mask, staged(mask), attn_recv_hbm, 3)
 
     for mask in far[: fsdp // 2]:
         grad_attn(mask)
@@ -1123,14 +1040,8 @@
     next(steps)
     for mask in far[fsdp // 2 :]:
         grad_attn(mask)
-    steps_gate = collect(
-        1, mlp_share, gate_recv, hidden, w_in.at[block(0), pl.ds(0, hidden)], lambda mask: grad_in.at[block(mask), pl.ds(0, hidden)],
-        place_columns, gate_out, joined,
-    )
-    next(steps_gate)
     next(steps)
     next(steps_gate)
-    next(steps)
     finish(steps)
 
     def norm_one(r):
@@ -1152,8 +1063,8 @@
         copy = pltpu.make_async_remote_copy(
             src_ref=terms.at[:, owner_columns(mask)],
             dst_ref=gain_in.at[mask],
-            send_sem=gain_send.at[mask],
-            recv_sem=gain_recv.at[mask],
+            send_sem=sum_send.at[mask],
+            recv_sem=sum_recv.at[mask],
             device_id=offset(0, mask),
             device_id_type=MESH,
         )
@@ -1166,9 +1077,8 @@
     )
     next(steps_up)
     next(steps_up)
-    next(steps_gate)
     steps_attn = collect(
-        3, attn_share, attn_recv, sizes.attn, staged(0), functools.partial(piece_at, g_all),
+        3, attn_share, attn_recv_hbm, sizes.attn, staged(0), functools.partial(piece_at, g_all),
         place_attn, attn_out, sizes.attn_joined,
     )
     next(steps_attn)
@@ -1200,7 +1110,7 @@
         copy.wait_send()
 
 
-def back(layout, sizes, *args):
+def layer(layout, sizes, *args):
     width, count, few = sizes.width, sizes.mlp_rows, sizes.attn_rows
     hbm, vmem = pl.BlockSpec(memory_space=pl.ANY), pl.BlockSpec(memory_space=pltpu.VMEM)
     share, depth, fsdp = layout.attn.share, sizes.depth, layout.fsdp
@@ -1219,11 +1129,12 @@
         ((fsdp, depth, hidden), bf16, hbm),
         ((fsdp, depth, hidden), bf16, hbm),
         ((fsdp, depth, sizes.attn), bf16, hbm),
+        ((few, width), bf16, hbm),
     ]
     dma = pltpu.SemaphoreType.DMA
     seq = layout.seq
     return pl.pallas_call(
-        functools.partial(back_kernel, layout, sizes),
+        functools.partial(layer_kernel, layout, sizes),
         out_shape=[jax.ShapeDtypeStruct(shape, dtype) for shape, dtype, _ in shapes],
         in_specs=[hbm] * len(args),
         out_specs=[spec for _, _, spec in shapes],
@@ -1256,17 +1167,19 @@
             pltpu.VMEM((rows, width), bf16),
             pltpu.VMEM((rows, width), bf16),
         ]
-        + gather_sems()
+        + gather_sems() * 3
         + scatter_sems()
         + [dma((PLAN_PIECES,)), dma((PLAN_PIECES,))]
-        + [pltpu.SemaphoreType.REGULAR]
+        + [pltpu.SemaphoreType.REGULAR, pltpu.SemaphoreType.REGULAR]
+        + [dma((fsdp,)), dma((fsdp,)), dma((fsdp,)), dma((fsdp,))]
+        + [dma((share,)), dma((share,)), dma((3, fsdp)), dma((3, fsdp)), dma((8,))]
         + [dma((4, fsdp)), dma((4, fsdp)), dma((4, seq)), dma((4, seq)), dma((4,))]
         + [dma((fsdp,)), dma((fsdp,)), dma((layout.seq_bits,)), dma((layout.seq_bits,))]
-        + [dma((16,)), dma((4, fsdp))],
+        + [dma((4, fsdp))],
         compiler_params=pltpu.CompilerParams(
-            collective_id=4, has_side_effects=True, vmem_limit_bytes=62 * 1024 * 1024
+            collective_id=1, has_side_effects=True, vmem_limit_bytes=125 * 512 * 1024
         ),
-        name="back",
+        name="layer",
     )(*args)
 
 
@@ -1291,19 +1204,7 @@
         [jnp.broadcast_to(gain[None], (8, depth)) for gain in (gain_attn, gain_mlp)], axis=0
     )
     ids_own = jnp.broadcast_to(block_ids, (8, block_ids.shape[1]))
-    (
-        normed_one,
-        normed_two,
-        grad_all,
-        in_all,
-        down_all,
-        attn_all,
-        qkv,
-        attended,
-        middle,
-        gains_all,
-        ids_all,
-    ) = front(
+    mixed, grad_tokens, gain_sum, grad_gate, grad_up, grad_down, grad_attn, *_ = layer(
         layout,
         sizes,
         tokens[0],
@@ -1318,47 +1219,33 @@
         w_up,
         w_down,
     )
-    mixed, grad_tokens, gain_sum, grad_gate, grad_up, grad_down, grad_attn, *_ = back(
-        layout,
-        sizes,
-        tokens[0],
-        cotangent[0],
-        normed_one,
-        normed_two,
-        grad_all,
-        in_all,
-        down_all,
-        attn_all,
-        qkv,
-        attended,
-        middle,
-        gains_all,
-        ids_all,
-    )
-    parts = grad_attn.reshape(depth, layout.seq, sizes.attn_joined)
     wide, narrow = layout.attn.share * sizes.query, sizes.kv_columns
 
-    def flat(columns):
-        return columns.astype(jnp.float32).reshape(depth, -1)
-
-    def heads(columns):
-        columns = columns.astype(jnp.float32)
+    def joined(start, size):
+        columns = [
+            grad_attn[:, i * sizes.attn_joined + start : i * sizes.attn_joined + start + size]
+            for i in range(layout.seq)
+        ]
+        return jnp.concatenate(columns, axis=1).astype(jnp.float32)
+
+    def heads(start):
+        columns = joined(start, narrow)
         if layout.seq * narrow > KVH * HD:
-            columns = jnp.sum(columns.reshape(depth, KVH, -1, HD), axis=2)
-        return columns.reshape(depth, -1)
+            columns = jnp.sum(columns.reshape(depth, KVH, -1, HD), axis=2).reshape(depth, -1)
+        return columns
 
     return (
         mixed[None],
         grad_tokens[None],
         gain_sum[0],
-        flat(parts[:, :, :wide]),
-        heads(parts[:, :, 2 * wide : 2 * wide + narrow]),
-        heads(parts[:, :, 2 * wide + narrow :]),
-        flat(parts[:, :, wide : 2 * wide]),
+        joined(0, wide),
+        heads(2 * wide),
+        heads(2 * wide + narrow),
+        joined(wide, wide),
         gain_sum[1],
-        flat(grad_gate),
-        flat(grad_up),
-        flat(grad_down),
+        grad_gate.astype(jnp.float32),
+        grad_up.astype(jnp.float32),
+        grad_down.astype(jnp.float32),
     )
 
 

time: 552 us -> 518 us (0.938)
  Pallas kernels: 511 us -> 481 us
  local copies, waits for them, and re-layouts: 16.5 us -> 9.34 us
    pallas_call x2 -> x1, Pallas kernels: 511 us -> 481 us  [layer(): pl.pallas_call(functools.partial(layer_kernel, layout, sizes), out_shape=...]
    reshape x2 -> x0, local copies, waits for them, and re-layouts: 5.86 us -> none  [the longest x1 4.82 us: body(): parts = grad_attn.reshape(depth, layout.seq, sizes.attn_joined)]
    convert_element_type x3 -> x5, other arithmetic: 13.1 us -> 16.8 us  [the longest x1 4.38 us: body(): grad_up.astype(jnp.float32)]
where the time goes in v6:
time: 518 us; the launch traced here: 509 us
  Pallas kernels  481 us (93%)
  other arithmetic  17.4 us (3%)
  local copies, waits for them, and re-layouts  9.34 us (2%)
    pallas_call x1, Pallas kernels, layer(): pl.pallas_call(functools.partial(layer_kernel, layout, sizes), out_shape=...  481 us

profile of v6, /device:TPU:15, one launch (start us, length us, event | category | flops | bytes accessed | tf_op | source)
XLA Modules:
  0.0 508.8 jit_solution(7354329884141407338)
XLA Ops:
  0.6 0.7 broadcast_in_dim.27
  1.3 0.7 broadcast_in_dim.28
  2.0 0.6 pad_maximum_fusion.gains_ref
  2.6 1.3 broadcast_in_dim.26.ids_ref
  3.9 480.9 %layer.1 = (bf16[128,2048]{1,0:T(8,128)(2,1)}, bf16[128,2048]{1,0:T(8,128)(2,1)}, f32[8,256]{1,0:T(8,128)}, bf16[256,8192]{1,0:T(8,128)(2,1)}, bf16[256,8192]{1,...) custom-call(bf16[128,2048]{1,0:T(8,128)(2,1)} %bitcast.7, ...), custom_call_target="tpu_custom_call" | custom-call | tf_op jit(solution)/shard_map/layer/pallas_call | solution.py:1136
  484.7 1.3 fusion.2
  486.1 1.1 fusion.1
  487.2 1.7 fusion
  488.8 1.0 maximum_convert_fusion.2
  489.9 0.0 copy-start.2
  489.9 2.7 maximum_convert_fusion
  492.6 1.0 copy-done.2
  493.6 0.0 copy-start.1
  493.6 4.4 convert_element_type.25
  498.0 0.0 copy-done.1
  498.0 0.0 copy-start
  498.0 4.4 convert_element_type.26
  502.3 0.0 copy-done
  502.3 0.0 copy-start.4
  502.3 0.0 copy-start.3
  502.3 4.4 convert_element_type.27
  506.7 0.0 copy-done.4
  506.7 0.8 copy.25
  507.5 0.0 copy-done.3
  507.5 0.8 copy.26
Async XLA Ops:
  489.9 3.7 copy-start.2
  493.6 4.4 copy-start.1
  498.0 4.4 copy-start
  502.3 4.4 copy-start.4
  502.3 5.2 %copy-start.3 = (bf16[128,2048]{1,0:T(8,128)(2,1)S(1)}, bf16[128,2048]{1,0:T(8,128)(2,1)}, u32[]{:S(2)}) copy-start(bf16[128,2048]{1,0:T(8,128)(2,1)} %get-tuple-element.19) | copy-start | bytes 1572868

commit v7 on v6

--- a/solution.py
+++ b/solution.py
@@ -27,9 +27,9 @@
 MLP_SCATTER = plan_of(THIRDS, ((1, 2, 3), (2, 1, 3), (1, 2, 3)))
 
 
-def attn_plan(group):
+def attn_plan(group, orders=((1, 2), (2, 1))):
     if group.bits == 3:
-        return plan_of(EVEN, ((1, 2), (2, 1)))
+        return plan_of(EVEN, orders)
     return plan_of(THIRDS, ((1, 2, 3), (2, 3, 1), (3, 1, 2)))
 
 
@@ -630,7 +630,7 @@
 
     loop_rows(rows, 32, norm)
     x_steps = gather_steps(
-        layout.attn, rows, attn_plan(layout.attn), grad_tok, h_all.at[near], (x_send, x_recv, x_relay, x_own)
+        layout.attn, rows, attn_plan(layout.attn, ((2, 1), (2, 1))), grad_tok, h_all.at[near], (x_send, x_recv, x_relay, x_own)
     )
     next(x_steps)
     id_copies = []
@@ -929,7 +929,7 @@
         place_columns, down_out, joined,
     )
     a_steps = gather_steps(
-        layout.attn, rows, attn_plan(layout.attn), last_out, g_all.at[near], (x_send, x_recv, x_relay, x_own)
+        layout.attn, rows, attn_plan(layout.attn, ((2, 1), (2, 1))), last_out, g_all.at[near], (x_send, x_recv, x_relay, x_own)
     )
     next(a_steps)
     next(a_steps)

time: 518 us -> 507 us (0.979)
  Pallas kernels: 481 us -> 469 us
    pallas_call x1, Pallas kernels: 481 us -> 469 us  [layer(): pl.pallas_call(functools.partial(layer_kernel, layout, sizes), out_shape=...]
where the time goes in v7:
time: 507 us; the launch traced here: 496 us
  Pallas kernels  469 us (93%)
  other arithmetic  17.4 us (3%)
  local copies, waits for them, and re-layouts  9.34 us (2%)
    pallas_call x1, Pallas kernels, layer(): pl.pallas_call(functools.partial(layer_kernel, layout, sizes), out_shape=...  469 us

profile of v7, /device:TPU:15, one launch (start us, length us, event | category | flops | bytes accessed | tf_op | source)
XLA Modules:
  0.0 496.5 jit_solution(5216131170915404558)
XLA Ops:
  0.6 0.7 broadcast_in_dim.27
  1.3 0.7 broadcast_in_dim.28
  2.0 0.6 pad_maximum_fusion.gains_ref
  2.6 1.3 broadcast_in_dim.26.ids_ref
  3.9 468.6 %layer.1 = (bf16[128,2048]{1,0:T(8,128)(2,1)}, bf16[128,2048]{1,0:T(8,128)(2,1)}, f32[8,256]{1,0:T(8,128)}, bf16[256,8192]{1,0:T(8,128)(2,1)}, bf16[256,8192]{1,...) custom-call(bf16[128,2048]{1,0:T(8,128)(2,1)} %bitcast.7, ...), custom_call_target="tpu_custom_call" | custom-call | tf_op jit(solution)/shard_map/layer/pallas_call | solution.py:1136
  472.4 1.3 fusion.2
  473.8 1.1 fusion.1
  474.9 1.7 fusion
  476.5 1.0 maximum_convert_fusion.2
  477.6 0.0 copy-start.2
  477.6 2.7 maximum_convert_fusion
  480.3 1.0 copy-done.2
  481.3 0.0 copy-start.1
  481.3 4.4 convert_element_type.25
  485.7 0.0 copy-done.1
  485.7 0.0 copy-start
  485.7 4.4 convert_element_type.26
  490.0 0.0 copy-done
  490.1 0.0 copy-start.4
  490.1 0.0 copy-start.3
  490.1 4.4 convert_element_type.27
  494.4 0.0 copy-done.4
  494.4 0.8 copy.25
  495.2 0.0 copy-done.3
  495.2 0.8 copy.26
Async XLA Ops:
  477.6 3.7 copy-start.2
  481.3 4.4 copy-start.1
  485.7 4.4 copy-start
  490.1 4.4 copy-start.4
  490.1 5.2 %copy-start.3 = (bf16[128,2048]{1,0:T(8,128)(2,1)S(1)}, bf16[128,2048]{1,0:T(8,128)(2,1)}, u32[]{:S(2)}) copy-start(bf16[128,2048]{1,0:T(8,128)(2,1)} %get-tuple-element.19) | copy-start | bytes 1572868
